TPU v7x, 32 devices: a whole 2x2x4 slice. The times are simulated.
32 devices in a mesh: dp: 2 (over x), ctx: 4 (over z), tp: 4 (over y, core).
Axes of the slice: x: 2, y: 2, z: 4, core: 2. Of those that a mesh axis runs over, the one named last changes fastest.
Arguments:
- query_proj: bfloat16 [2, 1024, 2048], P('dp', 'ctx', 'tp'), may hold values from -6 to 6
- key_proj: bfloat16 [2, 1024, 2048], P('dp', 'ctx', 'tp'), may hold values from -6 to 6
- value_proj: bfloat16 [2, 1024, 2048], P('dp', 'ctx', 'tp'), may hold values from -6 to 6
- filters: float32 [2048, 1024], P('tp', 'ctx'), may hold values from -2 to 2
- w_out: bfloat16 [2048, 2048], P('tp'), may hold values from -0.125 to 0.125
- cotangent: bfloat16 [2, 1024, 2048], P('dp', 'ctx', 'tp'), may hold values from -6 to 6
Outputs:
- output: bfloat16 [2, 1024, 2048], P('dp', 'ctx', 'tp')
- grad_query: bfloat16 [2, 1024, 2048], P('dp', 'ctx', 'tp')
- grad_key: bfloat16 [2, 1024, 2048], P('dp', 'ctx', 'tp')
- grad_value: bfloat16 [2, 1024, 2048], P('dp', 'ctx', 'tp')
- grad_filter: float32 [2048, 1024], P('tp', 'ctx')
- grad_wout: float32 [2048, 2048], P('tp', 'ctx')
All inputs are finite; a program needn't handle non-finite values.
Results may differ from a plain program's by a relative error of at most 0.0049.
Values may be sent and summed in bfloat16 or wider, within the bound.
No kernel may reach another device: no remote copies, remote signals or barrier semaphores. Data moves between devices by JAX's collectives and lax.ppermute only.
A program may use at most 64 MiB of HBM per device.

v0:
```python
import functools
import math

import jax
import jax.numpy as jnp
import ml_dtypes
import numpy as np
from jax import lax
from jax.experimental import pallas as pl
from jax.experimental.pallas import tpu as pltpu
from jax.sharding import PartitionSpec as P

F32 = jnp.float32
BF16 = jnp.bfloat16
LANES = 128
ROWS = 16


def build_tables(length_fft):
    blocks = length_fft // 128
    outer = jnp.arange(blocks, dtype=jnp.int32)
    inner = jnp.arange(blocks // 2, dtype=jnp.int32)
    column = jnp.arange(128, dtype=jnp.int32)
    first = (outer[:, None] * inner[None, :] % blocks).astype(jnp.float32) * (
        -2.0 * math.pi / blocks
    )
    turned = (outer[:, None] * column[None, :] % length_fft).astype(jnp.float32) * (
        -2.0 * math.pi / length_fft
    )
    second = (column[:, None] * column[None, :] % 128).astype(jnp.float32) * (-2.0 * math.pi / 128)
    return (
        jnp.cos(first),
        jnp.sin(first),
        jnp.cos(turned),
        jnp.sin(turned),
        jnp.cos(second),
        jnp.sin(second),
    )


def product(form, left, right):
    return jnp.einsum(form, left, right, precision=lax.Precision.HIGHEST)


def forward_transform(signal, tables):
    cos_first, sin_first, cos_turn, sin_turn, cos_second, sin_second = tables
    real_one = product("ia,cab->cib", cos_first, signal)
    imag_one = product("ia,cab->cib", sin_first, signal)
    real_two = real_one * cos_turn - imag_one * sin_turn
    imag_two = real_one * sin_turn + imag_one * cos_turn
    real_out = product("cib,bj->cij", real_two, cos_second) - product(
        "cib,bj->cij", imag_two, sin_second
    )
    imag_out = product("cib,bj->cij", real_two, sin_second) + product(
        "cib,bj->cij", imag_two, cos_second
    )
    return (real_out, imag_out)


def inverse_transform(real_in, imag_in, tables, length_fft):
    cos_first, sin_first, cos_turn, sin_turn, cos_second, sin_second = tables
    real_one = product("cij,jb->cib", real_in, cos_second) + product(
        "cij,jb->cib", imag_in, sin_second
    )
    imag_one = product("cij,jb->cib", imag_in, cos_second) - product(
        "cij,jb->cib", real_in, sin_second
    )
    real_two = real_one * cos_turn + imag_one * sin_turn
    imag_two = imag_one * cos_turn - real_one * sin_turn
    result = product("ia,cib->cab", cos_first, real_two) + product(
        "ia,cib->cab", sin_first, imag_two
    )
    return result / length_fft


def local_any_length(query_proj, key_proj, value_proj, filters, w_out, cotangent):
    query_rows = query_proj[0].astype(jnp.float32)
    key_rows = key_proj[0].astype(jnp.float32)
    value_rows = value_proj[0].astype(jnp.float32)
    positions, channels = query_rows.shape
    seq_devices = lax.axis_size("ctx")
    length_fft = 2 * positions * seq_devices
    tables = build_tables(length_fft)
    mixed = (key_rows * value_rows).T
    mixed_chan, filter_chan = (
        lax.all_to_all(mixed, "ctx", split_axis=0, concat_axis=1, tiled=True),
        lax.all_to_all(filters, "ctx", split_axis=0, concat_axis=1, tiled=True),
    )
    local_channels = mixed_chan.shape[0]
    block_shape = (local_channels, length_fft // 256, 128)
    mixed_real, mixed_imag = forward_transform(mixed_chan.reshape(block_shape), tables)
    filter_real, filter_imag = forward_transform(filter_chan.reshape(block_shape), tables)
    conv_real = filter_real * mixed_real - filter_imag * mixed_imag
    conv_imag = filter_real * mixed_imag + filter_imag * mixed_real
    conv_chan = inverse_transform(conv_real, conv_imag, tables, length_fft).reshape(
        local_channels, -1
    )
    conv_back = lax.all_to_all(conv_chan, "ctx", split_axis=1, concat_axis=0, tiled=True)
    conv = conv_back.T
    gated = (query_rows * conv).astype(jnp.bfloat16)
    partial_terms = jnp.dot(gated, w_out, preferred_element_type=jnp.float32)
    output = lax.psum_scatter(partial_terms, "tp", scatter_dimension=1, tiled=True).astype(
        jnp.bfloat16
    )
    piece = lax.all_gather(cotangent[0], "tp", axis=1, tiled=True)
    grad_gated = lax.dot_general(
        piece, w_out, (((1,), (1,)), ((), ())), preferred_element_type=jnp.float32
    )
    weight_piece = lax.dot_general(
        gated, piece, (((0,), (0,)), ((), ())), preferred_element_type=jnp.float32
    )
    weight_grad = weight_piece
    grad_gated, weight_grad = (grad_gated, weight_grad)
    grad_query = (grad_gated * conv).astype(jnp.bfloat16)
    grad_conv = (grad_gated * query_rows).T
    grad_chan = lax.all_to_all(grad_conv, "ctx", split_axis=0, concat_axis=1, tiled=True)
    grad_real, grad_imag = forward_transform(grad_chan.reshape(block_shape), tables)
    back_real = filter_real * grad_real + filter_imag * grad_imag
    back_imag = filter_real * grad_imag - filter_imag * grad_real
    taps_real = grad_real * mixed_real + grad_imag * mixed_imag
    taps_imag = grad_imag * mixed_real - grad_real * mixed_imag
    mixed_grad_chan = inverse_transform(back_real, back_imag, tables, length_fft).reshape(
        local_channels, -1
    )
    filter_grad_chan = inverse_transform(taps_real, taps_imag, tables, length_fft).reshape(
        local_channels, -1
    )
    mixed_grad_back, filter_grad_back = (
        lax.all_to_all(mixed_grad_chan, "ctx", split_axis=1, concat_axis=0, tiled=True),
        lax.all_to_all(filter_grad_chan, "ctx", split_axis=1, concat_axis=0, tiled=True),
    )
    grad_mixed = mixed_grad_back.T
    grad_key = (grad_mixed * value_rows).astype(jnp.bfloat16)
    grad_value = (grad_mixed * key_rows).astype(jnp.bfloat16)
    factor = 1.0 / math.sqrt(lax.axis_size("dp") * positions * seq_devices)
    grad_filter = lax.psum(filter_grad_back, "dp") * factor
    summed_seq = lax.psum_scatter(weight_grad, "ctx", scatter_dimension=1, tiled=True)
    summed_weight = lax.psum(summed_seq, "dp")
    grad_wout = summed_weight * factor
    return (
        output[None],
        grad_query[None],
        grad_key[None],
        grad_value[None],
        grad_filter,
        grad_wout,
    )


@functools.lru_cache
def transform_tables(blocks):
    length_fft = 2 * blocks * LANES
    b = np.arange(LANES, dtype=np.int64)
    angle = (2.0 * math.pi / LANES) * (b[:, None] * b[None, :] % LANES)
    cos, sin = np.cos(angle), np.sin(angle)
    whole = np.block([[cos, sin], [-sin, cos]])
    high = whole.astype(ml_dtypes.bfloat16)
    low = (whole - high.astype(np.float64)).astype(ml_dtypes.bfloat16)
    turn = np.zeros((LANES, LANES))
    i = np.arange(blocks + 1)
    angle = (2.0 * math.pi / length_fft) * (b[:, None] * i[None, :] % length_fft)
    turn[:, : blocks + 1] = np.cos(angle)
    turn[:, LANES // 2 : LANES // 2 + blocks + 1] = np.sin(angle)
    return np.stack([high, low]), turn.astype(np.float32)


def scaled_sum(terms):
    total = None
    for factor, term in terms:
        if abs(factor) < 1e-9:
            continue
        if abs(factor - 1.0) < 1e-9:
            total = term if total is None else total + term
        elif abs(factor + 1.0) < 1e-9:
            total = -term if total is None else total - term
        else:
            total = factor * term if total is None else total + factor * term
    return total


def split_bf16(value):
    high = value.astype(BF16)
    return high, (value - high.astype(F32)).astype(BF16)


def product3(matrix_ref, high, low):
    dot = functools.partial(jnp.dot, preferred_element_type=F32)
    return dot(matrix_ref[0], high) + (dot(matrix_ref[0], low) + dot(matrix_ref[1], high))


def turn_of(turn_ref, i, row):
    rows = pl.ds(row, ROWS)
    cos = turn_ref[rows, i : i + 1]
    sin = turn_ref[rows, LANES // 2 + i : LANES // 2 + i + 1]
    return jnp.broadcast_to(cos, (ROWS, LANES)), jnp.broadcast_to(sin, (ROWS, LANES))


def each_chunk(lanes, body):
    @pl.loop(0, LANES // ROWS)
    def _(step):
        for lane in range(0, lanes, LANES):
            body(pl.multiple_of(step * ROWS, ROWS), lane)


def over_blocks(read, blocks, lanes, turn_ref, high, low):
    def chunk(row, lane):
        def put(i, real, imag):
            if i > 0:
                cos, sin = turn_of(turn_ref, i, row)
                if imag is None:
                    real, imag = real * cos, -(real * sin)
                else:
                    real, imag = real * cos + imag * sin, imag * cos - real * sin
            for part, value in ((0, real), (1, jnp.zeros_like(real) if imag is None else imag)):
                top, rest = split_bf16(value)
                rows = pl.ds(pl.multiple_of(part * LANES + row, ROWS), ROWS)
                high[i, rows, pl.ds(lane, LANES)] = top
                low[i, rows, pl.ds(lane, LANES)] = rest

        slabs = [read(a, row, lane) for a in range(blocks)]
        for i in range(blocks // 2 + 1):
            sums = []
            for first in (0, 1):
                picked = range(first, blocks, 2)
                angle = [math.pi * ((i * a) % (2 * blocks)) / blocks for a in picked]
                sums.append(scaled_sum([(math.cos(g), slabs[a]) for g, a in zip(angle, picked)]))
                sums.append(scaled_sum([(-math.sin(g), slabs[a]) for g, a in zip(angle, picked)]))
            even_real, even_imag, odd_real, odd_imag = sums

            def joined(one, other, sign):
                if one is None or other is None:
                    return one if other is None else (other if sign > 0 else -other)
                return one + other if sign > 0 else one - other

            put(i, joined(even_real, odd_real, 1), joined(even_imag, odd_imag, 1))
            if blocks - i != i:
                put(blocks - i, joined(even_real, odd_real, -1), joined(odd_imag, even_imag, -1))

    each_chunk(lanes, chunk)


def back_to_blocks(turned, blocks, lanes, turn_ref, write):
    scale = 1.0 / (blocks * LANES)

    def chunk(row, lane):
        def get(i):
            real = turned[i, pl.ds(row, ROWS), pl.ds(lane, LANES)]
            imag = -turned[i, pl.ds(pl.multiple_of(LANES + row, ROWS), ROWS), pl.ds(lane, LANES)]
            if i > 0:
                cos, sin = turn_of(turn_ref, i, row)
                real, imag = real * cos - imag * sin, imag * cos + real * sin
            return real, imag

        terms = [[] for _ in range(blocks)]
        for i in range(blocks // 2 + 1):
            real, imag = get(i)
            if blocks - i != i:
                other_real, other_imag = get(blocks - i)
                pairs = ((real + other_real, imag - other_imag), (real - other_real, imag + other_imag))
            else:
                pairs = ((real, imag), (real, imag))
            if i == 0:
                pairs = tuple((0.5 * one, 0.5 * two) for one, two in pairs)
            for a in range(blocks):
                angle = math.pi * ((i * a) % (2 * blocks)) / blocks
                terms[a].append((math.cos(angle), pairs[a % 2][0]))
                terms[a].append((-math.sin(angle), pairs[a % 2][1]))
        for a in range(blocks):
            write(a, row, lane, scaled_sum(terms[a]) * scale)

    each_chunk(lanes, chunk)


def at_block(index, size=LANES):
    return pl.ds(pl.multiple_of(index * size, size), size)


def reader(ref):
    def read(a, row, lane):
        rows = pl.ds(pl.multiple_of(a * LANES + row, ROWS), ROWS)
        return ref[rows, pl.ds(lane, LANES)].astype(F32)

    return read


def writer(ref):
    def write(a, row, lane, value):
        rows = pl.ds(pl.multiple_of(a * LANES + row, ROWS), ROWS)
        ref[rows, pl.ds(lane, LANES)] = value.astype(ref.dtype)

    return write


def place_pieces(pieces, whole):
    me = lax.axis_index("ctx")
    for r, ref in enumerate(pieces):
        whole[at_block(me ^ r, ref.shape[0]), :] = ref[...]


def take_pieces(whole, pieces):
    me = lax.axis_index("ctx")
    for r, ref in enumerate(pieces):
        ref[...] = whole[at_block(me ^ r, ref.shape[0]), :]


def fetch(pairs, sems):
    copies = [pltpu.make_async_copy(source, target, sems.at[n]) for n, (source, target) in enumerate(pairs)]
    for copy in copies:
        copy.start()
    return copies


def prepare_kernel(*refs):
    *pieces, key_ref, value_ref, filter_ref, sems = refs[3:]
    for copy in fetch(list(zip(refs[:3], (key_ref, value_ref, filter_ref))), sems):
        copy.wait()
    me = lax.axis_index("ctx")
    for r, out_ref in enumerate(pieces):
        cols = at_block(me ^ r)
        mixed = key_ref[:, cols].astype(F32) * value_ref[:, cols].astype(F32)
        out_ref[:, pl.ds(0, LANES)] = mixed.astype(BF16)
        out_ref[:, pl.ds(LANES, LANES)] = filter_ref[cols, :].T.astype(BF16)


def forward_kernel(seqs, *refs):
    held, (matrix, turn, moved_ref), refs = refs[:seqs], refs[seqs : seqs + 3], refs[seqs + 4 :]
    sent, (spec_ref, passed_ref, whole, zh, zl, turned, conv) = refs[:seqs], refs[seqs:]
    blocks = spec_ref.shape[0] - 1
    passed_ref[...] = moved_ref[...]
    place_pieces(held, whole)
    over_blocks(reader(whole), blocks, 2 * LANES, turn, zh, zl)
    for i in range(blocks + 1):
        spec = product3(matrix, zh[i], zl[i])
        spec_ref[i] = spec
        mixed_real, mixed_imag = spec[:LANES, :LANES], spec[LANES:, :LANES]
        filter_real, filter_imag = spec[:LANES, LANES:], spec[LANES:, LANES:]
        real = filter_real * mixed_real - filter_imag * mixed_imag
        imag = filter_real * mixed_imag + filter_imag * mixed_real
        turned[i] = product3(matrix, *split_bf16(jnp.concatenate([real, -imag], axis=0)))
    back_to_blocks(turned, blocks, LANES, turn, writer(conv))
    take_pieces(conv, sent)


def backward_kernel(seqs, *refs):
    held, (spec_ref, matrix, turn), refs = refs[:seqs], refs[seqs : seqs + 3], refs[seqs + 4 :]
    sent, (whole, zh, zl, turned, back) = refs[:seqs], refs[seqs:]
    blocks = spec_ref.shape[0] - 1
    place_pieces(held, whole)
    over_blocks(reader(whole), blocks, LANES, turn, zh, zl)
    for i in range(blocks + 1):
        grad = product3(matrix, zh[i], zl[i])
        grad_real, grad_imag = grad[:LANES], grad[LANES:]
        mixed_real, mixed_imag = spec_ref[i, :LANES, :LANES], spec_ref[i, LANES:, :LANES]
        filter_real, filter_imag = spec_ref[i, :LANES, LANES:], spec_ref[i, LANES:, LANES:]
        back_real = filter_real * grad_real + filter_imag * grad_imag
        back_imag = filter_imag * grad_real - filter_real * grad_imag
        taps_real = grad_real * mixed_real + grad_imag * mixed_imag
        taps_imag = grad_real * mixed_imag - grad_imag * mixed_real
        real = jnp.concatenate([back_real, taps_real], axis=1)
        imag = jnp.concatenate([back_imag, taps_imag], axis=1)
        turned[i] = product3(matrix, *split_bf16(jnp.concatenate([real, imag], axis=0)))
    back_to_blocks(turned, blocks, 2 * LANES, turn, writer(back))
    take_pieces(back, sent)


def gradient_kernel(cot_ref, w_ref, query_ref, gated_grad_ref, *pieces):
    me = lax.axis_index("ctx")
    width = cot_ref.shape[2]
    total = None
    for j in range(cot_ref.shape[0]):
        term = lax.dot_general(
            cot_ref[j], w_ref[:, j * width : (j + 1) * width], (((1,), (1,)), ((), ())), preferred_element_type=F32
        )
        total = term if total is None else total + term
    gated_grad_ref[...] = total
    for r, out_ref in enumerate(pieces):
        cols = at_block(me ^ r)
        out_ref[...] = (gated_grad_ref[:, cols] * query_ref[:, cols].astype(F32)).astype(BF16)


def output_kernel(seqs, *refs):
    held, (query_ref, gated_grad_ref, w_ref), refs = refs[:seqs], refs[seqs : seqs + 3], refs[seqs + 4 :]
    turned_ref, grad_query_ref, keep_ref, send_ref, whole = refs
    me, part = lax.axis_index("ctx"), lax.axis_index("tp")
    width = keep_ref.shape[2]
    for r, ref in enumerate(held):
        whole[:, at_block(me ^ r)] = ref[...]
    conv = whole[...].astype(F32)
    gated = query_ref[...].astype(F32) * conv
    turned_ref[...] = gated.T.astype(BF16)
    gated = gated.astype(BF16)
    grad_query_ref[...] = (gated_grad_ref[...] * conv).astype(BF16)
    for y in range(keep_ref.shape[0]):
        for ref, core in ((keep_ref, part & 1), (send_ref, (part & 1) ^ 1)):
            ref[y] = jnp.dot(gated, w_ref[:, at_block(2 * y + core, width)], preferred_element_type=F32)


def pair_kernel(keep_ref, other_ref, mine_ref, far_ref):
    y = lax.axis_index("tp") >> 1
    mine_ref[...] = keep_ref[y] + other_ref[y]
    far_ref[...] = keep_ref[y ^ 1] + other_ref[y ^ 1]


def sum_kernel(mine_ref, other_ref, out_ref):
    out_ref[...] = (mine_ref[...] + other_ref[...]).astype(BF16)


def weight_kernel(own_ref, up1, up2, up3, down1, down2, down3, cot_ref, *refs):
    out_ref, gated, cot, sems = refs[-4:]
    me = lax.axis_index("ctx")
    seqs, size = cot_ref.shape[0], cot_ref.shape[1]
    blocks = [(cot_ref.at[p], cot.at[pl.ds(target_of(p) * size, size), :]) for p in range(seqs)]
    cot_copies = fetch([(own_ref, gated.at[0])] + blocks, sems)
    for r, (up, down) in enumerate(((up1, down3), (up2, down2), (up3, down1)), 1):

        @pl.when(me >= r)
        def _():
            pltpu.make_async_copy(up, gated.at[r], sems.at[seqs + r]).start()

        @pl.when(me < r)
        def _():
            pltpu.make_async_copy(down, gated.at[r], sems.at[seqs + r]).start()

    for copy in cot_copies:
        copy.wait()
    total = jnp.dot(gated[0], cot[at_block(me, size), :], preferred_element_type=F32)
    for r in range(1, seqs):
        pltpu.make_async_copy(up1, gated.at[r], sems.at[seqs + r]).wait()
        block = lax.rem(me + (seqs - r), seqs)
        total = total + jnp.dot(gated[r], cot[at_block(block, size), :], preferred_element_type=F32)
    out_ref[...] = total.astype(BF16)


def add_kernel(factor, one_ref, other_ref, out_ref):
    out_ref[...] = (one_ref[...].astype(F32) + other_ref[...].astype(F32)) * factor


def mixed_kernel(seqs, *refs):
    held, (key_ref, value_ref, grad_key_ref, grad_value_ref, taps_ref) = refs[:seqs], refs[seqs:]
    me = lax.axis_index("ctx")
    for r, ref in enumerate(held):
        cols = at_block(me ^ r)
        mixed_grad = ref[:, pl.ds(0, LANES)].astype(F32)
        grad_key_ref[:, cols] = (mixed_grad * value_ref[:, cols].astype(F32)).astype(BF16)
        grad_value_ref[:, cols] = (mixed_grad * key_ref[:, cols].astype(F32)).astype(BF16)
        taps_ref[:, cols] = ref[:, pl.ds(LANES, LANES)]


def taps_kernel(factor, one_ref, other_ref, out_ref):
    out_ref[...] = (one_ref[...].astype(F32) + other_ref[...].astype(F32)).T * factor


def shape_of(shape, dtype):
    return jax.ShapeDtypeStruct(shape, dtype)


def call(kernel, outs, flops, moved, *args, scratch=(), left=(), room=20):
    vmem, anywhere = pl.BlockSpec(memory_space=pltpu.VMEM), pl.BlockSpec(memory_space=pl.ANY)
    return pl.pallas_call(
        kernel,
        out_shape=outs,
        in_specs=[anywhere if n in left else vmem for n in range(len(args))],
        out_specs=jax.tree.map(lambda _: vmem, outs),
        scratch_shapes=scratch,
        cost_estimate=pl.CostEstimate(flops=flops, bytes_accessed=moved, transcendentals=0),
        compiler_params=pltpu.CompilerParams(vmem_limit_bytes=room * 2**20),
    )(*args)


def target_of(block):
    return ((block & 1) << 1) | (block >> 1)


def exchange(pieces, axis):
    size = lax.axis_size(axis)
    return [pieces[0]] + [lax.ppermute(pieces[r], axis, [(d, d ^ r) for d in range(size)]) for r in range(1, size)]


def local_short(query_proj, key_proj, value_proj, filters, w_out, cotangent):
    query, key, value, cot = query_proj[0], key_proj[0], value_proj[0], cotangent[0]
    positions, channels = query.shape
    seqs, parts, pairs = lax.axis_size("ctx"), lax.axis_size("tp"), lax.axis_size("dp")
    blocks = positions * seqs // LANES
    features = w_out.shape[1]
    width = features // parts
    factor = 1.0 / math.sqrt(pairs * positions * seqs)
    tables = [jnp.asarray(m) for m in transform_tables(blocks)]
    ring = [(d, (d + 1) % pairs) for d in range(pairs)]
    table = (blocks + 1, 2 * LANES)
    one = [shape_of((positions, LANES), BF16)] * seqs
    two = [shape_of((positions, 2 * LANES), BF16)] * seqs
    rows = (positions, channels)
    line = seqs * positions

    cot_rows = lax.all_gather(cot, "tp")
    swap = [(z * parts + j, j * parts + target_of(z)) for z in range(seqs) for j in range(parts)]
    cot_moved = lax.ppermute(cot, ("ctx", "tp"), swap)

    sent = call(
        prepare_kernel,
        two,
        10**6,
        2 * 10**6,
        key,
        value,
        filters,
        scratch=[
            pltpu.VMEM(rows, BF16),
            pltpu.VMEM(rows, BF16),
            pltpu.VMEM((channels, positions), F32),
            pltpu.SemaphoreType.DMA((3,)),
        ],
        left=(0, 1, 2),
        room=60,
    )
    held = exchange(sent, "ctx")

    gated_grad, *conv_grad = call(
        gradient_kernel,
        [shape_of(rows, F32)] + one,
        2 * positions * channels * features,
        5 * 10**6,
        cot_rows,
        w_out,
        query,
    )
    grad_held = exchange(conv_grad, "ctx")

    *conv_sent, spec, cot_passed = call(
        functools.partial(forward_kernel, seqs),
        one + [shape_of(table + (2 * LANES,), F32), shape_of(cot.shape, BF16)],
        10**9,
        9 * 10**6,
        *held,
        *tables,
        cot_moved,
        conv_grad[1],
        scratch=[
            pltpu.VMEM((line, 2 * LANES), BF16),
            pltpu.VMEM(table + (2 * LANES,), BF16),
            pltpu.VMEM(table + (2 * LANES,), BF16),
            pltpu.VMEM(table + (LANES,), F32),
            pltpu.VMEM((line, LANES), BF16),
        ],
        left=(seqs + 3,),
    )
    cot_cols = lax.all_gather(cot_passed, "tp")
    conv = exchange(conv_sent, "ctx")

    back_sent = call(
        functools.partial(backward_kernel, seqs),
        two,
        10**9,
        9 * 10**6,
        *grad_held,
        spec,
        *tables,
        conv_sent[1],
        scratch=[
            pltpu.VMEM((line, LANES), BF16),
            pltpu.VMEM(table + (LANES,), BF16),
            pltpu.VMEM(table + (LANES,), BF16),
            pltpu.VMEM(table + (2 * LANES,), F32),
            pltpu.VMEM((line, 2 * LANES), BF16),
        ],
        left=(seqs + 3,),
    )
    back = exchange(back_sent, "ctx")

    turned, grad_query, share_kept, share_sent = call(
        functools.partial(output_kernel, seqs),
        [shape_of((channels, positions), BF16), shape_of(rows, BF16)] + [shape_of((parts // 2, positions, width), F32)] * 2,
        2 * positions * channels * features,
        5 * 10**6,
        *conv,
        query,
        gated_grad,
        w_out,
        back_sent[1],
        scratch=[pltpu.VMEM(rows, BF16)],
        left=(seqs + 3,),
    )
    ups, downs = [turned], [turned]
    for r in range(1, seqs):
        ups.append(lax.ppermute(ups[-1], "ctx", [(d, d + 1) for d in range(r - 1, seqs - 1)]))
        downs.append(lax.ppermute(downs[-1], "ctx", [(d, d - 1) for d in range(seqs - r, 0, -1)]))
    mine, far = call(
        pair_kernel,
        [shape_of((positions, width), F32)] * 2,
        10**6,
        3 * 10**6,
        share_kept,
        lax.ppermute(share_sent, "tp", [(j, j ^ 1) for j in range(parts)]),
    )
    far = lax.ppermute(far, "tp", [(j, j ^ 2) for j in range(parts)])
    output = call(sum_kernel, shape_of((positions, width), BF16), 10**6, 2 * 10**6, mine, far)

    weight_grad = call(
        weight_kernel,
        shape_of((channels, width), BF16),
        2 * line * channels * width,
        3 * 10**6,
        turned,
        *ups[1:],
        *downs[1:],
        cot_cols,
        *back[1:],
        output,
        scratch=[
            pltpu.VMEM((seqs, channels, positions), BF16),
            pltpu.VMEM((line, width), BF16),
            pltpu.SemaphoreType.DMA((2 * seqs,)),
        ],
        left=range(2 * seqs + 4),
    )
    weight_other = lax.ppermute(weight_grad, "dp", ring)
    grad_wout = call(
        functools.partial(add_kernel, factor),
        shape_of((channels, width), F32),
        10**6,
        2 * 10**6,
        weight_grad,
        weight_other,
    )

    grad_key, grad_value, taps = call(
        functools.partial(mixed_kernel, seqs),
        [shape_of(rows, BF16)] * 3,
        10**6,
        2 * 10**6,
        *back,
        key,
        value,
    )
    grad_filter = call(
        functools.partial(taps_kernel, factor),
        shape_of((channels, positions), F32),
        10**6,
        10**6,
        taps,
        lax.ppermute(taps, "dp", ring),
    )
    return (output[None], grad_query[None], grad_key[None], grad_value[None], grad_filter, grad_wout)


def local(*args):
    positions, channels = args[0].shape[1:]
    seqs, parts, pairs = lax.axis_size("ctx"), lax.axis_size("tp"), lax.axis_size("dp")
    short = (
        channels == seqs * LANES
        and positions % LANES == 0
        and positions * seqs <= 8 * LANES
        and seqs == parts == 4
        and pairs == 2
        and args[4].shape[1] % (parts * LANES) == 0
    )
    return (local_short if short else local_any_length)(*args)


def solution(mesh):
    in_specs = (
        P("dp", "ctx", "tp"),
        P("dp", "ctx", "tp"),
        P("dp", "ctx", "tp"),
        P("tp", "ctx"),
        P("tp", None),
        P("dp", "ctx", "tp"),
    )
    out_specs = (
        P("dp", "ctx", "tp"),
        P("dp", "ctx", "tp"),
        P("dp", "ctx", "tp"),
        P("dp", "ctx", "tp"),
        P("tp", "ctx"),
        P("tp", "ctx"),
    )
    return jax.shard_map(local, mesh=mesh, in_specs=in_specs, out_specs=out_specs, check_vma=False)
```

profile of v0, /device:TPU:0, one launch (start us, length us, event | category | flops | bytes accessed | tf_op | source)
XLA Modules:
  0.0 127.0 jit_solution(11913225054353991993)
XLA Ops:
  7.2 0.0 copy-start.10
  7.2 0.0 copy-start.11
  7.2 0.0 all-gather.4.cloned.1.call-start
  7.2 0.7 all-gather.4.cloned.1.call-update
  7.9 0.0 all-gather.6.cloned.1.call-start
  8.0 1.6 %collective-permute-start.3 = (bf16[256,512]{1,0:T(8,128)(2,1)}, bf16[256,512]{1,0:T(8,128)(2,1)S(1)}, u32[]{:S(2)}, u32[]{:S(2)}) collective-permute-start(bf16[256,512]{1,0:T(8,128)(2,1)} %bitcast.17), channel_id=1, source_target_pairs={{0,0},{1,4},{2,8},{3,12},{4,2},{5,6},{6,10},{7,14},{8,1},{9,5},{10... | collective-permute-start | bytes 786440 | tf_op jit(solution)/shard_map/ppermute | solution.py:497
  9.6 2.1 %shard_map.127 = (bf16[256,256]{1,0:T(8,128)(2,1)}, bf16[256,256]{1,0:T(8,128)(2,1)}, bf16[256,256]{1,0:T(8,128)(2,1)}, bf16[256,256]{1,0:T(8,128)(2,1)}) custom-call(bf16[256,512]{1,0:T(8,128)(2,1)} %bitcast.13, bf16[256,512]{1,0:T(8,128)(2,1)} %bitcast.15, f32[512,256]{1,0:T(8,128)} %refs_2_.1), custom_call_target="tpu_custom_call" | custom-call | flops 1000000 | bytes 2000000 | tf_op jit(solution)/shard_map/pallas_call | solution.py:459
  11.7 4.8 %collective-permute-start = (bf16[256,256]{1,0:T(8,128)(2,1)}, bf16[256,256]{1,0:T(8,128)(2,1)S(1)}, u32[]{:S(2)}, u32[]{:S(2)}) collective-permute-start(bf16[256,256]{1,0:T(8,128)(2,1)} %get-tuple-element.35), channel_id=1, source_target_pairs={{0,4},{4,0},{8,12},{12,8},{1,5},{5,1},{9,13},{13,9},{2,6},{6,2},{1... | collective-permute-start | bytes 393224 | tf_op jit(solution)/shard_map/ppermute | solution.py:476
  16.5 1.8 %collective-permute-start.1 = (bf16[256,256]{1,0:T(8,128)(2,1)}, bf16[256,256]{1,0:T(8,128)(2,1)S(1)}, u32[]{:S(2)}, u32[]{:S(2)}) collective-permute-start(bf16[256,256]{1,0:T(8,128)(2,1)} %get-tuple-element.36), channel_id=1, source_target_pairs={{0,8},{4,12},{8,0},{12,4},{1,9},{5,13},{9,1},{13,5},{2,10},{6,14},... | collective-permute-start | bytes 393224 | tf_op jit(solution)/shard_map/ppermute | solution.py:476
  18.3 0.7 collective-permute-start.2
  19.0 10.1 %all-gather.4.cloned.1.call-done.cot_ref = bf16[4,256,512]{2,1,0:T(8,128)(2,1)} async-done(((bf16[1,256,512]{2,1,0:T(8,128)(2,1)}), bf16[4,256,512]{2,1,0:T(8,128)(2,1)}) %all-gather.4.cloned.1.call-update) | async-done | bytes 1048592 | tf_op jit(solution)/shard_map/all_gather | solution.py:495
  29.0 1.6 %copy-done = bf16[512,2048]{1,0:T(8,128)(2,1)S(1)} copy-done((bf16[512,2048]{1,0:T(8,128)(2,1)S(1)}, bf16[512,2048]{1,0:T(8,128)(2,1)}, u32[]{:S(2)}) %copy-start) | copy-done | bytes 2097176
  30.6 1.2 copy-done.3
  31.9 0.9 copy-done.5
  32.8 0.8 shard_map.128
  33.6 1.6 %collective-permute-start.7 = (bf16[256,128]{1,0:T(8,128)(2,1)S(1)}, bf16[256,128]{1,0:T(8,128)(2,1)S(1)}, u32[]{:S(2)}, u32[]{:S(2)}) collective-permute-start(bf16[256,128]{1,0:T(8,128)(2,1)S(1)} %get-tuple-element.38.refs_7_), channel_id=1, source_target_pairs={{0,4},{4,0},{8,12},{12,8},{1,5},{5,1},{9,13},{13,9},{2,6},{6,2},{1... | collective-permute-start | bytes 196616 | tf_op jit(solution)/shard_map/ppermute | solution.py:476
  35.2 3.0 %collective-permute-start.8 = (bf16[256,128]{1,0:T(8,128)(2,1)S(1)}, bf16[256,128]{1,0:T(8,128)(2,1)S(1)}, u32[]{:S(2)}, u32[]{:S(2)}) collective-permute-start(bf16[256,128]{1,0:T(8,128)(2,1)S(1)} %get-tuple-element.45), channel_id=1, source_target_pairs={{0,8},{4,12},{8,0},{12,4},{1,9},{5,13},{9,1},{13,5},{2,10},{6,14},... | collective-permute-start | bytes 196616 | tf_op jit(solution)/shard_map/ppermute | solution.py:476
  38.2 0.0 collective-permute-start.9
  38.2 0.0 collective-permute-done.2.refs_3_
  38.3 5.9 %shard_map.129 = (bf16[256,128]{1,0:T(8,128)(2,1)S(1)}, bf16[256,128]{1,0:T(8,128)(2,1)S(1)}, bf16[256,128]{1,0:T(8,128)(2,1)S(1)}, bf16[256,128]{1,0:T(8,128)(2...) custom-call(bf16[256,256]{1,0:T(8,128)(2,1)S(1)} %copy-done.9, ...), custom_call_target="tpu_custom_call" | custom-call | flops 1000000000 | bytes 9000000 | tf_op jit(solution)/shard_map/pallas_call | solution.py:459
  44.2 0.6 collective-permute-start.4
  44.8 3.8 %collective-permute-start.5 = (bf16[256,128]{1,0:T(8,128)(2,1)S(1)}, bf16[256,128]{1,0:T(8,128)(2,1)S(1)}, u32[]{:S(2)}, u32[]{:S(2)}) collective-permute-start(bf16[256,128]{1,0:T(8,128)(2,1)S(1)} %get-tuple-element.41), channel_id=1, source_target_pairs={{0,8},{4,12},{8,0},{12,4},{1,9},{5,13},{9,1},{13,5},{2,10},{6,14},... | collective-permute-start | bytes 196616 | tf_op jit(solution)/shard_map/ppermute | solution.py:476
  48.5 0.0 collective-permute-done.7.refs_1_
  48.5 0.0 collective-permute-start.6
  48.6 5.1 %shard_map.130 = (bf16[256,256]{1,0:T(8,128)(2,1)S(1)}, bf16[256,256]{1,0:T(8,128)(2,1)S(1)}, bf16[256,256]{1,0:T(8,128)(2,1)S(1)}, bf16[256,256]{1,0:T(8,128)(2,1)S(1)}) custom-call(bf16[256,128]{1,0:T(8,128)(2,1)S(1)} %get-tuple-element.44.refs_0_, bf16[256,128]{1,0:T(8,128)(2,1)S(1)} %collective-permute-done.7.refs_1_, ...), custom_call_target="tpu_custom_call" | custom-call | flops 1000000000 | bytes 9000000 | tf_op jit(solution)/shard_map/pallas_call | solution.py:459
  53.6 0.0 collective-permute-done.4.refs_1_
  53.6 0.0 collective-permute-done.5.refs_2_
  53.6 1.0 collective-permute-done.6.refs_3_
  54.6 1.7 %shard_map.131 = (bf16[512,256]{1,0:T(8,128)(2,1)S(1)}, bf16[256,512]{1,0:T(8,128)(2,1)}, f32[2,256,512]{2,1,0:T(8,128)S(1)}, f32[2,256,512]{2,1,0:T(8,128)}) custom-call(bf16[256,128]{1,0:T(8,128)(2,1)S(1)} %get-tuple-element.39.refs_0_, bf16[256,128]{1,0:T(8,128)(2,1)S(1)} %collective-permute-done.4.refs_1_, ...), custom_call_target="tpu_custom_call" | custom-call | flops 536870912 | bytes 5000000 | tf_op jit(solution)/shard_map/pallas_call | solution.py:459
  56.4 0.0 all-gather.6.cloned.1.call-update
  56.4 1.5 %collective-permute-start.16 = (bf16[512,256]{1,0:T(8,128)(2,1)S(1)}, bf16[512,256]{1,0:T(8,128)(2,1)S(1)}, u32[]{:S(2)}, u32[]{:S(2)}) collective-permute-start(bf16[512,256]{1,0:T(8,128)(2,1)S(1)} %get-tuple-element.60.own_ref), channel_id=1, source_target_pairs={{0,4},{4,8},{8,12},{1,5},{5,9},{9,13},{2,6},{6,10},{10,14},{3,7},{... | collective-permute-start | bytes 786440 | tf_op jit(solution)/shard_map/ppermute | solution.py:585
  57.9 1.3 %collective-permute-start.19 = (bf16[512,256]{1,0:T(8,128)(2,1)S(1)}, bf16[512,256]{1,0:T(8,128)(2,1)S(1)}, u32[]{:S(2)}, u32[]{:S(2)}) collective-permute-start(bf16[512,256]{1,0:T(8,128)(2,1)S(1)} %get-tuple-element.60.own_ref), channel_id=1, source_target_pairs={{12,8},{8,4},{4,0},{13,9},{9,5},{5,1},{14,10},{10,6},{6,2},{15,11}... | collective-permute-start | bytes 786440 | tf_op jit(solution)/shard_map/ppermute | solution.py:586
  59.2 0.0 collective-permute-done.10.other_ref
  59.2 0.1 shard_map.132
  59.4 1.9 %collective-permute-start.11 = (f32[256,512]{1,0:T(8,128)S(1)}, f32[256,512]{1,0:T(8,128)S(1)}, u32[]{:S(2)}, u32[]{:S(2)}) collective-permute-start(f32[256,512]{1,0:T(8,128)S(1)} %get-tuple-element.52), channel_id=1, source_target_pairs={{0,2},{1,3},{2,0},{3,1},{4,6},{5,7},{6,4},{7,5},{8,10},{9,11},{10,... | collective-permute-start | bytes 1572872 | tf_op jit(solution)/shard_map/ppermute | solution.py:595
  61.3 2.9 %collective-permute-done.16.up1 = bf16[512,256]{1,0:T(8,128)(2,1)S(1)} collective-permute-done((bf16[512,256]{1,0:T(8,128)(2,1)S(1)}, bf16[512,256]{1,0:T(8,128)(2,1)S(1)}, u32[]{:S(2)}, u32[]{:S(2)}) %collective-permute-start.16) | collective-permute-done | bytes 262176 | tf_op jit(solution)/shard_map/ppermute | solution.py:585
  64.2 0.7 collective-permute-start.17
  64.8 3.6 %collective-permute-done.19.down1 = bf16[512,256]{1,0:T(8,128)(2,1)S(1)} collective-permute-done((bf16[512,256]{1,0:T(8,128)(2,1)S(1)}, bf16[512,256]{1,0:T(8,128)(2,1)S(1)}, u32[]{:S(2)}, u32[]{:S(2)}) %collective-permute-start.19) | collective-permute-done | bytes 262176 | tf_op jit(solution)/shard_map/ppermute | solution.py:586
  68.4 1.3 %collective-permute-start.20 = (bf16[512,256]{1,0:T(8,128)(2,1)S(1)}, bf16[512,256]{1,0:T(8,128)(2,1)S(1)}, u32[]{:S(2)}, u32[]{:S(2)}) collective-permute-start(bf16[512,256]{1,0:T(8,128)(2,1)S(1)} %collective-permute-done.19.down1), channel_id=1, source_target_pairs={{8,4},{4,0},{9,5},{5,1},{10,6},{6,2},{11,7},{7,3},{24,20},{20,16},... | collective-permute-start | bytes 786440 | tf_op jit(solution)/shard_map/ppermute | solution.py:586
  69.7 0.0 collective-permute-done.17.up2
  69.7 0.7 collective-permute-start.18
  70.4 8.7 %collective-permute-done.20.down2 = bf16[512,256]{1,0:T(8,128)(2,1)S(1)} collective-permute-done((bf16[512,256]{1,0:T(8,128)(2,1)S(1)}, bf16[512,256]{1,0:T(8,128)(2,1)S(1)}, u32[]{:S(2)}, u32[]{:S(2)}) %collective-permute-start.20) | collective-permute-done | bytes 262176 | tf_op jit(solution)/shard_map/ppermute | solution.py:586
  79.1 1.3 %collective-permute-start.21 = (bf16[512,256]{1,0:T(8,128)(2,1)S(1)}, bf16[512,256]{1,0:T(8,128)(2,1)S(1)}, u32[]{:S(2)}, u32[]{:S(2)}) collective-permute-start(bf16[512,256]{1,0:T(8,128)(2,1)S(1)} %collective-permute-done.20.down2), channel_id=1, source_target_pairs={{4,0},{5,1},{6,2},{7,3},{20,16},{21,17},{22,18},{23,19}} | collective-permute-start | bytes 786440 | tf_op jit(solution)/shard_map/ppermute | solution.py:586
  80.4 2.7 %collective-permute-start.12 = (bf16[256,256]{1,0:T(8,128)(2,1)S(1)}, bf16[256,256]{1,0:T(8,128)(2,1)S(1)}, u32[]{:S(2)}, u32[]{:S(2)}) collective-permute-start(bf16[256,256]{1,0:T(8,128)(2,1)S(1)} %get-tuple-element.48.refs_7_), channel_id=1, source_target_pairs={{0,4},{4,0},{8,12},{12,8},{1,5},{5,1},{9,13},{13,9},{2,6},{6,2},{1... | collective-permute-start | bytes 393224 | tf_op jit(solution)/shard_map/ppermute | solution.py:476
  83.1 0.0 collective-permute-start.13
  83.1 0.0 collective-permute-done.11.other_ref
  83.1 2.4 %collective-permute-start.14 = (bf16[256,256]{1,0:T(8,128)(2,1)S(1)}, bf16[256,256]{1,0:T(8,128)(2,1)S(1)}, u32[]{:S(2)}, u32[]{:S(2)}) collective-permute-start(bf16[256,256]{1,0:T(8,128)(2,1)S(1)} %get-tuple-element.56), channel_id=1, source_target_pairs={{0,12},{4,8},{8,4},{12,0},{1,13},{5,9},{9,5},{13,1},{2,14},{6,10},... | collective-permute-start | bytes 393224 | tf_op jit(solution)/shard_map/ppermute | solution.py:476
  85.5 0.7 shard_map.133.refs_3_
  86.3 10.6 %collective-permute-done.12.refs_1_.refs_0_ = bf16[256,256]{1,0:T(8,128)(2,1)S(1)} collective-permute-done((bf16[256,256]{1,0:T(8,128)(2,1)S(1)}, bf16[256,256]{1,0:T(8,128)(2,1)S(1)}, u32[]{:S(2)}, u32[]{:S(2)}) %collective-permute-start.12) | collective-permute-done | bytes 131104 | tf_op jit(solution)/shard_map/ppermute | solution.py:476
  96.9 0.0 collective-permute-done.13.refs_2_.refs_1_
  96.9 0.0 collective-permute-done.14.refs_3_.refs_2_
  96.9 0.0 collective-permute-done.18.up3
  96.9 0.0 collective-permute-done.21.down3
  96.9 0.0 all-gather.6.cloned.1.call-done
  96.9 0.0 copy-start.2
  97.0 0.9 copy-done.2
  97.9 1.2 copy-done.4
  99.1 1.1 shard_map.136.one_ref
  100.2 1.5 %collective-permute-start.22 = (bf16[512,512]{1,0:T(8,128)(2,1)S(1)}, bf16[512,512]{1,0:T(8,128)(2,1)S(1)}, u32[]{:S(2)}, u32[]{:S(2)}) collective-permute-start(bf16[512,512]{1,0:T(8,128)(2,1)S(1)} %shard_map.136.one_ref), channel_id=1, source_target_pairs={{0,16},{16,0},{1,17},{17,1},{2,18},{18,2},{3,19},{19,3},{4,20},{20... | collective-permute-start | bytes 1572872 | tf_op jit(solution)/shard_map/ppermute | solution.py:616
  101.7 0.9 shard_map.134
  102.7 0.5 collective-permute-start.15
  103.2 14.8 %collective-permute-done.15.other_ref = bf16[256,512]{1,0:T(8,128)(2,1)S(1)} collective-permute-done((bf16[256,512]{1,0:T(8,128)(2,1)S(1)}, bf16[256,512]{1,0:T(8,128)(2,1)S(1)}, u32[]{:S(2)}, u32[]{:S(2)}) %collective-permute-start.15) | collective-permute-done | bytes 262176 | tf_op jit(solution)/shard_map/ppermute | solution.py:641
  118.1 1.0 shard_map.135
  119.1 1.1 shard_map.137
  (23 shorter events, 0.0 us)
Async XLA Ops:
  7.2 31.1 %copy-start.10 = (bf16[2,256,256]{2,1,0:T(8,128)(2,1)S(1)}, bf16[2,256,256]{2,1,0:T(8,128)(2,1)}, u32[]{:S(2)}) copy-start(bf16[2,256,256]{2,1,0:T(8,128)(2,1)} %constant.4.clone.refs_4_.refs_5_) | copy-start | bytes 786436
  7.2 31.1 %copy-start.11 = (f32[128,128]{1,0:T(8,128)S(1)}, f32[128,128]{1,0:T(8,128)}, u32[]{:S(2)}) copy-start(f32[128,128]{1,0:T(8,128)} %constant.5.clone.refs_5_.refs_6_) | copy-start | bytes 196612
  7.2 21.9 %all-gather.4.cloned.1.call-start = ((), (), s32[]{:S(2)}) async-start(), calls=%async_computation | async-start | bytes 1310720 | tf_op jit(solution)/shard_map/all_gather | solution.py:495
  7.9 89.0 %all-gather.6.cloned.1.call-start = ((), (), s32[]{:S(2)}) async-start(), calls=%async_computation.1 | async-start | bytes 1310720 | tf_op jit(solution)/shard_map/all_gather | solution.py:547
  8.0 30.3 %collective-permute-start.3 = (bf16[256,512]{1,0:T(8,128)(2,1)}, bf16[256,512]{1,0:T(8,128)(2,1)S(1)}, u32[]{:S(2)}, u32[]{:S(2)}) collective-permute-start(bf16[256,512]{1,0:T(8,128)(2,1)} %bitcast.17), channel_id=1, source_target_pairs={{0,0},{1,4},{2,8},{3,12},{4,2},{5,6},{6,10},{7,14},{8,1},{9,5},{10... | collective-permute-start | bytes 786440 | tf_op jit(solution)/shard_map/ppermute | solution.py:497
  11.7 23.5 %collective-permute-start = (bf16[256,256]{1,0:T(8,128)(2,1)}, bf16[256,256]{1,0:T(8,128)(2,1)S(1)}, u32[]{:S(2)}, u32[]{:S(2)}) collective-permute-start(bf16[256,256]{1,0:T(8,128)(2,1)} %get-tuple-element.35), channel_id=1, source_target_pairs={{0,4},{4,0},{8,12},{12,8},{1,5},{5,1},{9,13},{13,9},{2,6},{6,2},{1... | collective-permute-start | bytes 393224 | tf_op jit(solution)/shard_map/ppermute | solution.py:476
  16.5 21.7 %collective-permute-start.1 = (bf16[256,256]{1,0:T(8,128)(2,1)}, bf16[256,256]{1,0:T(8,128)(2,1)S(1)}, u32[]{:S(2)}, u32[]{:S(2)}) collective-permute-start(bf16[256,256]{1,0:T(8,128)(2,1)} %get-tuple-element.36), channel_id=1, source_target_pairs={{0,8},{4,12},{8,0},{12,4},{1,9},{5,13},{9,1},{13,5},{2,10},{6,14},... | collective-permute-start | bytes 393224 | tf_op jit(solution)/shard_map/ppermute | solution.py:476
  18.3 19.9 %collective-permute-start.2 = (bf16[256,256]{1,0:T(8,128)(2,1)}, bf16[256,256]{1,0:T(8,128)(2,1)S(1)}, u32[]{:S(2)}, u32[]{:S(2)}) collective-permute-start(bf16[256,256]{1,0:T(8,128)(2,1)} %get-tuple-element.37), channel_id=1, source_target_pairs={{0,12},{4,8},{8,4},{12,0},{1,13},{5,9},{9,5},{13,1},{2,14},{6,10},... | collective-permute-start | bytes 393224 | tf_op jit(solution)/shard_map/ppermute | solution.py:476
  29.0 1.6 %copy-start = (bf16[512,2048]{1,0:T(8,128)(2,1)S(1)}, bf16[512,2048]{1,0:T(8,128)(2,1)}, u32[]{:S(2)}) copy-start(bf16[512,2048]{1,0:T(8,128)(2,1)} %refs_6_.2) | copy-start | bytes 6291460
  30.6 1.2 copy-start.3
  31.9 0.9 copy-start.5
  32.8 5.4 %copy-start.9 = (bf16[256,256]{1,0:T(8,128)(2,1)S(1)}, bf16[256,256]{1,0:T(8,128)(2,1)}, u32[]{:S(2)}) copy-start(bf16[256,256]{1,0:T(8,128)(2,1)} %get-tuple-element.34.refs_0_) | copy-start | bytes 393220
  33.6 14.9 %collective-permute-start.7 = (bf16[256,128]{1,0:T(8,128)(2,1)S(1)}, bf16[256,128]{1,0:T(8,128)(2,1)S(1)}, u32[]{:S(2)}, u32[]{:S(2)}) collective-permute-start(bf16[256,128]{1,0:T(8,128)(2,1)S(1)} %get-tuple-element.38.refs_7_), channel_id=1, source_target_pairs={{0,4},{4,0},{8,12},{12,8},{1,5},{5,1},{9,13},{13,9},{2,6},{6,2},{1... | collective-permute-start | bytes 196616 | tf_op jit(solution)/shard_map/ppermute | solution.py:476
  35.2 13.3 %collective-permute-start.8 = (bf16[256,128]{1,0:T(8,128)(2,1)S(1)}, bf16[256,128]{1,0:T(8,128)(2,1)S(1)}, u32[]{:S(2)}, u32[]{:S(2)}) collective-permute-start(bf16[256,128]{1,0:T(8,128)(2,1)S(1)} %get-tuple-element.45), channel_id=1, source_target_pairs={{0,8},{4,12},{8,0},{12,4},{1,9},{5,13},{9,1},{13,5},{2,10},{6,14},... | collective-permute-start | bytes 196616 | tf_op jit(solution)/shard_map/ppermute | solution.py:476
  38.2 10.3 %collective-permute-start.9 = (bf16[256,128]{1,0:T(8,128)(2,1)S(1)}, bf16[256,128]{1,0:T(8,128)(2,1)S(1)}, u32[]{:S(2)}, u32[]{:S(2)}) collective-permute-start(bf16[256,128]{1,0:T(8,128)(2,1)S(1)} %get-tuple-element.46), channel_id=1, source_target_pairs={{0,12},{4,8},{8,4},{12,0},{1,13},{5,9},{9,5},{13,1},{2,14},{6,10},... | collective-permute-start | bytes 196616 | tf_op jit(solution)/shard_map/ppermute | solution.py:476
  44.2 10.4 %copy-start.1 = (bf16[512,2048]{1,0:T(8,128)(2,1)S(1)}, bf16[512,2048]{1,0:T(8,128)(2,1)}, u32[]{:S(2)}) copy-start(bf16[512,2048]{1,0:T(8,128)(2,1)} %refs_6_.2) | copy-start | bytes 6291460
  44.2 10.4 %copy-start.6 = (bf16[1,256,512]{2,1,0:T(8,128)(2,1)S(1)}, bf16[1,256,512]{2,1,0:T(8,128)(2,1)}, u32[]{:S(2)}) copy-start(bf16[1,256,512]{2,1,0:T(8,128)(2,1)} %param.8) | copy-start | bytes 786436
  44.2 9.5 %collective-permute-start.4 = (bf16[256,128]{1,0:T(8,128)(2,1)S(1)}, bf16[256,128]{1,0:T(8,128)(2,1)S(1)}, u32[]{:S(2)}, u32[]{:S(2)}) collective-permute-start(bf16[256,128]{1,0:T(8,128)(2,1)S(1)} %get-tuple-element.40.refs_7_), channel_id=1, source_target_pairs={{0,4},{4,0},{8,12},{12,8},{1,5},{5,1},{9,13},{13,9},{2,6},{6,2},{1... | collective-permute-start | bytes 196616 | tf_op jit(solution)/shard_map/ppermute | solution.py:476
  44.8 8.9 %collective-permute-start.5 = (bf16[256,128]{1,0:T(8,128)(2,1)S(1)}, bf16[256,128]{1,0:T(8,128)(2,1)S(1)}, u32[]{:S(2)}, u32[]{:S(2)}) collective-permute-start(bf16[256,128]{1,0:T(8,128)(2,1)S(1)} %get-tuple-element.41), channel_id=1, source_target_pairs={{0,8},{4,12},{8,0},{12,4},{1,9},{5,13},{9,1},{13,5},{2,10},{6,14},... | collective-permute-start | bytes 196616 | tf_op jit(solution)/shard_map/ppermute | solution.py:476
  48.5 6.1 %collective-permute-start.6 = (bf16[256,128]{1,0:T(8,128)(2,1)S(1)}, bf16[256,128]{1,0:T(8,128)(2,1)S(1)}, u32[]{:S(2)}, u32[]{:S(2)}) collective-permute-start(bf16[256,128]{1,0:T(8,128)(2,1)S(1)} %get-tuple-element.42), channel_id=1, source_target_pairs={{0,12},{4,8},{8,4},{12,0},{1,13},{5,9},{9,5},{13,1},{2,14},{6,10},... | collective-permute-start | bytes 196616 | tf_op jit(solution)/shard_map/ppermute | solution.py:476
  56.4 2.9 %collective-permute-start.10 = (f32[2,256,512]{2,1,0:T(8,128)}, f32[2,256,512]{2,1,0:T(8,128)S(1)}, u32[]{:S(2)}, u32[]{:S(2)}) collective-permute-start(f32[2,256,512]{2,1,0:T(8,128)} %get-tuple-element.50), channel_id=1, source_target_pairs={{0,1},{1,0},{2,3},{3,2},{4,5},{5,4},{6,7},{7,6},{8,9},{9,8},{10,11... | collective-permute-start | bytes 3145736 | tf_op jit(solution)/shard_map/ppermute | solution.py:593
  56.4 7.8 %collective-permute-start.16 = (bf16[512,256]{1,0:T(8,128)(2,1)S(1)}, bf16[512,256]{1,0:T(8,128)(2,1)S(1)}, u32[]{:S(2)}, u32[]{:S(2)}) collective-permute-start(bf16[512,256]{1,0:T(8,128)(2,1)S(1)} %get-tuple-element.60.own_ref), channel_id=1, source_target_pairs={{0,4},{4,8},{8,12},{1,5},{5,9},{9,13},{2,6},{6,10},{10,14},{3,7},{... | collective-permute-start | bytes 786440 | tf_op jit(solution)/shard_map/ppermute | solution.py:585
  57.9 10.5 %collective-permute-start.19 = (bf16[512,256]{1,0:T(8,128)(2,1)S(1)}, bf16[512,256]{1,0:T(8,128)(2,1)S(1)}, u32[]{:S(2)}, u32[]{:S(2)}) collective-permute-start(bf16[512,256]{1,0:T(8,128)(2,1)S(1)} %get-tuple-element.60.own_ref), channel_id=1, source_target_pairs={{12,8},{8,4},{4,0},{13,9},{9,5},{5,1},{14,10},{10,6},{6,2},{15,11}... | collective-permute-start | bytes 786440 | tf_op jit(solution)/shard_map/ppermute | solution.py:586
  59.4 23.7 %collective-permute-start.11 = (f32[256,512]{1,0:T(8,128)S(1)}, f32[256,512]{1,0:T(8,128)S(1)}, u32[]{:S(2)}, u32[]{:S(2)}) collective-permute-start(f32[256,512]{1,0:T(8,128)S(1)} %get-tuple-element.52), channel_id=1, source_target_pairs={{0,2},{1,3},{2,0},{3,1},{4,6},{5,7},{6,4},{7,5},{8,10},{9,11},{10,... | collective-permute-start | bytes 1572872 | tf_op jit(solution)/shard_map/ppermute | solution.py:595
  64.2 5.5 %collective-permute-start.17 = (bf16[512,256]{1,0:T(8,128)(2,1)S(1)}, bf16[512,256]{1,0:T(8,128)(2,1)S(1)}, u32[]{:S(2)}, u32[]{:S(2)}) collective-permute-start(bf16[512,256]{1,0:T(8,128)(2,1)S(1)} %collective-permute-done.16.up1), channel_id=1, source_target_pairs={{4,8},{8,12},{5,9},{9,13},{6,10},{10,14},{7,11},{11,15},{20,24},{2... | collective-permute-start | bytes 786440 | tf_op jit(solution)/shard_map/ppermute | solution.py:585
  68.4 10.7 %collective-permute-start.20 = (bf16[512,256]{1,0:T(8,128)(2,1)S(1)}, bf16[512,256]{1,0:T(8,128)(2,1)S(1)}, u32[]{:S(2)}, u32[]{:S(2)}) collective-permute-start(bf16[512,256]{1,0:T(8,128)(2,1)S(1)} %collective-permute-done.19.down1), channel_id=1, source_target_pairs={{8,4},{4,0},{9,5},{5,1},{10,6},{6,2},{11,7},{7,3},{24,20},{20,16},... | collective-permute-start | bytes 786440 | tf_op jit(solution)/shard_map/ppermute | solution.py:586
  69.7 27.2 %collective-permute-start.18 = (bf16[512,256]{1,0:T(8,128)(2,1)S(1)}, bf16[512,256]{1,0:T(8,128)(2,1)S(1)}, u32[]{:S(2)}, u32[]{:S(2)}) collective-permute-start(bf16[512,256]{1,0:T(8,128)(2,1)S(1)} %collective-permute-done.17.up2), channel_id=1, source_target_pairs={{8,12},{9,13},{10,14},{11,15},{24,28},{25,29},{26,30},{27,31}} | collective-permute-start | bytes 786440 | tf_op jit(solution)/shard_map/ppermute | solution.py:585
  79.1 17.8 %collective-permute-start.21 = (bf16[512,256]{1,0:T(8,128)(2,1)S(1)}, bf16[512,256]{1,0:T(8,128)(2,1)S(1)}, u32[]{:S(2)}, u32[]{:S(2)}) collective-permute-start(bf16[512,256]{1,0:T(8,128)(2,1)S(1)} %collective-permute-done.20.down2), channel_id=1, source_target_pairs={{4,0},{5,1},{6,2},{7,3},{20,16},{21,17},{22,18},{23,19}} | collective-permute-start | bytes 786440 | tf_op jit(solution)/shard_map/ppermute | solution.py:586
  80.4 16.5 %collective-permute-start.12 = (bf16[256,256]{1,0:T(8,128)(2,1)S(1)}, bf16[256,256]{1,0:T(8,128)(2,1)S(1)}, u32[]{:S(2)}, u32[]{:S(2)}) collective-permute-start(bf16[256,256]{1,0:T(8,128)(2,1)S(1)} %get-tuple-element.48.refs_7_), channel_id=1, source_target_pairs={{0,4},{4,0},{8,12},{12,8},{1,5},{5,1},{9,13},{13,9},{2,6},{6,2},{1... | collective-permute-start | bytes 393224 | tf_op jit(solution)/shard_map/ppermute | solution.py:476
  83.1 13.8 %collective-permute-start.13 = (bf16[256,256]{1,0:T(8,128)(2,1)S(1)}, bf16[256,256]{1,0:T(8,128)(2,1)S(1)}, u32[]{:S(2)}, u32[]{:S(2)}) collective-permute-start(bf16[256,256]{1,0:T(8,128)(2,1)S(1)} %get-tuple-element.55), channel_id=1, source_target_pairs={{0,8},{4,12},{8,0},{12,4},{1,9},{5,13},{9,1},{13,5},{2,10},{6,14},... | collective-permute-start | bytes 393224 | tf_op jit(solution)/shard_map/ppermute | solution.py:476
  83.1 13.8 %collective-permute-start.14 = (bf16[256,256]{1,0:T(8,128)(2,1)S(1)}, bf16[256,256]{1,0:T(8,128)(2,1)S(1)}, u32[]{:S(2)}, u32[]{:S(2)}) collective-permute-start(bf16[256,256]{1,0:T(8,128)(2,1)S(1)} %get-tuple-element.56), channel_id=1, source_target_pairs={{0,12},{4,8},{8,4},{12,0},{1,13},{5,9},{9,5},{13,1},{2,14},{6,10},... | collective-permute-start | bytes 393224 | tf_op jit(solution)/shard_map/ppermute | solution.py:476
  85.5 16.2 %copy-start.7 = (bf16[1,256,512]{2,1,0:T(8,128)(2,1)S(1)}, bf16[1,256,512]{2,1,0:T(8,128)(2,1)}, u32[]{:S(2)}) copy-start(bf16[1,256,512]{2,1,0:T(8,128)(2,1)} %param.9) | copy-start | bytes 786436
  85.5 16.2 %copy-start.8 = (bf16[1,256,512]{2,1,0:T(8,128)(2,1)S(1)}, bf16[1,256,512]{2,1,0:T(8,128)(2,1)}, u32[]{:S(2)}) copy-start(bf16[1,256,512]{2,1,0:T(8,128)(2,1)} %param.10) | copy-start | bytes 786436
  96.9 1.0 copy-start.2
  97.9 1.2 copy-start.4
  100.2 18.9 %collective-permute-start.22 = (bf16[512,512]{1,0:T(8,128)(2,1)S(1)}, bf16[512,512]{1,0:T(8,128)(2,1)S(1)}, u32[]{:S(2)}, u32[]{:S(2)}) collective-permute-start(bf16[512,512]{1,0:T(8,128)(2,1)S(1)} %shard_map.136.one_ref), channel_id=1, source_target_pairs={{0,16},{16,0},{1,17},{17,1},{2,18},{18,2},{3,19},{19,3},{4,20},{20... | collective-permute-start | bytes 1572872 | tf_op jit(solution)/shard_map/ppermute | solution.py:616
  102.7 15.4 %collective-permute-start.15 = (bf16[256,512]{1,0:T(8,128)(2,1)S(1)}, bf16[256,512]{1,0:T(8,128)(2,1)S(1)}, u32[]{:S(2)}, u32[]{:S(2)}) collective-permute-start(bf16[256,512]{1,0:T(8,128)(2,1)S(1)} %get-tuple-element.59.one_ref), channel_id=1, source_target_pairs={{0,16},{16,0},{1,17},{17,1},{2,18},{18,2},{3,19},{19,3},{4,20},{20... | collective-permute-start | bytes 786440 | tf_op jit(solution)/shard_map/ppermute | solution.py:641
Sparse Core Ops, SparseCore 0:
  9.6 19.4 all-gather.3
  56.5 22.1 all-gather.5
where the time goes:
time: 127 us
  waiting for transfers between devices  52.4 us (41%)
  starting transfers between devices  33.8 us (27%)
  Pallas kernels  20.6 us (16%)
  between operations  14.3 us (11%)
  local copies, waits for them, and re-layouts  5.97 us (5%)
    ppermute x12, starting transfers between devices, exchange(): lax.ppermute(pieces[r], axis, [(d, d ^ r) for d in range(size)])  21.4 us
    pallas_call x11, Pallas kernels, call(): pl.pallas_call(kernel, out_shape=outs, in_specs=[anywhere if n in left el...  20.6 us
    ppermute x1, waiting for transfers between devices, local_short(): lax.ppermute(taps, 'dp', ring)  14.8 us
    ppermute x3, waiting for transfers between devices, local_short(): lax.ppermute(downs[-1], 'ctx', [(d, d - 1) for d in range(seqs - r, 0, -1)])  12.3 us
    ppermute x12, waiting for transfers between devices, exchange(): lax.ppermute(pieces[r], axis, [(d, d ^ r) for d in range(size)])  11.6 us
    all_gather x1, waiting for transfers between devices, local_short(): cot_rows = lax.all_gather(cot, 'tp')  10.1 us
    unnamed x24, local copies, waits for them, and re-layouts  5.97 us
    ppermute x3, starting transfers between devices, local_short(): lax.ppermute(downs[-1], 'ctx', [(d, d - 1) for d in range(seqs - r, 0, -1)])  3.85 us
  transfers between devices with their start and end apart: 25, of which 7 were waited for; matrix products, arithmetic and copies ran while one was open for 0% of the time, Pallas kernels for 13%

commit v1 on v0

--- a/solution.py
+++ b/solution.py
@@ -294,7 +294,7 @@
 def place_pieces(pieces, whole):
     me = lax.axis_index("ctx")
     for r, ref in enumerate(pieces):
-        whole[at_block(me ^ r, ref.shape[0]), :] = ref[...]
+        whole[at_block(me ^ r, ref.shape[0]), :] = ref[:, pl.ds(0, whole.shape[1])]
 
 
 def take_pieces(whole, pieces):
@@ -323,10 +323,9 @@
 
 
 def forward_kernel(seqs, *refs):
-    held, (matrix, turn, moved_ref), refs = refs[:seqs], refs[seqs : seqs + 3], refs[seqs + 4 :]
-    sent, (spec_ref, passed_ref, whole, zh, zl, turned, conv) = refs[:seqs], refs[seqs:]
+    held, (matrix, turn), refs = refs[:seqs], refs[seqs : seqs + 2], refs[seqs + 2 :]
+    sent, (spec_ref, whole, zh, zl, turned, conv) = refs[:seqs], refs[seqs:]
     blocks = spec_ref.shape[0] - 1
-    passed_ref[...] = moved_ref[...]
     place_pieces(held, whole)
     over_blocks(reader(whole), blocks, 2 * LANES, turn, zh, zl)
     for i in range(blocks + 1):
@@ -342,7 +341,7 @@
 
 
 def backward_kernel(seqs, *refs):
-    held, (spec_ref, matrix, turn), refs = refs[:seqs], refs[seqs : seqs + 3], refs[seqs + 4 :]
+    held, (spec_ref, matrix, turn), refs = refs[:seqs], refs[seqs : seqs + 3], refs[seqs + 5 :]
     sent, (whole, zh, zl, turned, back) = refs[:seqs], refs[seqs:]
     blocks = spec_ref.shape[0] - 1
     place_pieces(held, whole)
@@ -363,11 +362,12 @@
     take_pieces(back, sent)
 
 
-def gradient_kernel(cot_ref, w_ref, query_ref, gated_grad_ref, *pieces):
-    me = lax.axis_index("ctx")
-    width = cot_ref.shape[2]
+def gradient_kernel(cot_ref, w_ref, query_ref, _, gated_grad_ref, *pieces):
+    me, part = lax.axis_index("ctx"), lax.axis_index("tp")
+    parts, positions, width = cot_ref.shape
+    quarter = positions // parts
     total = None
-    for j in range(cot_ref.shape[0]):
+    for j in range(parts):
         term = lax.dot_general(
             cot_ref[j], w_ref[:, j * width : (j + 1) * width], (((1,), (1,)), ((), ())), preferred_element_type=F32
         )
@@ -375,7 +375,22 @@
     gated_grad_ref[...] = total
     for r, out_ref in enumerate(pieces):
         cols = at_block(me ^ r)
-        out_ref[...] = (gated_grad_ref[:, cols] * query_ref[:, cols].astype(F32)).astype(BF16)
+        out_ref[:, pl.ds(0, LANES)] = (gated_grad_ref[:, cols] * query_ref[:, cols].astype(F32)).astype(BF16)
+        for k in range(width // LANES):
+            out_ref[pl.ds(k * quarter, quarter), pl.ds(LANES, LANES)] = cot_ref[
+                me ^ r, at_block(part, quarter), pl.ds(k * LANES, LANES)
+            ]
+
+
+def quarter_kernel(seqs, *refs):
+    held, out_ref = refs[:seqs], refs[seqs]
+    me = lax.axis_index("ctx")
+    quarter = out_ref.shape[0] // seqs
+    for r, ref in enumerate(held):
+        for k in range(out_ref.shape[1] // LANES):
+            out_ref[at_block(me ^ r, quarter), pl.ds(k * LANES, LANES)] = ref[
+                pl.ds(k * quarter, quarter), pl.ds(LANES, LANES)
+            ]
 
 
 def output_kernel(seqs, *refs):
@@ -398,37 +413,46 @@
 def pair_kernel(keep_ref, other_ref, mine_ref, far_ref):
     y = lax.axis_index("tp") >> 1
     mine_ref[...] = keep_ref[y] + other_ref[y]
-    far_ref[...] = keep_ref[y ^ 1] + other_ref[y ^ 1]
+    far_ref[...] = (keep_ref[y ^ 1] + other_ref[y ^ 1]).astype(BF16)
 
 
 def sum_kernel(mine_ref, other_ref, out_ref):
-    out_ref[...] = (mine_ref[...] + other_ref[...]).astype(BF16)
-
-
-def weight_kernel(own_ref, up1, up2, up3, down1, down2, down3, cot_ref, *refs):
-    out_ref, gated, cot, sems = refs[-4:]
+    out_ref[...] = (mine_ref[...] + other_ref[...].astype(F32)).astype(BF16)
+
+
+def pick_kernel(up_ref, down_ref, _, out_ref):
+    high = lax.axis_index("ctx") >= 2
+
+    @pl.when(high)
+    def _():
+        out_ref[...] = up_ref[...]
+
+    @pl.when(jnp.logical_not(high))
+    def _():
+        out_ref[...] = down_ref[...]
+
+
+def weight_kernel(own_ref, up_ref, down_ref, two_ref, end_ref, cot_ref, *refs):
+    out_ref, total, cot = refs[-3:]
     me = lax.axis_index("ctx")
-    seqs, size = cot_ref.shape[0], cot_ref.shape[1]
-    blocks = [(cot_ref.at[p], cot.at[pl.ds(target_of(p) * size, size), :]) for p in range(seqs)]
-    cot_copies = fetch([(own_ref, gated.at[0])] + blocks, sems)
-    for r, (up, down) in enumerate(((up1, down3), (up2, down2), (up3, down1)), 1):
-
-        @pl.when(me >= r)
-        def _():
-            pltpu.make_async_copy(up, gated.at[r], sems.at[seqs + r]).start()
-
-        @pl.when(me < r)
-        def _():
-            pltpu.make_async_copy(down, gated.at[r], sems.at[seqs + r]).start()
-
-    for copy in cot_copies:
-        copy.wait()
-    total = jnp.dot(gated[0], cot[at_block(me, size), :], preferred_element_type=F32)
-    for r in range(1, seqs):
-        pltpu.make_async_copy(up1, gated.at[r], sems.at[seqs + r]).wait()
-        block = lax.rem(me + (seqs - r), seqs)
-        total = total + jnp.dot(gated[r], cot[at_block(block, size), :], preferred_element_type=F32)
-    out_ref[...] = total.astype(BF16)
+    parts = cot_ref.shape[0]
+    quarter = cot_ref.shape[1] // parts
+    top = parts - 1
+
+    def term(gated_ref, block):
+        for p in range(parts):
+            cot[pl.ds(p * quarter, quarter), :] = cot_ref[p, at_block(block, quarter), :]
+        return jnp.dot(gated_ref[...], cot[...], preferred_element_type=F32)
+
+    def add(gated_ref, block):
+        total[...] += term(gated_ref, block)
+
+    total[...] = term(own_ref, me)
+    add(two_ref, me ^ 2)
+    pl.when(me > 0)(lambda: add(up_ref, me - 1))
+    pl.when(me < top)(lambda: add(down_ref, me + 1))
+    pl.when(jnp.logical_or(me == 0, me == top))(lambda: add(end_ref, top - me))
+    out_ref[...] = total[...].astype(BF16)
 
 
 def add_kernel(factor, one_ref, other_ref, out_ref):
@@ -465,10 +489,6 @@
         cost_estimate=pl.CostEstimate(flops=flops, bytes_accessed=moved, transcendentals=0),
         compiler_params=pltpu.CompilerParams(vmem_limit_bytes=room * 2**20),
     )(*args)
-
-
-def target_of(block):
-    return ((block & 1) << 1) | (block >> 1)
 
 
 def exchange(pieces, axis):
@@ -493,9 +513,6 @@
     line = seqs * positions
 
     cot_rows = lax.all_gather(cot, "tp")
-    swap = [(z * parts + j, j * parts + target_of(z)) for z in range(seqs) for j in range(parts)]
-    cot_moved = lax.ppermute(cot, ("ctx", "tp"), swap)
-
     sent = call(
         prepare_kernel,
         two,
@@ -515,26 +532,13 @@
     )
     held = exchange(sent, "ctx")
 
-    gated_grad, *conv_grad = call(
-        gradient_kernel,
-        [shape_of(rows, F32)] + one,
-        2 * positions * channels * features,
-        5 * 10**6,
-        cot_rows,
-        w_out,
-        query,
-    )
-    grad_held = exchange(conv_grad, "ctx")
-
-    *conv_sent, spec, cot_passed = call(
+    *conv_sent, spec = call(
         functools.partial(forward_kernel, seqs),
-        one + [shape_of(table + (2 * LANES,), F32), shape_of(cot.shape, BF16)],
+        one + [shape_of(table + (2 * LANES,), F32)],
         10**9,
         9 * 10**6,
         *held,
         *tables,
-        cot_moved,
-        conv_grad[1],
         scratch=[
             pltpu.VMEM((line, 2 * LANES), BF16),
             pltpu.VMEM(table + (2 * LANES,), BF16),
@@ -542,30 +546,25 @@
             pltpu.VMEM(table + (LANES,), F32),
             pltpu.VMEM((line, LANES), BF16),
         ],
-        left=(seqs + 3,),
-    )
-    cot_cols = lax.all_gather(cot_passed, "tp")
+    )
     conv = exchange(conv_sent, "ctx")
 
-    back_sent = call(
-        functools.partial(backward_kernel, seqs),
-        two,
-        10**9,
-        9 * 10**6,
-        *grad_held,
-        spec,
-        *tables,
+    gated_grad, *conv_grad = call(
+        gradient_kernel,
+        [shape_of(rows, F32)] + two,
+        2 * positions * channels * features,
+        5 * 10**6,
+        cot_rows,
+        w_out,
+        query,
         conv_sent[1],
-        scratch=[
-            pltpu.VMEM((line, LANES), BF16),
-            pltpu.VMEM(table + (LANES,), BF16),
-            pltpu.VMEM(table + (LANES,), BF16),
-            pltpu.VMEM(table + (2 * LANES,), F32),
-            pltpu.VMEM((line, 2 * LANES), BF16),
-        ],
-        left=(seqs + 3,),
-    )
-    back = exchange(back_sent, "ctx")
+        left=(3,),
+    )
+    grad_held = exchange(conv_grad, "ctx")
+    cot_quarters = call(
+        functools.partial(quarter_kernel, seqs), shape_of((positions, width), BF16), 10**6, 10**6, *grad_held
+    )
+    cot_cols = lax.all_gather(cot_quarters, "tp")
 
     turned, grad_query, share_kept, share_sent = call(
         functools.partial(output_kernel, seqs),
@@ -576,17 +575,43 @@
         query,
         gated_grad,
         w_out,
-        back_sent[1],
+        grad_held[1],
         scratch=[pltpu.VMEM(rows, BF16)],
-        left=(seqs + 3,),
+        left=range(seqs + 3, seqs + 4),
     )
     ups, downs = [turned], [turned]
-    for r in range(1, seqs):
+    for r in (1, 2):
         ups.append(lax.ppermute(ups[-1], "ctx", [(d, d + 1) for d in range(r - 1, seqs - 1)]))
         downs.append(lax.ppermute(downs[-1], "ctx", [(d, d - 1) for d in range(seqs - r, 0, -1)]))
+
+    back_sent = call(
+        functools.partial(backward_kernel, seqs),
+        two,
+        10**9,
+        9 * 10**6,
+        *grad_held,
+        spec,
+        *tables,
+        turned,
+        cot_quarters,
+        scratch=[
+            pltpu.VMEM((line, LANES), BF16),
+            pltpu.VMEM(table + (LANES,), BF16),
+            pltpu.VMEM(table + (LANES,), BF16),
+            pltpu.VMEM(table + (2 * LANES,), F32),
+            pltpu.VMEM((line, 2 * LANES), BF16),
+        ],
+        left=(seqs + 3, seqs + 4),
+    )
+    back = exchange(back_sent, "ctx")
+
+    two_away = call(pick_kernel, shape_of((channels, positions), BF16), 10**6, 10**6, ups[2], downs[2], back[1], left=(2,))
+    end_away = lax.ppermute(two_away, "ctx", [(1, 0), (2, 3)])
+
+
     mine, far = call(
         pair_kernel,
-        [shape_of((positions, width), F32)] * 2,
+        [shape_of((positions, width), F32), shape_of((positions, width), BF16)],
         10**6,
         3 * 10**6,
         share_kept,
@@ -595,23 +620,31 @@
     far = lax.ppermute(far, "tp", [(j, j ^ 2) for j in range(parts)])
     output = call(sum_kernel, shape_of((positions, width), BF16), 10**6, 2 * 10**6, mine, far)
 
+    grad_key, grad_value, taps = call(
+        functools.partial(mixed_kernel, seqs),
+        [shape_of(rows, BF16)] * 3,
+        10**6,
+        2 * 10**6,
+        *back,
+        key,
+        value,
+    )
+    taps_other = lax.ppermute(taps, "dp", ring)
     weight_grad = call(
         weight_kernel,
         shape_of((channels, width), BF16),
         2 * line * channels * width,
         3 * 10**6,
         turned,
-        *ups[1:],
-        *downs[1:],
+        ups[1],
+        downs[1],
+        two_away,
+        end_away,
         cot_cols,
-        *back[1:],
-        output,
-        scratch=[
-            pltpu.VMEM((seqs, channels, positions), BF16),
-            pltpu.VMEM((line, width), BF16),
-            pltpu.SemaphoreType.DMA((2 * seqs,)),
-        ],
-        left=range(2 * seqs + 4),
+        taps,
+        mine,
+        scratch=[pltpu.VMEM((channels, width), F32), pltpu.VMEM((positions, width), BF16)],
+        left=range(6, 8),
     )
     weight_other = lax.ppermute(weight_grad, "dp", ring)
     grad_wout = call(
@@ -623,22 +656,13 @@
         weight_other,
     )
 
-    grad_key, grad_value, taps = call(
-        functools.partial(mixed_kernel, seqs),
-        [shape_of(rows, BF16)] * 3,
-        10**6,
-        2 * 10**6,
-        *back,
-        key,
-        value,
-    )
     grad_filter = call(
         functools.partial(taps_kernel, factor),
         shape_of((channels, positions), F32),
         10**6,
         10**6,
         taps,
-        lax.ppermute(taps, "dp", ring),
+        taps_other,
     )
     return (output[None], grad_query[None], grad_key[None], grad_value[None], grad_filter, grad_wout)
 
@@ -649,10 +673,10 @@
     short = (
         channels == seqs * LANES
         and positions % LANES == 0
+        and args[4].shape[1] == parts * parts * LANES
         and positions * seqs <= 8 * LANES
         and seqs == parts == 4
         and pairs == 2
-        and args[4].shape[1] % (parts * LANES) == 0
     )
     return (local_short if short else local_any_length)(*args)
 

time: 127 us -> 137 us (1.079); the launches traced: 127 us -> 134 us
  local copies, waits for them, and re-layouts: 5.97 us -> 11.1 us
  waiting for transfers between devices: 52.4 us -> 57 us
  starting transfers between devices: 33.8 us -> 32.1 us
    ppermute x12, waiting for transfers between devices: 11.6 us -> 36.2 us  [exchange(): lax.ppermute(pieces[r], axis, [(d, d ^ r) for d in range(size)])]
    all_gather x1, waiting for transfers between devices: 10.1 us -> 0.01 us  [local_short(): cot_rows = lax.all_gather(cot, 'tp')]
    ppermute x3 -> x2, waiting for transfers between devices: 12.3 us -> 3.46 us  [local_short(): lax.ppermute(downs[-1], 'ctx', [(d, d - 1) for d in range(seqs - r, 0, -1)])]
    unnamed x24 -> x36, local copies, waits for them, and re-layouts: 5.97 us -> 11.1 us
    ppermute x2, waiting for transfers between devices: 14.8 us -> 11.6 us  [the longest x1 11.6 us: local_short(): taps_other = lax.ppermute(taps, 'dp', ring)]
    ppermute x3 -> x2, waiting for transfers between devices: 2.92 us -> 4.99 us  [local_short(): lax.ppermute(ups[-1], 'ctx', [(d, d + 1) for d in range(r - 1, seqs - 1)])]
    ppermute x3 -> x2, starting transfers between devices: 3.85 us -> 2.57 us  [local_short(): lax.ppermute(downs[-1], 'ctx', [(d, d - 1) for d in range(seqs - r, 0, -1)])]
    ppermute x3 -> x2, starting transfers between devices: 2.88 us -> 2.16 us  [local_short(): lax.ppermute(ups[-1], 'ctx', [(d, d + 1) for d in range(r - 1, seqs - 1)])]
  transfers between devices with their start and end apart: 25 -> 23, of which waited for: 7 -> 12; matrix products, arithmetic and copies ran while one was open for 0% -> 0% of each run, Pallas kernels for 13% -> 12%
where the time goes in v1:
time: 137 us; the launch traced here: 134 us
  waiting for transfers between devices  57 us (42%)
  starting transfers between devices  32.1 us (23%)
  Pallas kernels  20 us (15%)
  between operations  14.3 us (10%)
  local copies, waits for them, and re-layouts  11.1 us (8%)
    ppermute x12, waiting for transfers between devices, exchange(): lax.ppermute(pieces[r], axis, [(d, d ^ r) for d in range(size)])  36.2 us
    ppermute x12, starting transfers between devices, exchange(): lax.ppermute(pieces[r], axis, [(d, d ^ r) for d in range(size)])  22.4 us
    pallas_call x13, Pallas kernels, call(): pl.pallas_call(kernel, out_shape=outs, in_specs=[anywhere if n in left el...  20 us
    ppermute x1, waiting for transfers between devices, local_short(): taps_other = lax.ppermute(taps, 'dp', ring)  11.6 us
    unnamed x36, local copies, waits for them, and re-layouts  11.1 us
    ppermute x2, waiting for transfers between devices, local_short(): lax.ppermute(ups[-1], 'ctx', [(d, d + 1) for d in range(r - 1, seqs - 1)])  4.99 us
    ppermute x2, waiting for transfers between devices, local_short(): lax.ppermute(downs[-1], 'ctx', [(d, d - 1) for d in range(seqs - r, 0, -1)])  3.46 us
  transfers between devices with their start and end apart: 23, of which 12 were waited for; matrix products, arithmetic and copies ran while one was open for 0% of the time, Pallas kernels for 12%

profile of v1, /device:TPU:0, one launch (start us, length us, event | category | flops | bytes accessed | tf_op | source)
XLA Modules:
  0.0 134.5 jit_solution(12564589261157362627)
XLA Ops:
  7.2 0.0 all-gather.4.cloned.1.call-start
  7.2 0.7 all-gather.4.cloned.1.call-update
  7.9 0.0 all-gather.6.cloned.1.call-start
  8.0 2.3 %shard_map.127 = (bf16[256,256]{1,0:T(8,128)(2,1)}, bf16[256,256]{1,0:T(8,128)(2,1)}, bf16[256,256]{1,0:T(8,128)(2,1)}, bf16[256,256]{1,0:T(8,128)(2,1)}) custom-call(bf16[256,512]{1,0:T(8,128)(2,1)} %bitcast.11, bf16[256,512]{1,0:T(8,128)(2,1)} %bitcast.13, f32[512,256]{1,0:T(8,128)} %refs_2_.1), custom_call_target="tpu_custom_call" | custom-call | flops 1000000 | bytes 2000000 | tf_op jit(solution)/shard_map/pallas_call | solution.py:483
  10.3 3.1 %collective-permute-start = (bf16[256,256]{1,0:T(8,128)(2,1)}, bf16[256,256]{1,0:T(8,128)(2,1)S(1)}, u32[]{:S(2)}, u32[]{:S(2)}) collective-permute-start(bf16[256,256]{1,0:T(8,128)(2,1)} %get-tuple-element.34), channel_id=1, source_target_pairs={{0,4},{4,0},{8,12},{12,8},{1,5},{5,1},{9,13},{13,9},{2,6},{6,2},{1... | collective-permute-start | bytes 393224 | tf_op jit(solution)/shard_map/ppermute | solution.py:496
  13.3 2.6 %collective-permute-start.1 = (bf16[256,256]{1,0:T(8,128)(2,1)}, bf16[256,256]{1,0:T(8,128)(2,1)S(1)}, u32[]{:S(2)}, u32[]{:S(2)}) collective-permute-start(bf16[256,256]{1,0:T(8,128)(2,1)} %get-tuple-element.35), channel_id=1, source_target_pairs={{0,8},{4,12},{8,0},{12,4},{1,9},{5,13},{9,1},{13,5},{2,10},{6,14},... | collective-permute-start | bytes 393224 | tf_op jit(solution)/shard_map/ppermute | solution.py:496
  15.9 2.6 %collective-permute-done.refs_1_ = bf16[256,256]{1,0:T(8,128)(2,1)S(1)} collective-permute-done((bf16[256,256]{1,0:T(8,128)(2,1)}, bf16[256,256]{1,0:T(8,128)(2,1)S(1)}, u32[]{:S(2)}, u32[]{:S(2)}) %collective-permute-start) | collective-permute-done | bytes 131104 | tf_op jit(solution)/shard_map/ppermute | solution.py:496
  18.6 7.9 %collective-permute-done.1.refs_2_ = bf16[256,256]{1,0:T(8,128)(2,1)S(1)} collective-permute-done((bf16[256,256]{1,0:T(8,128)(2,1)}, bf16[256,256]{1,0:T(8,128)(2,1)S(1)}, u32[]{:S(2)}, u32[]{:S(2)}) %collective-permute-start.1) | collective-permute-done | bytes 131104 | tf_op jit(solution)/shard_map/ppermute | solution.py:496
  26.5 0.0 collective-permute-done.2.refs_3_
  26.5 0.9 copy-done.10
  27.4 0.8 copy-done.12
  28.3 0.9 copy-done.16
  29.2 5.2 %shard_map.128 = (bf16[256,128]{1,0:T(8,128)(2,1)S(1)}, bf16[256,128]{1,0:T(8,128)(2,1)S(1)}, bf16[256,128]{1,0:T(8,128)(2,1)S(1)}, bf16[256,128]{1,0:T(8,128)(2,1)S(1)}, f32[9,256,256]{2,1,0:T(8,128)S(1)}) custom-call(bf16[256,256]{1,0:T(8,128)(2,1)S(1)} %copy-done.16, bf16[256,256]{1,0:T(8,128)(2,1)S(1)} %collective-permute-done.refs_1_, ...), custom_call_target="tpu_custom_call" | custom-call | flops 1000000000 | bytes 9000000 | tf_op jit(solution)/shard_map/pallas_call | solution.py:483
  34.4 1.4 %copy-done.1 = f32[9,256,256]{2,1,0:T(8,128)} copy-done((f32[9,256,256]{2,1,0:T(8,128)}, f32[9,256,256]{2,1,0:T(8,128)S(1)}, u32[]{:S(2)}) %copy-start.1) | copy-done | bytes 2359320
  35.8 0.6 copy-done.14
  36.4 0.6 copy-done.17
  37.0 1.2 copy-done.4
  38.3 0.9 shard_map.129
  39.1 2.0 %collective-permute-start.6 = (bf16[256,256]{1,0:T(8,128)(2,1)S(1)}, bf16[256,256]{1,0:T(8,128)(2,1)S(1)}, u32[]{:S(2)}, u32[]{:S(2)}) collective-permute-start(bf16[256,256]{1,0:T(8,128)(2,1)S(1)} %get-tuple-element.42), channel_id=1, source_target_pairs={{0,4},{4,0},{8,12},{12,8},{1,5},{5,1},{9,13},{13,9},{2,6},{6,2},{1... | collective-permute-start | bytes 393224 | tf_op jit(solution)/shard_map/ppermute | solution.py:496
  41.2 2.5 %collective-permute-start.10 = (bf16[256,256]{1,0:T(8,128)(2,1)S(1)}, bf16[256,256]{1,0:T(8,128)(2,1)S(1)}, u32[]{:S(2)}, u32[]{:S(2)}) collective-permute-start(bf16[256,256]{1,0:T(8,128)(2,1)S(1)} %get-tuple-element.50), channel_id=1, source_target_pairs={{0,12},{4,8},{8,4},{12,0},{1,13},{5,9},{9,5},{13,1},{2,14},{6,10},... | collective-permute-start | bytes 393224 | tf_op jit(solution)/shard_map/ppermute | solution.py:496
  43.6 0.0 collective-permute-start.9
  43.6 1.2 collective-permute-done.6.refs_7_.refs_1_
  44.9 5.3 %collective-permute-done.10.refs_3_ = bf16[256,256]{1,0:T(8,128)(2,1)S(1)} collective-permute-done((bf16[256,256]{1,0:T(8,128)(2,1)S(1)}, bf16[256,256]{1,0:T(8,128)(2,1)S(1)}, u32[]{:S(2)}, u32[]{:S(2)}) %collective-permute-start.10) | collective-permute-done | bytes 131104 | tf_op jit(solution)/shard_map/ppermute | solution.py:496
  50.2 3.9 %collective-permute-done.9.refs_2_ = bf16[256,256]{1,0:T(8,128)(2,1)S(1)} collective-permute-done((bf16[256,256]{1,0:T(8,128)(2,1)S(1)}, bf16[256,256]{1,0:T(8,128)(2,1)S(1)}, u32[]{:S(2)}, u32[]{:S(2)}) %collective-permute-start.9) | collective-permute-done | bytes 131104 | tf_op jit(solution)/shard_map/ppermute | solution.py:496
  54.1 0.8 shard_map.133.refs_8_
  54.8 0.7 copy-done.8
  55.5 0.0 all-gather.6.cloned.1.call-update
  55.5 0.1 collective-permute-start.3
  55.6 3.0 %collective-permute-start.4 = (bf16[256,128]{1,0:T(8,128)(2,1)}, bf16[256,128]{1,0:T(8,128)(2,1)S(1)}, u32[]{:S(2)}, u32[]{:S(2)}) collective-permute-start(bf16[256,128]{1,0:T(8,128)(2,1)} %copy-done.17), channel_id=1, source_target_pairs={{0,8},{4,12},{8,0},{12,4},{1,9},{5,13},{9,1},{13,5},{2,10},{6,14},... | collective-permute-start | bytes 196616 | tf_op jit(solution)/shard_map/ppermute | solution.py:496
  58.6 1.4 %collective-permute-start.5 = (bf16[256,128]{1,0:T(8,128)(2,1)S(1)}, bf16[256,128]{1,0:T(8,128)(2,1)S(1)}, u32[]{:S(2)}, u32[]{:S(2)}) collective-permute-start(bf16[256,128]{1,0:T(8,128)(2,1)S(1)} %get-tuple-element.40), channel_id=1, source_target_pairs={{0,12},{4,8},{8,4},{12,0},{1,13},{5,9},{9,5},{13,1},{2,14},{6,10},... | collective-permute-start | bytes 196616 | tf_op jit(solution)/shard_map/ppermute | solution.py:496
  60.0 0.0 collective-permute-done.3.refs_1_
  60.0 2.8 %collective-permute-done.4.refs_2_ = bf16[256,128]{1,0:T(8,128)(2,1)S(1)} collective-permute-done((bf16[256,128]{1,0:T(8,128)(2,1)}, bf16[256,128]{1,0:T(8,128)(2,1)S(1)}, u32[]{:S(2)}, u32[]{:S(2)}) %collective-permute-start.4) | collective-permute-done | bytes 65568 | tf_op jit(solution)/shard_map/ppermute | solution.py:496
  62.8 1.8 %collective-permute-done.5.refs_3_ = bf16[256,128]{1,0:T(8,128)(2,1)S(1)} collective-permute-done((bf16[256,128]{1,0:T(8,128)(2,1)S(1)}, bf16[256,128]{1,0:T(8,128)(2,1)S(1)}, u32[]{:S(2)}, u32[]{:S(2)}) %collective-permute-start.5) | collective-permute-done | bytes 65568 | tf_op jit(solution)/shard_map/ppermute | solution.py:496
  64.7 0.8 copy-done.15
  65.5 0.9 shard_map.130
  66.4 1.5 %collective-permute-start.15 = (bf16[512,256]{1,0:T(8,128)(2,1)S(1)}, bf16[512,256]{1,0:T(8,128)(2,1)S(1)}, u32[]{:S(2)}, u32[]{:S(2)}) collective-permute-start(bf16[512,256]{1,0:T(8,128)(2,1)S(1)} %get-tuple-element.52.refs_7_.own_ref), channel_id=1, source_target_pairs={{0,4},{4,8},{8,12},{1,5},{5,9},{9,13},{2,6},{6,10},{10,14},{3,7},{... | collective-permute-start | bytes 786440 | tf_op jit(solution)/shard_map/ppermute | solution.py:584
  67.9 1.3 collective-permute-start.16
  69.2 5.0 %collective-permute-done.15.up_ref = bf16[512,256]{1,0:T(8,128)(2,1)S(1)} collective-permute-done((bf16[512,256]{1,0:T(8,128)(2,1)S(1)}, bf16[512,256]{1,0:T(8,128)(2,1)S(1)}, u32[]{:S(2)}, u32[]{:S(2)}) %collective-permute-start.15) | collective-permute-done | bytes 262176 | tf_op jit(solution)/shard_map/ppermute | solution.py:584
  74.2 0.7 collective-permute-start.17
  74.9 3.5 %collective-permute-done.16.down_ref = bf16[512,256]{1,0:T(8,128)(2,1)S(1)} collective-permute-done((bf16[512,256]{1,0:T(8,128)(2,1)S(1)}, bf16[512,256]{1,0:T(8,128)(2,1)S(1)}, u32[]{:S(2)}, u32[]{:S(2)}) %collective-permute-start.16) | collective-permute-done | bytes 262176 | tf_op jit(solution)/shard_map/ppermute | solution.py:585
  78.3 1.3 collective-permute-start.18
  79.7 0.0 copy-start.11
  79.7 0.9 copy-done.11
  80.6 0.8 copy-done.13
  81.4 5.1 %shard_map.134 = (bf16[256,256]{1,0:T(8,128)(2,1)S(1)}, bf16[256,256]{1,0:T(8,128)(2,1)S(1)}, bf16[256,256]{1,0:T(8,128)(2,1)S(1)}, bf16[256,256]{1,0:T(8,128)(2,1)S(1)}) custom-call(bf16[256,256]{1,0:T(8,128)(2,1)S(1)} %get-tuple-element.48.refs_0_, bf16[256,256]{1,0:T(8,128)(2,1)S(1)} %collective-permute-done.6.refs_7_.refs_1_, ...), custom_call_target="tpu_custom_call" | custom-call | flops 1000000000 | bytes 9000000 | tf_op jit(solution)/shard_map/pallas_call | solution.py:483
  86.5 2.7 %collective-permute-start.11 = (bf16[256,256]{1,0:T(8,128)(2,1)S(1)}, bf16[256,256]{1,0:T(8,128)(2,1)S(1)}, u32[]{:S(2)}, u32[]{:S(2)}) collective-permute-start(bf16[256,256]{1,0:T(8,128)(2,1)S(1)} %get-tuple-element.54), channel_id=1, source_target_pairs={{0,4},{4,0},{8,12},{12,8},{1,5},{5,1},{9,13},{13,9},{2,6},{6,2},{1... | collective-permute-start | bytes 393224 | tf_op jit(solution)/shard_map/ppermute | solution.py:496
  89.2 2.9 %collective-permute-done.11.refs_1_._ = bf16[256,256]{1,0:T(8,128)(2,1)S(1)} collective-permute-done((bf16[256,256]{1,0:T(8,128)(2,1)S(1)}, bf16[256,256]{1,0:T(8,128)(2,1)S(1)}, u32[]{:S(2)}, u32[]{:S(2)}) %collective-permute-start.11) | collective-permute-done | bytes 131104 | tf_op jit(solution)/shard_map/ppermute | solution.py:496
  92.2 0.0 collective-permute-done.17.up_ref
  92.2 1.3 collective-permute-start.19
  93.5 4.1 %collective-permute-start.12 = (bf16[256,256]{1,0:T(8,128)(2,1)S(1)}, bf16[256,256]{1,0:T(8,128)(2,1)S(1)}, u32[]{:S(2)}, u32[]{:S(2)}) collective-permute-start(bf16[256,256]{1,0:T(8,128)(2,1)S(1)} %get-tuple-element.55), channel_id=1, source_target_pairs={{0,8},{4,12},{8,0},{12,4},{1,9},{5,13},{9,1},{13,5},{2,10},{6,14},... | collective-permute-start | bytes 393224 | tf_op jit(solution)/shard_map/ppermute | solution.py:496
  97.6 1.0 collective-permute-start.13
  98.6 7.6 %collective-permute-done.12.refs_2_ = bf16[256,256]{1,0:T(8,128)(2,1)S(1)} collective-permute-done((bf16[256,256]{1,0:T(8,128)(2,1)S(1)}, bf16[256,256]{1,0:T(8,128)(2,1)S(1)}, u32[]{:S(2)}, u32[]{:S(2)}) %collective-permute-start.12) | collective-permute-done | bytes 131104 | tf_op jit(solution)/shard_map/ppermute | solution.py:496
  106.2 0.9 shard_map.135
  107.1 0.1 shard_map.131
  107.2 0.0 all-gather.6.cloned.1.call-done
  107.3 1.2 copy-done.3
  108.5 1.1 shard_map.138.one_ref
  109.6 1.5 %collective-permute-start.20 = (bf16[512,512]{1,0:T(8,128)(2,1)S(1)}, bf16[512,512]{1,0:T(8,128)(2,1)S(1)}, u32[]{:S(2)}, u32[]{:S(2)}) collective-permute-start(bf16[512,512]{1,0:T(8,128)(2,1)S(1)} %shard_map.138.one_ref), channel_id=1, source_target_pairs={{0,16},{16,0},{1,17},{17,1},{2,18},{18,2},{3,19},{19,3},{4,20},{20... | collective-permute-start | bytes 1572872 | tf_op jit(solution)/shard_map/ppermute | solution.py:649
  111.1 0.5 collective-permute-start.14
  111.7 1.5 %collective-permute-start.8 = (bf16[256,512]{1,0:T(8,128)(2,1)S(1)}, bf16[256,512]{1,0:T(8,128)(2,1)S(1)}, u32[]{:S(2)}, u32[]{:S(2)}) collective-permute-start(bf16[256,512]{1,0:T(8,128)(2,1)S(1)} %get-tuple-element.46), channel_id=1, source_target_pairs={{0,2},{1,3},{2,0},{3,1},{4,6},{5,7},{6,4},{7,5},{8,10},{9,11},{10,... | collective-permute-start | bytes 786440 | tf_op jit(solution)/shard_map/ppermute | solution.py:620
  113.2 11.6 %collective-permute-done.14.other_ref = bf16[256,512]{1,0:T(8,128)(2,1)S(1)} collective-permute-done((bf16[256,512]{1,0:T(8,128)(2,1)S(1)}, bf16[256,512]{1,0:T(8,128)(2,1)S(1)}, u32[]{:S(2)}, u32[]{:S(2)}) %collective-permute-start.14) | collective-permute-done | bytes 262176 | tf_op jit(solution)/shard_map/ppermute | solution.py:632
  124.8 1.0 shard_map.136
  125.8 0.7 shard_map.132
  126.5 1.1 shard_map.139
  (33 shorter events, 0.1 us)
Async XLA Ops:
  7.2 29.9 %all-gather.4.cloned.1.call-start = ((), (), s32[]{:S(2)}) async-start(), calls=%async_computation | async-start | bytes 1310720 | tf_op jit(solution)/shard_map/all_gather | solution.py:515
  7.9 99.4 %all-gather.6.cloned.1.call-start = ((), (), s32[]{:S(2)}) async-start(), calls=%async_computation.1 | async-start | bytes 1310720 | tf_op jit(solution)/shard_map/all_gather | solution.py:567
  7.9 29.1 %copy-start = (bf16[512,2048]{1,0:T(8,128)(2,1)S(1)}, bf16[512,2048]{1,0:T(8,128)(2,1)}, u32[]{:S(2)}) copy-start(bf16[512,2048]{1,0:T(8,128)(2,1)} %refs_6_.2) | copy-start | bytes 6291460
  8.0 29.1 %copy-start.5 = (bf16[1,256,512]{2,1,0:T(8,128)(2,1)S(1)}, bf16[1,256,512]{2,1,0:T(8,128)(2,1)}, u32[]{:S(2)}) copy-start(bf16[1,256,512]{2,1,0:T(8,128)(2,1)} %param.8) | copy-start | bytes 786436
  10.3 8.3 %collective-permute-start = (bf16[256,256]{1,0:T(8,128)(2,1)}, bf16[256,256]{1,0:T(8,128)(2,1)S(1)}, u32[]{:S(2)}, u32[]{:S(2)}) collective-permute-start(bf16[256,256]{1,0:T(8,128)(2,1)} %get-tuple-element.34), channel_id=1, source_target_pairs={{0,4},{4,0},{8,12},{12,8},{1,5},{5,1},{9,13},{13,9},{2,6},{6,2},{1... | collective-permute-start | bytes 393224 | tf_op jit(solution)/shard_map/ppermute | solution.py:496
  13.3 13.1 %collective-permute-start.1 = (bf16[256,256]{1,0:T(8,128)(2,1)}, bf16[256,256]{1,0:T(8,128)(2,1)S(1)}, u32[]{:S(2)}, u32[]{:S(2)}) collective-permute-start(bf16[256,256]{1,0:T(8,128)(2,1)} %get-tuple-element.35), channel_id=1, source_target_pairs={{0,8},{4,12},{8,0},{12,4},{1,9},{5,13},{9,1},{13,5},{2,10},{6,14},... | collective-permute-start | bytes 393224 | tf_op jit(solution)/shard_map/ppermute | solution.py:496
  15.9 10.6 %collective-permute-start.2 = (bf16[256,256]{1,0:T(8,128)(2,1)}, bf16[256,256]{1,0:T(8,128)(2,1)S(1)}, u32[]{:S(2)}, u32[]{:S(2)}) collective-permute-start(bf16[256,256]{1,0:T(8,128)(2,1)} %get-tuple-element.36), channel_id=1, source_target_pairs={{0,12},{4,8},{8,4},{12,0},{1,13},{5,9},{9,5},{13,1},{2,14},{6,10},... | collective-permute-start | bytes 393224 | tf_op jit(solution)/shard_map/ppermute | solution.py:496
  26.5 1.0 copy-start.10
  27.4 0.8 copy-start.12
  28.3 0.9 copy-start.16
  34.4 1.4 %copy-start.1 = (f32[9,256,256]{2,1,0:T(8,128)}, f32[9,256,256]{2,1,0:T(8,128)S(1)}, u32[]{:S(2)}) copy-start(f32[9,256,256]{2,1,0:T(8,128)S(1)} %get-tuple-element.51.refs_4_) | copy-start | bytes 7077892
  35.8 0.6 copy-start.14
  36.4 0.6 copy-start.17
  37.0 1.2 copy-start.4
  39.1 5.7 %collective-permute-start.6 = (bf16[256,256]{1,0:T(8,128)(2,1)S(1)}, bf16[256,256]{1,0:T(8,128)(2,1)S(1)}, u32[]{:S(2)}, u32[]{:S(2)}) collective-permute-start(bf16[256,256]{1,0:T(8,128)(2,1)S(1)} %get-tuple-element.42), channel_id=1, source_target_pairs={{0,4},{4,0},{8,12},{12,8},{1,5},{5,1},{9,13},{13,9},{2,6},{6,2},{1... | collective-permute-start | bytes 393224 | tf_op jit(solution)/shard_map/ppermute | solution.py:496
  41.2 9.0 %collective-permute-start.10 = (bf16[256,256]{1,0:T(8,128)(2,1)S(1)}, bf16[256,256]{1,0:T(8,128)(2,1)S(1)}, u32[]{:S(2)}, u32[]{:S(2)}) collective-permute-start(bf16[256,256]{1,0:T(8,128)(2,1)S(1)} %get-tuple-element.50), channel_id=1, source_target_pairs={{0,12},{4,8},{8,4},{12,0},{1,13},{5,9},{9,5},{13,1},{2,14},{6,10},... | collective-permute-start | bytes 393224 | tf_op jit(solution)/shard_map/ppermute | solution.py:496
  43.6 10.4 %collective-permute-start.9 = (bf16[256,256]{1,0:T(8,128)(2,1)S(1)}, bf16[256,256]{1,0:T(8,128)(2,1)S(1)}, u32[]{:S(2)}, u32[]{:S(2)}) collective-permute-start(bf16[256,256]{1,0:T(8,128)(2,1)S(1)} %get-tuple-element.49), channel_id=1, source_target_pairs={{0,8},{4,12},{8,0},{12,4},{1,9},{5,13},{9,1},{13,5},{2,10},{6,14},... | collective-permute-start | bytes 393224 | tf_op jit(solution)/shard_map/ppermute | solution.py:496
  54.8 0.7 copy-start.8
  55.5 24.1 %copy-start.2 = (f32[9,256,256]{2,1,0:T(8,128)S(1)}, f32[9,256,256]{2,1,0:T(8,128)}, u32[]{:S(2)}) copy-start(f32[9,256,256]{2,1,0:T(8,128)} %copy-done.1) | copy-start | bytes 7077892
  55.5 24.1 %copy-start.9 = (bf16[256,256]{1,0:T(8,128)(2,1)S(1)}, bf16[256,256]{1,0:T(8,128)(2,1)}, u32[]{:S(2)}) copy-start(bf16[256,256]{1,0:T(8,128)(2,1)} %copy-done.8) | copy-start | bytes 393220
  55.5 4.5 %collective-permute-start.3 = (bf16[256,128]{1,0:T(8,128)(2,1)S(1)}, bf16[256,128]{1,0:T(8,128)(2,1)S(1)}, u32[]{:S(2)}, u32[]{:S(2)}) collective-permute-start(bf16[256,128]{1,0:T(8,128)(2,1)S(1)} %get-tuple-element.38._), channel_id=1, source_target_pairs={{0,4},{4,0},{8,12},{12,8},{1,5},{5,1},{9,13},{13,9},{2,6},{6,2},{1... | collective-permute-start | bytes 196616 | tf_op jit(solution)/shard_map/ppermute | solution.py:496
  55.6 7.2 %collective-permute-start.4 = (bf16[256,128]{1,0:T(8,128)(2,1)}, bf16[256,128]{1,0:T(8,128)(2,1)S(1)}, u32[]{:S(2)}, u32[]{:S(2)}) collective-permute-start(bf16[256,128]{1,0:T(8,128)(2,1)} %copy-done.17), channel_id=1, source_target_pairs={{0,8},{4,12},{8,0},{12,4},{1,9},{5,13},{9,1},{13,5},{2,10},{6,14},... | collective-permute-start | bytes 196616 | tf_op jit(solution)/shard_map/ppermute | solution.py:496
  58.6 6.1 %collective-permute-start.5 = (bf16[256,128]{1,0:T(8,128)(2,1)S(1)}, bf16[256,128]{1,0:T(8,128)(2,1)S(1)}, u32[]{:S(2)}, u32[]{:S(2)}) collective-permute-start(bf16[256,128]{1,0:T(8,128)(2,1)S(1)} %get-tuple-element.40), channel_id=1, source_target_pairs={{0,12},{4,8},{8,4},{12,0},{1,13},{5,9},{9,5},{13,1},{2,14},{6,10},... | collective-permute-start | bytes 196616 | tf_op jit(solution)/shard_map/ppermute | solution.py:496
  64.7 0.8 copy-start.15
  66.4 39.8 %copy-start.6 = (bf16[1,256,512]{2,1,0:T(8,128)(2,1)S(1)}, bf16[1,256,512]{2,1,0:T(8,128)(2,1)}, u32[]{:S(2)}) copy-start(bf16[1,256,512]{2,1,0:T(8,128)(2,1)} %param.9) | copy-start | bytes 786436
  66.4 39.8 %copy-start.7 = (bf16[1,256,512]{2,1,0:T(8,128)(2,1)S(1)}, bf16[1,256,512]{2,1,0:T(8,128)(2,1)}, u32[]{:S(2)}) copy-start(bf16[1,256,512]{2,1,0:T(8,128)(2,1)} %param.10) | copy-start | bytes 786436
  66.4 40.7 %collective-permute-start.7 = (f32[2,256,512]{2,1,0:T(8,128)S(1)}, f32[2,256,512]{2,1,0:T(8,128)S(1)}, u32[]{:S(2)}, u32[]{:S(2)}) collective-permute-start(f32[2,256,512]{2,1,0:T(8,128)S(1)} %get-tuple-element.44), channel_id=1, source_target_pairs={{0,1},{1,0},{2,3},{3,2},{4,5},{5,4},{6,7},{7,6},{8,9},{9,8},{10,11... | collective-permute-start | bytes 3145736 | tf_op jit(solution)/shard_map/ppermute | solution.py:618
  66.4 7.8 %collective-permute-start.15 = (bf16[512,256]{1,0:T(8,128)(2,1)S(1)}, bf16[512,256]{1,0:T(8,128)(2,1)S(1)}, u32[]{:S(2)}, u32[]{:S(2)}) collective-permute-start(bf16[512,256]{1,0:T(8,128)(2,1)S(1)} %get-tuple-element.52.refs_7_.own_ref), channel_id=1, source_target_pairs={{0,4},{4,8},{8,12},{1,5},{5,9},{9,13},{2,6},{6,10},{10,14},{3,7},{... | collective-permute-start | bytes 786440 | tf_op jit(solution)/shard_map/ppermute | solution.py:584
  67.9 10.4 %collective-permute-start.16 = (bf16[512,256]{1,0:T(8,128)(2,1)S(1)}, bf16[512,256]{1,0:T(8,128)(2,1)S(1)}, u32[]{:S(2)}, u32[]{:S(2)}) collective-permute-start(bf16[512,256]{1,0:T(8,128)(2,1)S(1)} %get-tuple-element.52.refs_7_.own_ref), channel_id=1, source_target_pairs={{12,8},{8,4},{4,0},{13,9},{9,5},{5,1},{14,10},{10,6},{6,2},{15,11}... | collective-permute-start | bytes 786440 | tf_op jit(solution)/shard_map/ppermute | solution.py:585
  74.2 18.0 %collective-permute-start.17 = (bf16[512,256]{1,0:T(8,128)(2,1)S(1)}, bf16[512,256]{1,0:T(8,128)(2,1)S(1)}, u32[]{:S(2)}, u32[]{:S(2)}) collective-permute-start(bf16[512,256]{1,0:T(8,128)(2,1)S(1)} %collective-permute-done.15.up_ref), channel_id=1, source_target_pairs={{4,8},{8,12},{5,9},{9,13},{6,10},{10,14},{7,11},{11,15},{20,24},{2... | collective-permute-start | bytes 786440 | tf_op jit(solution)/shard_map/ppermute | solution.py:584
  78.3 13.8 %collective-permute-start.18 = (bf16[512,256]{1,0:T(8,128)(2,1)S(1)}, bf16[512,256]{1,0:T(8,128)(2,1)S(1)}, u32[]{:S(2)}, u32[]{:S(2)}) collective-permute-start(bf16[512,256]{1,0:T(8,128)(2,1)S(1)} %collective-permute-done.16.down_ref), channel_id=1, source_target_pairs={{8,4},{4,0},{9,5},{5,1},{10,6},{6,2},{11,7},{7,3},{24,20},{20,16},... | collective-permute-start | bytes 786440 | tf_op jit(solution)/shard_map/ppermute | solution.py:585
  79.7 1.0 copy-start.11
  80.6 0.8 copy-start.13
  86.5 5.7 %collective-permute-start.11 = (bf16[256,256]{1,0:T(8,128)(2,1)S(1)}, bf16[256,256]{1,0:T(8,128)(2,1)S(1)}, u32[]{:S(2)}, u32[]{:S(2)}) collective-permute-start(bf16[256,256]{1,0:T(8,128)(2,1)S(1)} %get-tuple-element.54), channel_id=1, source_target_pairs={{0,4},{4,0},{8,12},{12,8},{1,5},{5,1},{9,13},{13,9},{2,6},{6,2},{1... | collective-permute-start | bytes 393224 | tf_op jit(solution)/shard_map/ppermute | solution.py:496
  92.2 15.0 %collective-permute-start.19 = (bf16[512,256]{1,0:T(8,128)(2,1)S(1)}, bf16[512,256]{1,0:T(8,128)(2,1)S(1)}, u32[]{:S(2)}, u32[]{:S(2)}) collective-permute-start(bf16[512,256]{1,0:T(8,128)(2,1)S(1)} %shard_map.137.two_ref), channel_id=1, source_target_pairs={{4,0},{8,12},{5,1},{9,13},{6,2},{10,14},{7,3},{11,15},{20,16},{24,... | collective-permute-start | bytes 786440 | tf_op jit(solution)/shard_map/ppermute | solution.py:609
  93.5 12.7 %collective-permute-start.12 = (bf16[256,256]{1,0:T(8,128)(2,1)S(1)}, bf16[256,256]{1,0:T(8,128)(2,1)S(1)}, u32[]{:S(2)}, u32[]{:S(2)}) collective-permute-start(bf16[256,256]{1,0:T(8,128)(2,1)S(1)} %get-tuple-element.55), channel_id=1, source_target_pairs={{0,8},{4,12},{8,0},{12,4},{1,9},{5,13},{9,1},{13,5},{2,10},{6,14},... | collective-permute-start | bytes 393224 | tf_op jit(solution)/shard_map/ppermute | solution.py:496
  97.6 8.5 %collective-permute-start.13 = (bf16[256,256]{1,0:T(8,128)(2,1)S(1)}, bf16[256,256]{1,0:T(8,128)(2,1)S(1)}, u32[]{:S(2)}, u32[]{:S(2)}) collective-permute-start(bf16[256,256]{1,0:T(8,128)(2,1)S(1)} %get-tuple-element.56), channel_id=1, source_target_pairs={{0,12},{4,8},{8,4},{12,0},{1,13},{5,9},{9,5},{13,1},{2,14},{6,10},... | collective-permute-start | bytes 393224 | tf_op jit(solution)/shard_map/ppermute | solution.py:496
  107.3 1.2 copy-start.3
  109.6 16.9 %collective-permute-start.20 = (bf16[512,512]{1,0:T(8,128)(2,1)S(1)}, bf16[512,512]{1,0:T(8,128)(2,1)S(1)}, u32[]{:S(2)}, u32[]{:S(2)}) collective-permute-start(bf16[512,512]{1,0:T(8,128)(2,1)S(1)} %shard_map.138.one_ref), channel_id=1, source_target_pairs={{0,16},{16,0},{1,17},{17,1},{2,18},{18,2},{3,19},{19,3},{4,20},{20... | collective-permute-start | bytes 1572872 | tf_op jit(solution)/shard_map/ppermute | solution.py:649
  111.1 13.6 %collective-permute-start.14 = (bf16[256,512]{1,0:T(8,128)(2,1)S(1)}, bf16[256,512]{1,0:T(8,128)(2,1)S(1)}, u32[]{:S(2)}, u32[]{:S(2)}) collective-permute-start(bf16[256,512]{1,0:T(8,128)(2,1)S(1)} %get-tuple-element.59.one_ref.refs_0_), channel_id=1, source_target_pairs={{0,16},{16,0},{1,17},{17,1},{2,18},{18,2},{3,19},{19,3},{4,20},{20... | collective-permute-start | bytes 786440 | tf_op jit(solution)/shard_map/ppermute | solution.py:632
  111.7 14.1 %collective-permute-start.8 = (bf16[256,512]{1,0:T(8,128)(2,1)S(1)}, bf16[256,512]{1,0:T(8,128)(2,1)S(1)}, u32[]{:S(2)}, u32[]{:S(2)}) collective-permute-start(bf16[256,512]{1,0:T(8,128)(2,1)S(1)} %get-tuple-element.46), channel_id=1, source_target_pairs={{0,2},{1,3},{2,0},{3,1},{4,6},{5,7},{6,4},{7,5},{8,10},{9,11},{10,... | collective-permute-start | bytes 786440 | tf_op jit(solution)/shard_map/ppermute | solution.py:620
Sparse Core Ops, SparseCore 0:
  9.6 19.4 all-gather.3
  55.6 16.8 all-gather.5

commit v2 on v1

--- a/solution.py
+++ b/solution.py
@@ -323,7 +323,7 @@
 
 
 def forward_kernel(seqs, *refs):
-    held, (matrix, turn), refs = refs[:seqs], refs[seqs : seqs + 2], refs[seqs + 2 :]
+    held, (matrix, turn), refs = refs[:seqs], refs[seqs : seqs + 2], refs[seqs + 3 :]
     sent, (spec_ref, whole, zh, zl, turned, conv) = refs[:seqs], refs[seqs:]
     blocks = spec_ref.shape[0] - 1
     place_pieces(held, whole)
@@ -362,14 +362,17 @@
     take_pieces(back, sent)
 
 
-def gradient_kernel(cot_ref, w_ref, query_ref, _, gated_grad_ref, *pieces):
+def gradient_kernel(parts, *refs):
+    cots, (w_ref, query_ref), refs = refs[:parts], refs[parts : parts + 2], refs[parts + 5 :]
+    gated_grad_ref, *pieces, cot = refs
     me, part = lax.axis_index("ctx"), lax.axis_index("tp")
-    parts, positions, width = cot_ref.shape
+    positions, width = cots[0].shape
     quarter = positions // parts
     total = None
-    for j in range(parts):
+    for r, ref in enumerate(cots):
+        cot[part ^ r] = ref[...]
         term = lax.dot_general(
-            cot_ref[j], w_ref[:, j * width : (j + 1) * width], (((1,), (1,)), ((), ())), preferred_element_type=F32
+            ref[...], w_ref[:, at_block(part ^ r, width)], (((1,), (1,)), ((), ())), preferred_element_type=F32
         )
         total = term if total is None else total + term
     gated_grad_ref[...] = total
@@ -377,13 +380,13 @@
         cols = at_block(me ^ r)
         out_ref[:, pl.ds(0, LANES)] = (gated_grad_ref[:, cols] * query_ref[:, cols].astype(F32)).astype(BF16)
         for k in range(width // LANES):
-            out_ref[pl.ds(k * quarter, quarter), pl.ds(LANES, LANES)] = cot_ref[
+            out_ref[pl.ds(k * quarter, quarter), pl.ds(LANES, LANES)] = cot[
                 me ^ r, at_block(part, quarter), pl.ds(k * LANES, LANES)
             ]
 
 
 def quarter_kernel(seqs, *refs):
-    held, out_ref = refs[:seqs], refs[seqs]
+    held, out_ref = refs[:seqs], refs[-1]
     me = lax.axis_index("ctx")
     quarter = out_ref.shape[0] // seqs
     for r, ref in enumerate(held):
@@ -420,19 +423,13 @@
     out_ref[...] = (mine_ref[...] + other_ref[...].astype(F32)).astype(BF16)
 
 
-def pick_kernel(up_ref, down_ref, _, out_ref):
-    high = lax.axis_index("ctx") >= 2
-
-    @pl.when(high)
-    def _():
-        out_ref[...] = up_ref[...]
-
-    @pl.when(jnp.logical_not(high))
-    def _():
-        out_ref[...] = down_ref[...]
-
-
-def weight_kernel(own_ref, up_ref, down_ref, two_ref, end_ref, cot_ref, *refs):
+def pass_kernel(one_ref, two_ref, *refs):
+    one_out, two_out = refs[-2:]
+    one_out[...] = one_ref[...]
+    two_out[...] = two_ref[...]
+
+
+def weight_kernel(own_ref, up_ref, down_ref, up2_ref, down2_ref, end_ref, cot_ref, *refs):
     out_ref, total, cot = refs[-3:]
     me = lax.axis_index("ctx")
     parts = cot_ref.shape[0]
@@ -448,7 +445,8 @@
         total[...] += term(gated_ref, block)
 
     total[...] = term(own_ref, me)
-    add(two_ref, me ^ 2)
+    pl.when(me > 1)(lambda: add(up2_ref, me - 2))
+    pl.when(me < top - 1)(lambda: add(down2_ref, me + 2))
     pl.when(me > 0)(lambda: add(up_ref, me - 1))
     pl.when(me < top)(lambda: add(down_ref, me + 1))
     pl.when(jnp.logical_or(me == 0, me == top))(lambda: add(end_ref, top - me))
@@ -512,7 +510,8 @@
     rows = (positions, channels)
     line = seqs * positions
 
-    cot_rows = lax.all_gather(cot, "tp")
+    cot_rows = exchange([cot] * parts, "tp")
+
     sent = call(
         prepare_kernel,
         two,
@@ -532,6 +531,20 @@
     )
     held = exchange(sent, "ctx")
 
+    gated_grad, *conv_grad = call(
+        functools.partial(gradient_kernel, parts),
+        [shape_of(rows, F32)] + two,
+        2 * positions * channels * features,
+        5 * 10**6,
+        *cot_rows,
+        w_out,
+        query,
+        *held[1:],
+        scratch=[pltpu.VMEM((parts, positions, width), BF16)],
+        left=range(parts + 2, parts + 5),
+    )
+    grad_held = exchange(conv_grad, "ctx")
+
     *conv_sent, spec = call(
         functools.partial(forward_kernel, seqs),
         one + [shape_of(table + (2 * LANES,), F32)],
@@ -539,6 +552,7 @@
         9 * 10**6,
         *held,
         *tables,
+        conv_grad[1],
         scratch=[
             pltpu.VMEM((line, 2 * LANES), BF16),
             pltpu.VMEM(table + (2 * LANES,), BF16),
@@ -546,25 +560,41 @@
             pltpu.VMEM(table + (LANES,), F32),
             pltpu.VMEM((line, LANES), BF16),
         ],
+        left=(seqs + 2,),
     )
     conv = exchange(conv_sent, "ctx")
 
-    gated_grad, *conv_grad = call(
-        gradient_kernel,
-        [shape_of(rows, F32)] + two,
-        2 * positions * channels * features,
-        5 * 10**6,
-        cot_rows,
-        w_out,
-        query,
+
+    cot_quarters = call(
+        functools.partial(quarter_kernel, seqs),
+        shape_of((positions, width), BF16),
+        10**6,
+        10**6,
+        *grad_held,
         conv_sent[1],
-        left=(3,),
-    )
-    grad_held = exchange(conv_grad, "ctx")
-    cot_quarters = call(
-        functools.partial(quarter_kernel, seqs), shape_of((positions, width), BF16), 10**6, 10**6, *grad_held
+        left=(seqs,),
     )
     cot_cols = lax.all_gather(cot_quarters, "tp")
+    back_sent = call(
+        functools.partial(backward_kernel, seqs),
+        two,
+        10**9,
+        9 * 10**6,
+        *grad_held,
+        spec,
+        *tables,
+        conv_sent[1],
+        cot_quarters,
+        scratch=[
+            pltpu.VMEM((line, LANES), BF16),
+            pltpu.VMEM(table + (LANES,), BF16),
+            pltpu.VMEM(table + (LANES,), BF16),
+            pltpu.VMEM(table + (2 * LANES,), F32),
+            pltpu.VMEM((line, 2 * LANES), BF16),
+        ],
+        left=(seqs + 3, seqs + 4),
+    )
+    back = exchange(back_sent, "ctx")
 
     turned, grad_query, share_kept, share_sent = call(
         functools.partial(output_kernel, seqs),
@@ -575,38 +605,15 @@
         query,
         gated_grad,
         w_out,
-        grad_held[1],
+        back_sent[1],
         scratch=[pltpu.VMEM(rows, BF16)],
-        left=range(seqs + 3, seqs + 4),
-    )
-    ups, downs = [turned], [turned]
-    for r in (1, 2):
-        ups.append(lax.ppermute(ups[-1], "ctx", [(d, d + 1) for d in range(r - 1, seqs - 1)]))
-        downs.append(lax.ppermute(downs[-1], "ctx", [(d, d - 1) for d in range(seqs - r, 0, -1)]))
-
-    back_sent = call(
-        functools.partial(backward_kernel, seqs),
-        two,
-        10**9,
-        9 * 10**6,
-        *grad_held,
-        spec,
-        *tables,
-        turned,
-        cot_quarters,
-        scratch=[
-            pltpu.VMEM((line, LANES), BF16),
-            pltpu.VMEM(table + (LANES,), BF16),
-            pltpu.VMEM(table + (LANES,), BF16),
-            pltpu.VMEM(table + (2 * LANES,), F32),
-            pltpu.VMEM((line, 2 * LANES), BF16),
-        ],
-        left=(seqs + 3, seqs + 4),
-    )
-    back = exchange(back_sent, "ctx")
-
-    two_away = call(pick_kernel, shape_of((channels, positions), BF16), 10**6, 10**6, ups[2], downs[2], back[1], left=(2,))
-    end_away = lax.ppermute(two_away, "ctx", [(1, 0), (2, 3)])
+        left=(seqs + 3,),
+    )
+    up, down = [[(d, d + o) for d in range(seqs) if 0 <= d + o < seqs] for o in (1, -1)]
+    above, below = lax.ppermute(turned, "ctx", up), lax.ppermute(turned, "ctx", down)
+    across = lax.ppermute(turned, "ctx", [(0, seqs - 1), (seqs - 1, 0)])
+    passed = call(pass_kernel, [shape_of((channels, positions), BF16)] * 2, 10**6, 10**6, above, below, back[1], left=(2,))
+    above2, below2 = lax.ppermute(passed[0], "ctx", up[1:]), lax.ppermute(passed[1], "ctx", down[:-1])
 
 
     mine, far = call(
@@ -636,15 +643,16 @@
         2 * line * channels * width,
         3 * 10**6,
         turned,
-        ups[1],
-        downs[1],
-        two_away,
-        end_away,
+        above,
+        below,
+        above2,
+        below2,
+        across,
         cot_cols,
-        taps,
-        mine,
+        taps_other,
+        left=(7,),
+        room=60,
         scratch=[pltpu.VMEM((channels, width), F32), pltpu.VMEM((positions, width), BF16)],
-        left=range(6, 8),
     )
     weight_other = lax.ppermute(weight_grad, "dp", ring)
     grad_wout = call(

time: 137 us -> 129 us (0.942); the launches traced: 134 us -> 128 us
  waiting for transfers between devices: 57 us -> 40.7 us
  starting transfers between devices: 32.1 us -> 39.8 us
  Pallas kernels: 20 us -> 23.5 us
    ppermute x12 -> x15, waiting for transfers between devices: 36.2 us -> 24.2 us  [exchange(): lax.ppermute(pieces[r], axis, [(d, d ^ r) for d in range(size)])]
    ppermute x1, waiting for transfers between devices: 11.6 us -> 0.01 us  [local_short(): taps_other = lax.ppermute(taps, 'dp', ring)]
    ppermute x12 -> x15, starting transfers between devices: 22.4 us -> 27.2 us  [exchange(): lax.ppermute(pieces[r], axis, [(d, d ^ r) for d in range(size)])]
    ppermute x1, waiting for transfers between devices: 0.01 us -> 4.38 us  [local_short(): far = lax.ppermute(far, 'tp', [(j, j ^ 2) for j in range(parts)])]
    ppermute x1, waiting for transfers between devices: 0.01 us -> 3.51 us  [local_short(): weight_other = lax.ppermute(weight_grad, 'dp', ring)]
    pallas_call x13, Pallas kernels: 20 us -> 23.5 us  [call(): pl.pallas_call(kernel, out_shape=outs, in_specs=[anywhere if n in left el...]
    ppermute x5, starting transfers between devices: 6.02 us -> 8.07 us  [the longest x1 2.9 us: local_short(): lax.ppermute(turned, 'ctx', up)]
    unnamed x36 -> x44, local copies, waits for them, and re-layouts: 11.1 us -> 10.1 us
  transfers between devices with their start and end apart: 23 -> 25, of which waited for: 12 -> 7; matrix products, arithmetic and copies ran while one was open for 0% -> 0% of each run, Pallas kernels for 12% -> 14%
where the time goes in v2:
time: 129 us; the launch traced here: 128 us
  waiting for transfers between devices  40.7 us (32%)
  starting transfers between devices  39.8 us (31%)
  Pallas kernels  23.5 us (18%)
  between operations  14.3 us (11%)
  local copies, waits for them, and re-layouts  10.1 us (8%)
    ppermute x15, starting transfers between devices, exchange(): lax.ppermute(pieces[r], axis, [(d, d ^ r) for d in range(size)])  27.2 us
    ppermute x15, waiting for transfers between devices, exchange(): lax.ppermute(pieces[r], axis, [(d, d ^ r) for d in range(size)])  24.2 us
    pallas_call x13, Pallas kernels, call(): pl.pallas_call(kernel, out_shape=outs, in_specs=[anywhere if n in left el...  23.5 us
    unnamed x44, local copies, waits for them, and re-layouts  10.1 us
    ppermute x1, waiting for transfers between devices, local_short(): lax.ppermute(passed[1], 'ctx', down[:-1])  4.91 us
    ppermute x1, waiting for transfers between devices, local_short(): far = lax.ppermute(far, 'tp', [(j, j ^ 2) for j in range(parts)])  4.38 us
    ppermute x1, waiting for transfers between devices, local_short(): across = lax.ppermute(turned, 'ctx', [(0, seqs - 1), (seqs - 1, 0)])  3.72 us
    ppermute x1, waiting for transfers between devices, local_short(): weight_other = lax.ppermute(weight_grad, 'dp', ring)  3.51 us
  transfers between devices with their start and end apart: 25, of which 7 were waited for; matrix products, arithmetic and copies ran while one was open for 0% of the time, Pallas kernels for 14%

profile of v2, /device:TPU:0, one launch (start us, length us, event | category | flops | bytes accessed | tf_op | source)
XLA Modules:
  0.0 128.4 jit_solution(6952189790713168645)
XLA Ops:
  7.2 0.0 all-gather.3.cloned.1.call-start
  7.2 0.0 copy-start.16
  7.2 0.0 copy-start.17
  7.2 2.2 %shard_map.127 = (bf16[256,256]{1,0:T(8,128)(2,1)}, bf16[256,256]{1,0:T(8,128)(2,1)}, bf16[256,256]{1,0:T(8,128)(2,1)}, bf16[256,256]{1,0:T(8,128)(2,1)}) custom-call(bf16[256,512]{1,0:T(8,128)(2,1)} %bitcast.9, bf16[256,512]{1,0:T(8,128)(2,1)} %bitcast.11, f32[512,256]{1,0:T(8,128)} %refs_2_.1), custom_call_target="tpu_custom_call" | custom-call | flops 1000000 | bytes 2000000 | tf_op jit(solution)/shard_map/pallas_call | solution.py:481
  9.4 3.1 %collective-permute-start = (bf16[256,256]{1,0:T(8,128)(2,1)}, bf16[256,256]{1,0:T(8,128)(2,1)S(1)}, u32[]{:S(2)}, u32[]{:S(2)}) collective-permute-start(bf16[256,256]{1,0:T(8,128)(2,1)} %get-tuple-element.36), channel_id=1, source_target_pairs={{0,4},{4,0},{8,12},{12,8},{1,5},{5,1},{9,13},{13,9},{2,6},{6,2},{1... | collective-permute-start | bytes 393224 | tf_op jit(solution)/shard_map/ppermute | solution.py:494
  12.5 0.0 collective-permute-start.3
  12.5 1.5 %collective-permute-start.4 = (bf16[256,512]{1,0:T(8,128)(2,1)}, bf16[256,512]{1,0:T(8,128)(2,1)S(1)}, u32[]{:S(2)}, u32[]{:S(2)}) collective-permute-start(bf16[256,512]{1,0:T(8,128)(2,1)} %bitcast.16), channel_id=1, source_target_pairs={{0,2},{1,3},{2,0},{3,1},{4,6},{5,7},{6,4},{7,5},{8,10},{9,11},{10,... | collective-permute-start | bytes 786440 | tf_op jit(solution)/shard_map/ppermute | solution.py:494
  14.0 0.3 collective-permute-start.5
  14.4 2.6 %collective-permute-start.1 = (bf16[256,256]{1,0:T(8,128)(2,1)}, bf16[256,256]{1,0:T(8,128)(2,1)S(1)}, u32[]{:S(2)}, u32[]{:S(2)}) collective-permute-start(bf16[256,256]{1,0:T(8,128)(2,1)} %get-tuple-element.37), channel_id=1, source_target_pairs={{0,8},{4,12},{8,0},{12,4},{1,9},{5,13},{9,1},{13,5},{2,10},{6,14},... | collective-permute-start | bytes 393224 | tf_op jit(solution)/shard_map/ppermute | solution.py:494
  17.0 0.0 collective-permute-done.refs_6_.refs_1_
  17.0 3.0 %collective-permute-start.2 = (bf16[256,256]{1,0:T(8,128)(2,1)}, bf16[256,256]{1,0:T(8,128)(2,1)S(1)}, u32[]{:S(2)}, u32[]{:S(2)}) collective-permute-start(bf16[256,256]{1,0:T(8,128)(2,1)} %get-tuple-element.38), channel_id=1, source_target_pairs={{0,12},{4,8},{8,4},{12,0},{1,13},{5,9},{9,5},{13,1},{2,14},{6,10},... | collective-permute-start | bytes 393224 | tf_op jit(solution)/shard_map/ppermute | solution.py:494
  20.0 6.9 %collective-permute-done.1.refs_7_.refs_2_ = bf16[256,256]{1,0:T(8,128)(2,1)S(1)} collective-permute-done((bf16[256,256]{1,0:T(8,128)(2,1)}, bf16[256,256]{1,0:T(8,128)(2,1)S(1)}, u32[]{:S(2)}, u32[]{:S(2)}) %collective-permute-start.1) | collective-permute-done | bytes 131104 | tf_op jit(solution)/shard_map/ppermute | solution.py:494
  26.9 0.0 collective-permute-done.5.refs_3_
  27.0 0.0 copy-start
  27.0 1.6 %copy-done = bf16[512,2048]{1,0:T(8,128)(2,1)S(1)} copy-done((bf16[512,2048]{1,0:T(8,128)(2,1)S(1)}, bf16[512,2048]{1,0:T(8,128)(2,1)}, u32[]{:S(2)}) %copy-start) | copy-done | bytes 2097176
  28.5 0.9 copy-done.9
  29.5 0.9 copy-done.14
  30.4 0.9 shard_map.128
  31.3 0.0 copy-start.11
  31.3 0.8 copy-done.11
  32.1 3.2 %collective-permute-start.9 = (bf16[256,256]{1,0:T(8,128)(2,1)S(1)}, bf16[256,256]{1,0:T(8,128)(2,1)S(1)}, u32[]{:S(2)}, u32[]{:S(2)}) collective-permute-start(bf16[256,256]{1,0:T(8,128)(2,1)S(1)} %get-tuple-element.39.refs_6_), channel_id=1, source_target_pairs={{0,4},{4,0},{8,12},{12,8},{1,5},{5,1},{9,13},{13,9},{2,6},{6,2},{1... | collective-permute-start | bytes 393224 | tf_op jit(solution)/shard_map/ppermute | solution.py:494
  35.3 1.1 collective-permute-start.10
  36.4 1.5 %collective-permute-start.11 = (bf16[256,256]{1,0:T(8,128)(2,1)S(1)}, bf16[256,256]{1,0:T(8,128)(2,1)S(1)}, u32[]{:S(2)}, u32[]{:S(2)}) collective-permute-start(bf16[256,256]{1,0:T(8,128)(2,1)S(1)} %get-tuple-element.47), channel_id=1, source_target_pairs={{0,12},{4,8},{8,4},{12,0},{1,13},{5,9},{9,5},{13,1},{2,14},{6,10},... | collective-permute-start | bytes 393224 | tf_op jit(solution)/shard_map/ppermute | solution.py:494
  37.8 5.2 %shard_map.129 = (bf16[256,128]{1,0:T(8,128)(2,1)S(1)}, bf16[256,128]{1,0:T(8,128)(2,1)S(1)}, bf16[256,128]{1,0:T(8,128)(2,1)S(1)}, bf16[256,128]{1,0:T(8,128)(2,1)S(1)}, f32[9,256,256]{2,1,0:T(8,128)S(1)}) custom-call(bf16[256,256]{1,0:T(8,128)(2,1)S(1)} %copy-done.15, bf16[256,256]{1,0:T(8,128)(2,1)S(1)} %collective-permute-done.refs_6_.refs_1_, ...), custom_call_target="tpu_custom_call" | custom-call | flops 1000000000 | bytes 9000000 | tf_op jit(solution)/shard_map/pallas_call | solution.py:481
  43.0 1.4 %copy-done.18 = f32[9,256,256]{2,1,0:T(8,128)} copy-done((f32[9,256,256]{2,1,0:T(8,128)}, f32[9,256,256]{2,1,0:T(8,128)S(1)}, u32[]{:S(2)}) %copy-start.18) | copy-done | bytes 2359320
  44.4 0.0 collective-permute-done.9.refs_1_
  44.4 3.5 %collective-permute-done.10.refs_2_ = bf16[256,256]{1,0:T(8,128)(2,1)S(1)} collective-permute-done((bf16[256,256]{1,0:T(8,128)(2,1)S(1)}, bf16[256,256]{1,0:T(8,128)(2,1)S(1)}, u32[]{:S(2)}, u32[]{:S(2)}) %collective-permute-start.10) | collective-permute-done | bytes 131104 | tf_op jit(solution)/shard_map/ppermute | solution.py:494
  47.9 0.8 shard_map.130.refs_8_
  48.7 0.0 all-gather.3.cloned.1.call-update
  48.7 2.4 %collective-permute-start.6 = (bf16[256,128]{1,0:T(8,128)(2,1)S(1)}, bf16[256,128]{1,0:T(8,128)(2,1)S(1)}, u32[]{:S(2)}, u32[]{:S(2)}) collective-permute-start(bf16[256,128]{1,0:T(8,128)(2,1)S(1)} %get-tuple-element.41.refs_4_.refs_7_), channel_id=1, source_target_pairs={{0,4},{4,0},{8,12},{12,8},{1,5},{5,1},{9,13},{13,9},{2,6},{6,2},{1... | collective-permute-start | bytes 196616 | tf_op jit(solution)/shard_map/ppermute | solution.py:494
  51.1 0.7 collective-permute-start.7
  51.8 1.7 %collective-permute-start.8 = (bf16[256,128]{1,0:T(8,128)(2,1)S(1)}, bf16[256,128]{1,0:T(8,128)(2,1)S(1)}, u32[]{:S(2)}, u32[]{:S(2)}) collective-permute-start(bf16[256,128]{1,0:T(8,128)(2,1)S(1)} %get-tuple-element.43), channel_id=1, source_target_pairs={{0,12},{4,8},{8,4},{12,0},{1,13},{5,9},{9,5},{13,1},{2,14},{6,10},... | collective-permute-start | bytes 196616 | tf_op jit(solution)/shard_map/ppermute | solution.py:494
  53.5 1.7 %copy-done.19 = f32[9,256,256]{2,1,0:T(8,128)S(1)} copy-done((f32[9,256,256]{2,1,0:T(8,128)S(1)}, f32[9,256,256]{2,1,0:T(8,128)}, u32[]{:S(2)}) %copy-start.19) | copy-done | bytes 2359320
  55.2 5.1 %shard_map.131 = (bf16[256,256]{1,0:T(8,128)(2,1)S(1)}, bf16[256,256]{1,0:T(8,128)(2,1)S(1)}, bf16[256,256]{1,0:T(8,128)(2,1)S(1)}, bf16[256,256]{1,0:T(8,128)(2,1)S(1)}) custom-call(bf16[256,256]{1,0:T(8,128)(2,1)S(1)} %get-tuple-element.45.refs_0_, bf16[256,256]{1,0:T(8,128)(2,1)S(1)} %collective-permute-done.9.refs_1_, ...), custom_call_target="tpu_custom_call" | custom-call | flops 1000000000 | bytes 9000000 | tf_op jit(solution)/shard_map/pallas_call | solution.py:481
  60.3 0.0 copy-start.3
  60.3 0.0 copy-start.4
  60.3 0.0 copy-start.12
  60.3 1.1 copy-done.12
  61.4 1.7 %shard_map.132 = (bf16[512,256]{1,0:T(8,128)(2,1)S(1)}, bf16[256,512]{1,0:T(8,128)(2,1)}, f32[2,256,512]{2,1,0:T(8,128)S(1)}, f32[2,256,512]{2,1,0:T(8,128)}) custom-call(bf16[256,128]{1,0:T(8,128)(2,1)S(1)} %get-tuple-element.40.refs_0_, bf16[256,128]{1,0:T(8,128)(2,1)S(1)} %collective-permute-done.6.refs_1_, ...), custom_call_target="tpu_custom_call" | custom-call | flops 536870912 | bytes 5000000 | tf_op jit(solution)/shard_map/pallas_call | solution.py:481
  63.2 1.0 collective-permute-start.14
  64.2 2.9 %collective-permute-start.18 = (bf16[512,256]{1,0:T(8,128)(2,1)S(1)}, bf16[512,256]{1,0:T(8,128)(2,1)S(1)}, u32[]{:S(2)}, u32[]{:S(2)}) collective-permute-start(bf16[512,256]{1,0:T(8,128)(2,1)S(1)} %get-tuple-element.61.own_ref), channel_id=1, source_target_pairs={{0,4},{4,8},{8,12},{1,5},{5,9},{9,13},{2,6},{6,10},{10,14},{3,7},{... | collective-permute-start | bytes 786440 | tf_op jit(solution)/shard_map/ppermute | solution.py:613
  67.1 1.3 %collective-permute-start.19 = (bf16[512,256]{1,0:T(8,128)(2,1)S(1)}, bf16[512,256]{1,0:T(8,128)(2,1)S(1)}, u32[]{:S(2)}, u32[]{:S(2)}) collective-permute-start(bf16[512,256]{1,0:T(8,128)(2,1)S(1)} %get-tuple-element.61.own_ref), channel_id=1, source_target_pairs={{4,0},{8,4},{12,8},{5,1},{9,5},{13,9},{6,2},{10,6},{14,10},{7,3},{... | collective-permute-start | bytes 786440 | tf_op jit(solution)/shard_map/ppermute | solution.py:613
  68.4 3.3 %collective-permute-start.15 = (bf16[256,256]{1,0:T(8,128)(2,1)S(1)}, bf16[256,256]{1,0:T(8,128)(2,1)S(1)}, u32[]{:S(2)}, u32[]{:S(2)}) collective-permute-start(bf16[256,256]{1,0:T(8,128)(2,1)S(1)} %get-tuple-element.56), channel_id=1, source_target_pairs={{0,8},{4,12},{8,0},{12,4},{1,9},{5,13},{9,1},{13,5},{2,10},{6,14},... | collective-permute-start | bytes 393224 | tf_op jit(solution)/shard_map/ppermute | solution.py:494
  71.7 1.8 %collective-permute-start.16 = (bf16[256,256]{1,0:T(8,128)(2,1)S(1)}, bf16[256,256]{1,0:T(8,128)(2,1)S(1)}, u32[]{:S(2)}, u32[]{:S(2)}) collective-permute-start(bf16[256,256]{1,0:T(8,128)(2,1)S(1)} %get-tuple-element.57), channel_id=1, source_target_pairs={{0,12},{4,8},{8,4},{12,0},{1,13},{5,9},{9,5},{13,1},{2,14},{6,10},... | collective-permute-start | bytes 393224 | tf_op jit(solution)/shard_map/ppermute | solution.py:494
  73.5 13.7 %collective-permute-done.15.refs_2_ = bf16[256,256]{1,0:T(8,128)(2,1)S(1)} collective-permute-done((bf16[256,256]{1,0:T(8,128)(2,1)S(1)}, bf16[256,256]{1,0:T(8,128)(2,1)S(1)}, u32[]{:S(2)}, u32[]{:S(2)}) %collective-permute-start.15) | collective-permute-done | bytes 131104 | tf_op jit(solution)/shard_map/ppermute | solution.py:494
  87.2 1.9 %collective-permute-start.22 = (bf16[512,256]{1,0:T(8,128)(2,1)S(1)}, bf16[512,256]{1,0:T(8,128)(2,1)S(1)}, u32[]{:S(2)}, u32[]{:S(2)}) collective-permute-start(bf16[512,256]{1,0:T(8,128)(2,1)S(1)} %get-tuple-element.61.own_ref), channel_id=1, source_target_pairs={{0,12},{12,0},{1,13},{13,1},{2,14},{14,2},{3,15},{15,3},{16,28},{2... | collective-permute-start | bytes 786440 | tf_op jit(solution)/shard_map/ppermute | solution.py:614
  89.2 0.9 shard_map.135
  90.1 1.5 %collective-permute-start.17 = (bf16[256,512]{1,0:T(8,128)(2,1)S(1)}, bf16[256,512]{1,0:T(8,128)(2,1)S(1)}, u32[]{:S(2)}, u32[]{:S(2)}) collective-permute-start(bf16[256,512]{1,0:T(8,128)(2,1)S(1)} %get-tuple-element.60.one_ref), channel_id=1, source_target_pairs={{0,16},{16,0},{1,17},{17,1},{2,18},{18,2},{3,19},{19,3},{4,20},{20... | collective-permute-start | bytes 786440 | tf_op jit(solution)/shard_map/ppermute | solution.py:639
  91.7 0.7 collective-permute-start.20
  92.4 1.3 %collective-permute-start.21 = (bf16[512,256]{1,0:T(8,128)(2,1)S(1)}, bf16[512,256]{1,0:T(8,128)(2,1)}, u32[]{:S(2)}, u32[]{:S(2)}) collective-permute-start(bf16[512,256]{1,0:T(8,128)(2,1)S(1)} %get-tuple-element.63), channel_id=1, source_target_pairs={{4,0},{8,4},{5,1},{9,5},{6,2},{10,6},{7,3},{11,7},{20,16},{24,20},... | collective-permute-start | bytes 786440 | tf_op jit(solution)/shard_map/ppermute | solution.py:616
  93.7 3.7 %collective-permute-done.22.end_ref = bf16[512,256]{1,0:T(8,128)(2,1)S(1)} collective-permute-done((bf16[512,256]{1,0:T(8,128)(2,1)S(1)}, bf16[512,256]{1,0:T(8,128)(2,1)S(1)}, u32[]{:S(2)}, u32[]{:S(2)}) %collective-permute-start.22) | collective-permute-done | bytes 262176 | tf_op jit(solution)/shard_map/ppermute | solution.py:614
  97.4 0.0 copy-start.7
  97.4 0.7 copy-done.20
  98.1 4.9 %collective-permute-done.21.down2_ref = bf16[512,256]{1,0:T(8,128)(2,1)} collective-permute-done((bf16[512,256]{1,0:T(8,128)(2,1)S(1)}, bf16[512,256]{1,0:T(8,128)(2,1)}, u32[]{:S(2)}, u32[]{:S(2)}) %collective-permute-start.21) | collective-permute-done | bytes 262176 | tf_op jit(solution)/shard_map/ppermute | solution.py:616
  103.0 3.8 %shard_map.138.one_ref = bf16[512,512]{1,0:T(8,128)(2,1)} custom-call(bf16[512,256]{1,0:T(8,128)(2,1)} %copy-done.13, bf16[512,256]{1,0:T(8,128)(2,1)} %copy-done.5, bf16[512,256]{1,0:T(8,128)(2,1)} %copy-done.6, bf16[512,256]{1,0:T(8,128)(2,1)} %copy-done.21, bf16[512,256]{1,0:T(8,128)(2,1)} %collective-permute-done.21.down2_ref, ...), custom_call_target="tpu_custom_call" | custom-call | flops 536870912 | bytes 3000000 | tf_op jit(solution)/shard_map/pallas_call | solution.py:481
  106.8 1.4 %collective-permute-start.23 = (bf16[512,512]{1,0:T(8,128)(2,1)}, bf16[512,512]{1,0:T(8,128)(2,1)S(1)}, u32[]{:S(2)}, u32[]{:S(2)}) collective-permute-start(bf16[512,512]{1,0:T(8,128)(2,1)} %shard_map.138.one_ref), channel_id=1, source_target_pairs={{0,16},{16,0},{1,17},{17,1},{2,18},{18,2},{3,19},{19,3},{4,20},{20... | collective-permute-start | bytes 1572872 | tf_op jit(solution)/shard_map/ppermute | solution.py:657
  108.2 0.1 shard_map.133
  108.3 1.6 %collective-permute-start.13 = (bf16[256,512]{1,0:T(8,128)(2,1)S(1)}, bf16[256,512]{1,0:T(8,128)(2,1)S(1)}, u32[]{:S(2)}, u32[]{:S(2)}) collective-permute-start(bf16[256,512]{1,0:T(8,128)(2,1)S(1)} %get-tuple-element.53), channel_id=1, source_target_pairs={{0,2},{1,3},{2,0},{3,1},{4,6},{5,7},{6,4},{7,5},{8,10},{9,11},{10,... | collective-permute-start | bytes 786440 | tf_op jit(solution)/shard_map/ppermute | solution.py:627
  109.9 0.9 copy-done.8
  110.9 1.0 shard_map.136
  111.8 4.4 %collective-permute-done.13.other_ref = bf16[256,512]{1,0:T(8,128)(2,1)S(1)} collective-permute-done((bf16[256,512]{1,0:T(8,128)(2,1)S(1)}, bf16[256,512]{1,0:T(8,128)(2,1)S(1)}, u32[]{:S(2)}, u32[]{:S(2)}) %collective-permute-start.13) | collective-permute-done | bytes 262176 | tf_op jit(solution)/shard_map/ppermute | solution.py:627
  116.2 0.7 shard_map.134
  117.0 3.5 %collective-permute-done.23.other_ref = bf16[512,512]{1,0:T(8,128)(2,1)S(1)} collective-permute-done((bf16[512,512]{1,0:T(8,128)(2,1)}, bf16[512,512]{1,0:T(8,128)(2,1)S(1)}, u32[]{:S(2)}, u32[]{:S(2)}) %collective-permute-start.23) | collective-permute-done | bytes 524320 | tf_op jit(solution)/shard_map/ppermute | solution.py:657
  120.5 1.1 shard_map.139
  (44 shorter events, 0.1 us)
Async XLA Ops:
  7.2 95.8 %all-gather.3.cloned.1.call-start = ((), (), s32[]{:S(2)}) async-start(), calls=%async_computation | async-start | bytes 1310720 | tf_op jit(solution)/shard_map/all_gather | solution.py:577
  7.2 30.6 %copy-start.16 = (bf16[2,256,256]{2,1,0:T(8,128)(2,1)S(1)}, bf16[2,256,256]{2,1,0:T(8,128)(2,1)}, u32[]{:S(2)}) copy-start(bf16[2,256,256]{2,1,0:T(8,128)(2,1)} %constant.4.clone.refs_4_.refs_5_) | copy-start | bytes 786436
  7.2 30.6 %copy-start.17 = (f32[128,128]{1,0:T(8,128)S(1)}, f32[128,128]{1,0:T(8,128)}, u32[]{:S(2)}) copy-start(f32[128,128]{1,0:T(8,128)} %constant.5.clone.refs_5_.refs_6_) | copy-start | bytes 196612
  9.4 7.5 %collective-permute-start = (bf16[256,256]{1,0:T(8,128)(2,1)}, bf16[256,256]{1,0:T(8,128)(2,1)S(1)}, u32[]{:S(2)}, u32[]{:S(2)}) collective-permute-start(bf16[256,256]{1,0:T(8,128)(2,1)} %get-tuple-element.36), channel_id=1, source_target_pairs={{0,4},{4,0},{8,12},{12,8},{1,5},{5,1},{9,13},{13,9},{2,6},{6,2},{1... | collective-permute-start | bytes 393224 | tf_op jit(solution)/shard_map/ppermute | solution.py:494
  12.5 14.4 %collective-permute-start.3 = (bf16[256,512]{1,0:T(8,128)(2,1)}, bf16[256,512]{1,0:T(8,128)(2,1)S(1)}, u32[]{:S(2)}, u32[]{:S(2)}) collective-permute-start(bf16[256,512]{1,0:T(8,128)(2,1)} %bitcast.15), channel_id=1, source_target_pairs={{0,1},{1,0},{2,3},{3,2},{4,5},{5,4},{6,7},{7,6},{8,9},{9,8},{10,11... | collective-permute-start | bytes 786440 | tf_op jit(solution)/shard_map/ppermute | solution.py:494
  12.5 14.4 %collective-permute-start.4 = (bf16[256,512]{1,0:T(8,128)(2,1)}, bf16[256,512]{1,0:T(8,128)(2,1)S(1)}, u32[]{:S(2)}, u32[]{:S(2)}) collective-permute-start(bf16[256,512]{1,0:T(8,128)(2,1)} %bitcast.16), channel_id=1, source_target_pairs={{0,2},{1,3},{2,0},{3,1},{4,6},{5,7},{6,4},{7,5},{8,10},{9,11},{10,... | collective-permute-start | bytes 786440 | tf_op jit(solution)/shard_map/ppermute | solution.py:494
  14.0 12.9 %collective-permute-start.5 = (bf16[256,512]{1,0:T(8,128)(2,1)}, bf16[256,512]{1,0:T(8,128)(2,1)S(1)}, u32[]{:S(2)}, u32[]{:S(2)}) collective-permute-start(bf16[256,512]{1,0:T(8,128)(2,1)} %bitcast.17), channel_id=1, source_target_pairs={{0,3},{1,2},{2,1},{3,0},{4,7},{5,6},{6,5},{7,4},{8,11},{9,10},{10,... | collective-permute-start | bytes 786440 | tf_op jit(solution)/shard_map/ppermute | solution.py:494
  14.4 12.6 %collective-permute-start.1 = (bf16[256,256]{1,0:T(8,128)(2,1)}, bf16[256,256]{1,0:T(8,128)(2,1)S(1)}, u32[]{:S(2)}, u32[]{:S(2)}) collective-permute-start(bf16[256,256]{1,0:T(8,128)(2,1)} %get-tuple-element.37), channel_id=1, source_target_pairs={{0,8},{4,12},{8,0},{12,4},{1,9},{5,13},{9,1},{13,5},{2,10},{6,14},... | collective-permute-start | bytes 393224 | tf_op jit(solution)/shard_map/ppermute | solution.py:494
  17.0 10.0 %collective-permute-start.2 = (bf16[256,256]{1,0:T(8,128)(2,1)}, bf16[256,256]{1,0:T(8,128)(2,1)S(1)}, u32[]{:S(2)}, u32[]{:S(2)}) collective-permute-start(bf16[256,256]{1,0:T(8,128)(2,1)} %get-tuple-element.38), channel_id=1, source_target_pairs={{0,12},{4,8},{8,4},{12,0},{1,13},{5,9},{9,5},{13,1},{2,14},{6,10},... | collective-permute-start | bytes 393224 | tf_op jit(solution)/shard_map/ppermute | solution.py:494
  27.0 1.6 %copy-start = (bf16[512,2048]{1,0:T(8,128)(2,1)S(1)}, bf16[512,2048]{1,0:T(8,128)(2,1)}, u32[]{:S(2)}) copy-start(bf16[512,2048]{1,0:T(8,128)(2,1)} %refs_6_.2) | copy-start | bytes 6291460
  28.5 0.9 copy-start.9
  29.5 0.9 copy-start.14
  30.4 7.4 %copy-start.15 = (bf16[256,256]{1,0:T(8,128)(2,1)S(1)}, bf16[256,256]{1,0:T(8,128)(2,1)}, u32[]{:S(2)}) copy-start(bf16[256,256]{1,0:T(8,128)(2,1)} %get-tuple-element.35.refs_0_) | copy-start | bytes 393220
  31.3 0.8 copy-start.11
  32.1 12.3 %collective-permute-start.9 = (bf16[256,256]{1,0:T(8,128)(2,1)S(1)}, bf16[256,256]{1,0:T(8,128)(2,1)S(1)}, u32[]{:S(2)}, u32[]{:S(2)}) collective-permute-start(bf16[256,256]{1,0:T(8,128)(2,1)S(1)} %get-tuple-element.39.refs_6_), channel_id=1, source_target_pairs={{0,4},{4,0},{8,12},{12,8},{1,5},{5,1},{9,13},{13,9},{2,6},{6,2},{1... | collective-permute-start | bytes 393224 | tf_op jit(solution)/shard_map/ppermute | solution.py:494
  35.3 12.6 %collective-permute-start.10 = (bf16[256,256]{1,0:T(8,128)(2,1)S(1)}, bf16[256,256]{1,0:T(8,128)(2,1)S(1)}, u32[]{:S(2)}, u32[]{:S(2)}) collective-permute-start(bf16[256,256]{1,0:T(8,128)(2,1)S(1)} %get-tuple-element.46), channel_id=1, source_target_pairs={{0,8},{4,12},{8,0},{12,4},{1,9},{5,13},{9,1},{13,5},{2,10},{6,14},... | collective-permute-start | bytes 393224 | tf_op jit(solution)/shard_map/ppermute | solution.py:494
  36.4 11.5 %collective-permute-start.11 = (bf16[256,256]{1,0:T(8,128)(2,1)S(1)}, bf16[256,256]{1,0:T(8,128)(2,1)S(1)}, u32[]{:S(2)}, u32[]{:S(2)}) collective-permute-start(bf16[256,256]{1,0:T(8,128)(2,1)S(1)} %get-tuple-element.47), channel_id=1, source_target_pairs={{0,12},{4,8},{8,4},{12,0},{1,13},{5,9},{9,5},{13,1},{2,14},{6,10},... | collective-permute-start | bytes 393224 | tf_op jit(solution)/shard_map/ppermute | solution.py:494
  43.0 1.4 %copy-start.18 = (f32[9,256,256]{2,1,0:T(8,128)}, f32[9,256,256]{2,1,0:T(8,128)S(1)}, u32[]{:S(2)}) copy-start(f32[9,256,256]{2,1,0:T(8,128)S(1)} %get-tuple-element.48.refs_4_) | copy-start | bytes 7077892
  47.9 12.4 %copy-start.1 = (bf16[512,2048]{1,0:T(8,128)(2,1)S(1)}, bf16[512,2048]{1,0:T(8,128)(2,1)}, u32[]{:S(2)}) copy-start(bf16[512,2048]{1,0:T(8,128)(2,1)} %refs_6_.2) | copy-start | bytes 6291460
  47.9 12.4 %copy-start.10 = (bf16[1,256,512]{2,1,0:T(8,128)(2,1)S(1)}, bf16[1,256,512]{2,1,0:T(8,128)(2,1)}, u32[]{:S(2)}) copy-start(bf16[1,256,512]{2,1,0:T(8,128)(2,1)} %param.8) | copy-start | bytes 786436
  48.7 11.6 %collective-permute-start.6 = (bf16[256,128]{1,0:T(8,128)(2,1)S(1)}, bf16[256,128]{1,0:T(8,128)(2,1)S(1)}, u32[]{:S(2)}, u32[]{:S(2)}) collective-permute-start(bf16[256,128]{1,0:T(8,128)(2,1)S(1)} %get-tuple-element.41.refs_4_.refs_7_), channel_id=1, source_target_pairs={{0,4},{4,0},{8,12},{12,8},{1,5},{5,1},{9,13},{13,9},{2,6},{6,2},{1... | collective-permute-start | bytes 196616 | tf_op jit(solution)/shard_map/ppermute | solution.py:494
  51.1 9.2 %collective-permute-start.7 = (bf16[256,128]{1,0:T(8,128)(2,1)S(1)}, bf16[256,128]{1,0:T(8,128)(2,1)S(1)}, u32[]{:S(2)}, u32[]{:S(2)}) collective-permute-start(bf16[256,128]{1,0:T(8,128)(2,1)S(1)} %get-tuple-element.42), channel_id=1, source_target_pairs={{0,8},{4,12},{8,0},{12,4},{1,9},{5,13},{9,1},{13,5},{2,10},{6,14},... | collective-permute-start | bytes 196616 | tf_op jit(solution)/shard_map/ppermute | solution.py:494
  51.8 8.5 %collective-permute-start.8 = (bf16[256,128]{1,0:T(8,128)(2,1)S(1)}, bf16[256,128]{1,0:T(8,128)(2,1)S(1)}, u32[]{:S(2)}, u32[]{:S(2)}) collective-permute-start(bf16[256,128]{1,0:T(8,128)(2,1)S(1)} %get-tuple-element.43), channel_id=1, source_target_pairs={{0,12},{4,8},{8,4},{12,0},{1,13},{5,9},{9,5},{13,1},{2,14},{6,10},... | collective-permute-start | bytes 196616 | tf_op jit(solution)/shard_map/ppermute | solution.py:494
  53.5 1.7 %copy-start.19 = (f32[9,256,256]{2,1,0:T(8,128)S(1)}, f32[9,256,256]{2,1,0:T(8,128)}, u32[]{:S(2)}) copy-start(f32[9,256,256]{2,1,0:T(8,128)} %copy-done.18) | copy-start | bytes 7077892
  60.3 28.9 %copy-start.3 = (bf16[1,256,512]{2,1,0:T(8,128)(2,1)S(1)}, bf16[1,256,512]{2,1,0:T(8,128)(2,1)}, u32[]{:S(2)}) copy-start(bf16[1,256,512]{2,1,0:T(8,128)(2,1)} %param.9) | copy-start | bytes 786436
  60.3 28.9 %copy-start.4 = (bf16[1,256,512]{2,1,0:T(8,128)(2,1)S(1)}, bf16[1,256,512]{2,1,0:T(8,128)(2,1)}, u32[]{:S(2)}) copy-start(bf16[1,256,512]{2,1,0:T(8,128)(2,1)} %param.10) | copy-start | bytes 786436
  60.3 1.1 copy-start.12
  63.2 34.2 %copy-start.13 = (bf16[512,256]{1,0:T(8,128)(2,1)}, bf16[512,256]{1,0:T(8,128)(2,1)S(1)}, u32[]{:S(2)}) copy-start(bf16[512,256]{1,0:T(8,128)(2,1)S(1)} %get-tuple-element.61.own_ref) | copy-start | bytes 786436
  63.2 45.0 %collective-permute-start.12 = (f32[2,256,512]{2,1,0:T(8,128)}, f32[2,256,512]{2,1,0:T(8,128)S(1)}, u32[]{:S(2)}, u32[]{:S(2)}) collective-permute-start(f32[2,256,512]{2,1,0:T(8,128)} %get-tuple-element.51), channel_id=1, source_target_pairs={{0,1},{1,0},{2,3},{3,2},{4,5},{5,4},{6,7},{7,6},{8,9},{9,8},{10,11... | collective-permute-start | bytes 3145736 | tf_op jit(solution)/shard_map/ppermute | solution.py:625
  63.2 8.6 %collective-permute-start.14 = (bf16[256,256]{1,0:T(8,128)(2,1)S(1)}, bf16[256,256]{1,0:T(8,128)(2,1)S(1)}, u32[]{:S(2)}, u32[]{:S(2)}) collective-permute-start(bf16[256,256]{1,0:T(8,128)(2,1)S(1)} %get-tuple-element.49.refs_7_), channel_id=1, source_target_pairs={{0,4},{4,0},{8,12},{12,8},{1,5},{5,1},{9,13},{13,9},{2,6},{6,2},{1... | collective-permute-start | bytes 393224 | tf_op jit(solution)/shard_map/ppermute | solution.py:494
  64.2 27.4 %collective-permute-start.18 = (bf16[512,256]{1,0:T(8,128)(2,1)S(1)}, bf16[512,256]{1,0:T(8,128)(2,1)S(1)}, u32[]{:S(2)}, u32[]{:S(2)}) collective-permute-start(bf16[512,256]{1,0:T(8,128)(2,1)S(1)} %get-tuple-element.61.own_ref), channel_id=1, source_target_pairs={{0,4},{4,8},{8,12},{1,5},{5,9},{9,13},{2,6},{6,10},{10,14},{3,7},{... | collective-permute-start | bytes 786440 | tf_op jit(solution)/shard_map/ppermute | solution.py:613
  67.1 24.5 %collective-permute-start.19 = (bf16[512,256]{1,0:T(8,128)(2,1)S(1)}, bf16[512,256]{1,0:T(8,128)(2,1)S(1)}, u32[]{:S(2)}, u32[]{:S(2)}) collective-permute-start(bf16[512,256]{1,0:T(8,128)(2,1)S(1)} %get-tuple-element.61.own_ref), channel_id=1, source_target_pairs={{4,0},{8,4},{12,8},{5,1},{9,5},{13,9},{6,2},{10,6},{14,10},{7,3},{... | collective-permute-start | bytes 786440 | tf_op jit(solution)/shard_map/ppermute | solution.py:613
  68.4 18.8 %collective-permute-start.15 = (bf16[256,256]{1,0:T(8,128)(2,1)S(1)}, bf16[256,256]{1,0:T(8,128)(2,1)S(1)}, u32[]{:S(2)}, u32[]{:S(2)}) collective-permute-start(bf16[256,256]{1,0:T(8,128)(2,1)S(1)} %get-tuple-element.56), channel_id=1, source_target_pairs={{0,8},{4,12},{8,0},{12,4},{1,9},{5,13},{9,1},{13,5},{2,10},{6,14},... | collective-permute-start | bytes 393224 | tf_op jit(solution)/shard_map/ppermute | solution.py:494
  71.7 17.4 %collective-permute-start.16 = (bf16[256,256]{1,0:T(8,128)(2,1)S(1)}, bf16[256,256]{1,0:T(8,128)(2,1)S(1)}, u32[]{:S(2)}, u32[]{:S(2)}) collective-permute-start(bf16[256,256]{1,0:T(8,128)(2,1)S(1)} %get-tuple-element.57), channel_id=1, source_target_pairs={{0,12},{4,8},{8,4},{12,0},{1,13},{5,9},{9,5},{13,1},{2,14},{6,10},... | collective-permute-start | bytes 393224 | tf_op jit(solution)/shard_map/ppermute | solution.py:494
  87.2 10.2 %collective-permute-start.22 = (bf16[512,256]{1,0:T(8,128)(2,1)S(1)}, bf16[512,256]{1,0:T(8,128)(2,1)S(1)}, u32[]{:S(2)}, u32[]{:S(2)}) collective-permute-start(bf16[512,256]{1,0:T(8,128)(2,1)S(1)} %get-tuple-element.61.own_ref), channel_id=1, source_target_pairs={{0,12},{12,0},{1,13},{13,1},{2,14},{14,2},{3,15},{15,3},{16,28},{2... | collective-permute-start | bytes 786440 | tf_op jit(solution)/shard_map/ppermute | solution.py:614
  90.1 7.3 %collective-permute-start.17 = (bf16[256,512]{1,0:T(8,128)(2,1)S(1)}, bf16[256,512]{1,0:T(8,128)(2,1)S(1)}, u32[]{:S(2)}, u32[]{:S(2)}) collective-permute-start(bf16[256,512]{1,0:T(8,128)(2,1)S(1)} %get-tuple-element.60.one_ref), channel_id=1, source_target_pairs={{0,16},{16,0},{1,17},{17,1},{2,18},{18,2},{3,19},{19,3},{4,20},{20... | collective-permute-start | bytes 786440 | tf_op jit(solution)/shard_map/ppermute | solution.py:639
  91.6 11.4 %copy-start.5 = (bf16[512,256]{1,0:T(8,128)(2,1)}, bf16[512,256]{1,0:T(8,128)(2,1)S(1)}, u32[]{:S(2)}) copy-start(bf16[512,256]{1,0:T(8,128)(2,1)S(1)} %collective-permute-done.18.one_ref.up_ref) | copy-start | bytes 786436
  91.6 11.4 %copy-start.6 = (bf16[512,256]{1,0:T(8,128)(2,1)}, bf16[512,256]{1,0:T(8,128)(2,1)S(1)}, u32[]{:S(2)}) copy-start(bf16[512,256]{1,0:T(8,128)(2,1)S(1)} %collective-permute-done.19.two_ref.down_ref) | copy-start | bytes 786436
  91.7 5.7 %collective-permute-start.20 = (bf16[512,256]{1,0:T(8,128)(2,1)S(1)}, bf16[512,256]{1,0:T(8,128)(2,1)S(1)}, u32[]{:S(2)}, u32[]{:S(2)}) collective-permute-start(bf16[512,256]{1,0:T(8,128)(2,1)S(1)} %get-tuple-element.62), channel_id=1, source_target_pairs={{4,8},{8,12},{5,9},{9,13},{6,10},{10,14},{7,11},{11,15},{20,24},{2... | collective-permute-start | bytes 786440 | tf_op jit(solution)/shard_map/ppermute | solution.py:616
  92.4 10.6 %collective-permute-start.21 = (bf16[512,256]{1,0:T(8,128)(2,1)S(1)}, bf16[512,256]{1,0:T(8,128)(2,1)}, u32[]{:S(2)}, u32[]{:S(2)}) collective-permute-start(bf16[512,256]{1,0:T(8,128)(2,1)S(1)} %get-tuple-element.63), channel_id=1, source_target_pairs={{4,0},{8,4},{5,1},{9,5},{6,2},{10,6},{7,3},{11,7},{20,16},{24,20},... | collective-permute-start | bytes 786440 | tf_op jit(solution)/shard_map/ppermute | solution.py:616
  97.4 0.7 copy-start.20
  97.4 5.6 %copy-start.7 = (bf16[256,512]{1,0:T(8,128)(2,1)}, bf16[256,512]{1,0:T(8,128)(2,1)S(1)}, u32[]{:S(2)}) copy-start(bf16[256,512]{1,0:T(8,128)(2,1)S(1)} %collective-permute-done.17.other_ref.refs_0_) | copy-start | bytes 786436
  98.1 4.9 %copy-start.21 = (bf16[512,256]{1,0:T(8,128)(2,1)}, bf16[512,256]{1,0:T(8,128)(2,1)S(1)}, u32[]{:S(2)}) copy-start(bf16[512,256]{1,0:T(8,128)(2,1)S(1)} %collective-permute-done.20.up2_ref) | copy-start | bytes 786436
  106.8 13.7 %copy-start.2 = (bf16[512,512]{1,0:T(8,128)(2,1)S(1)}, bf16[512,512]{1,0:T(8,128)(2,1)}, u32[]{:S(2)}) copy-start(bf16[512,512]{1,0:T(8,128)(2,1)} %shard_map.138.one_ref) | copy-start | bytes 1572868
  106.8 13.7 %collective-permute-start.23 = (bf16[512,512]{1,0:T(8,128)(2,1)}, bf16[512,512]{1,0:T(8,128)(2,1)S(1)}, u32[]{:S(2)}, u32[]{:S(2)}) collective-permute-start(bf16[512,512]{1,0:T(8,128)(2,1)} %shard_map.138.one_ref), channel_id=1, source_target_pairs={{0,16},{16,0},{1,17},{17,1},{2,18},{18,2},{3,19},{19,3},{4,20},{20... | collective-permute-start | bytes 1572872 | tf_op jit(solution)/shard_map/ppermute | solution.py:657
  108.3 7.9 %collective-permute-start.13 = (bf16[256,512]{1,0:T(8,128)(2,1)S(1)}, bf16[256,512]{1,0:T(8,128)(2,1)S(1)}, u32[]{:S(2)}, u32[]{:S(2)}) collective-permute-start(bf16[256,512]{1,0:T(8,128)(2,1)S(1)} %get-tuple-element.53), channel_id=1, source_target_pairs={{0,2},{1,3},{2,0},{3,1},{4,6},{5,7},{6,4},{7,5},{8,10},{9,11},{10,... | collective-permute-start | bytes 786440 | tf_op jit(solution)/shard_map/ppermute | solution.py:627
  109.9 0.9 copy-start.8
Sparse Core Ops, SparseCore 0:
  48.8 17.3 all-gather.2

commit v3 on v2

--- a/solution.py
+++ b/solution.py
@@ -196,7 +196,7 @@
 
 
 def each_chunk(lanes, body):
-    @pl.loop(0, LANES // ROWS)
+    @pl.loop(0, LANES // ROWS, unroll=2)
     def _(step):
         for lane in range(0, lanes, LANES):
             body(pl.multiple_of(step * ROWS, ROWS), lane)
@@ -363,7 +363,7 @@
 
 
 def gradient_kernel(parts, *refs):
-    cots, (w_ref, query_ref), refs = refs[:parts], refs[parts : parts + 2], refs[parts + 5 :]
+    cots, (w_ref, query_ref), refs = refs[:parts], refs[parts : parts + 2], refs[parts + 3 :]
     gated_grad_ref, *pieces, cot = refs
     me, part = lax.axis_index("ctx"), lax.axis_index("tp")
     positions, width = cots[0].shape
@@ -423,34 +423,22 @@
     out_ref[...] = (mine_ref[...] + other_ref[...].astype(F32)).astype(BF16)
 
 
-def pass_kernel(one_ref, two_ref, *refs):
-    one_out, two_out = refs[-2:]
-    one_out[...] = one_ref[...]
-    two_out[...] = two_ref[...]
-
-
-def weight_kernel(own_ref, up_ref, down_ref, up2_ref, down2_ref, end_ref, cot_ref, *refs):
-    out_ref, total, cot = refs[-3:]
+def pass_kernel(one_ref, _, out_ref):
+    out_ref[...] = one_ref[...]
+
+
+def weight_kernel(seqs, *refs):
+    pieces, cot_ref, (out_ref, cot) = refs[:seqs], refs[seqs], refs[-2:]
     me = lax.axis_index("ctx")
     parts = cot_ref.shape[0]
     quarter = cot_ref.shape[1] // parts
-    top = parts - 1
-
-    def term(gated_ref, block):
+    total = None
+    for r, ref in enumerate(pieces):
         for p in range(parts):
-            cot[pl.ds(p * quarter, quarter), :] = cot_ref[p, at_block(block, quarter), :]
-        return jnp.dot(gated_ref[...], cot[...], preferred_element_type=F32)
-
-    def add(gated_ref, block):
-        total[...] += term(gated_ref, block)
-
-    total[...] = term(own_ref, me)
-    pl.when(me > 1)(lambda: add(up2_ref, me - 2))
-    pl.when(me < top - 1)(lambda: add(down2_ref, me + 2))
-    pl.when(me > 0)(lambda: add(up_ref, me - 1))
-    pl.when(me < top)(lambda: add(down_ref, me + 1))
-    pl.when(jnp.logical_or(me == 0, me == top))(lambda: add(end_ref, top - me))
-    out_ref[...] = total[...].astype(BF16)
+            cot[r, pl.ds(p * quarter, quarter), :] = cot_ref[p, at_block(me ^ r, quarter), :]
+        term = jnp.dot(ref[...], cot[r], preferred_element_type=F32)
+        total = term if total is None else total + term
+    out_ref[...] = total.astype(BF16)
 
 
 def add_kernel(factor, one_ref, other_ref, out_ref):
@@ -539,9 +527,9 @@
         *cot_rows,
         w_out,
         query,
-        *held[1:],
+        held[1],
         scratch=[pltpu.VMEM((parts, positions, width), BF16)],
-        left=range(parts + 2, parts + 5),
+        left=(parts + 2,),
     )
     grad_held = exchange(conv_grad, "ctx")
 
@@ -609,13 +597,11 @@
         scratch=[pltpu.VMEM(rows, BF16)],
         left=(seqs + 3,),
     )
-    up, down = [[(d, d + o) for d in range(seqs) if 0 <= d + o < seqs] for o in (1, -1)]
-    above, below = lax.ppermute(turned, "ctx", up), lax.ppermute(turned, "ctx", down)
-    across = lax.ppermute(turned, "ctx", [(0, seqs - 1), (seqs - 1, 0)])
-    passed = call(pass_kernel, [shape_of((channels, positions), BF16)] * 2, 10**6, 10**6, above, below, back[1], left=(2,))
-    above2, below2 = lax.ppermute(passed[0], "ctx", up[1:]), lax.ppermute(passed[1], "ctx", down[:-1])
-
-
+    first, third = [[(d, d ^ r) for d in range(seqs)] for r in (1, 3)]
+    across = lax.ppermute(turned, "ctx", third)
+    near = lax.ppermute(turned, "ctx", first)
+    passed = call(pass_kernel, shape_of((channels, positions), BF16), 10**6, 10**6, across, back[1], left=(1,))
+    gathered = [turned, near, lax.ppermute(passed, "ctx", first), across]
     mine, far = call(
         pair_kernel,
         [shape_of((positions, width), F32), shape_of((positions, width), BF16)],
@@ -638,21 +624,16 @@
     )
     taps_other = lax.ppermute(taps, "dp", ring)
     weight_grad = call(
-        weight_kernel,
+        functools.partial(weight_kernel, seqs),
         shape_of((channels, width), BF16),
         2 * line * channels * width,
         3 * 10**6,
-        turned,
-        above,
-        below,
-        above2,
-        below2,
-        across,
+        *gathered,
         cot_cols,
-        taps_other,
-        left=(7,),
+        back[2],
+        left=(seqs + 1,),
         room=60,
-        scratch=[pltpu.VMEM((channels, width), F32), pltpu.VMEM((positions, width), BF16)],
+        scratch=[pltpu.VMEM((seqs, positions, width), BF16)],
     )
     weight_other = lax.ppermute(weight_grad, "dp", ring)
     grad_wout = call(

time: 129 us -> 120 us (0.930)
  starting transfers between devices: 39.8 us -> 32.7 us
  waiting for transfers between devices: 40.7 us -> 37.7 us
  local copies, waits for them, and re-layouts: 10.1 us -> 11.5 us
    ppermute x5 -> x3, waiting for transfers between devices: 8.64 us -> 2.01 us  [the longest x1 2.01 us: local_short(): gathered = [turned, near, lax.ppermute(passed, 'ctx', first), across]]
    ppermute x1, waiting for transfers between devices: 0.01 us -> 5.82 us  [local_short(): taps_other = lax.ppermute(taps, 'dp', ring)]
    ppermute x15, waiting for transfers between devices: 24.2 us -> 29.9 us  [exchange(): lax.ppermute(pieces[r], axis, [(d, d ^ r) for d in range(size)])]
    ppermute x1, waiting for transfers between devices: 4.38 us -> 0.01 us  [local_short(): far = lax.ppermute(far, 'tp', [(j, j ^ 2) for j in range(parts)])]
    ppermute x15, starting transfers between devices: 27.2 us -> 22.9 us  [exchange(): lax.ppermute(pieces[r], axis, [(d, d ^ r) for d in range(size)])]
    ppermute x1, waiting for transfers between devices: 3.51 us -> 0.01 us  [local_short(): weight_other = lax.ppermute(weight_grad, 'dp', ring)]
    ppermute x5 -> x3, starting transfers between devices: 8.07 us -> 6.19 us  [the longest x1 2.37 us: local_short(): across = lax.ppermute(turned, 'ctx', third)]
    unnamed x44 -> x50, local copies, waits for them, and re-layouts: 10.1 us -> 11.5 us
  transfers between devices with their start and end apart: 25 -> 23, of which waited for: 7 -> 7; matrix products, arithmetic and copies ran while one was open for 0% -> 0% of each run, Pallas kernels for 14% -> 18%
where the time goes in v3:
time: 120 us; the launch traced here: 119 us
  waiting for transfers between devices  37.7 us (31%)
  starting transfers between devices  32.7 us (27%)
  Pallas kernels  22.9 us (19%)
  between operations  14.3 us (12%)
  local copies, waits for them, and re-layouts  11.5 us (10%)
    ppermute x15, waiting for transfers between devices, exchange(): lax.ppermute(pieces[r], axis, [(d, d ^ r) for d in range(size)])  29.9 us
    pallas_call x13, Pallas kernels, call(): pl.pallas_call(kernel, out_shape=outs, in_specs=[anywhere if n in left el...  22.9 us
    ppermute x15, starting transfers between devices, exchange(): lax.ppermute(pieces[r], axis, [(d, d ^ r) for d in range(size)])  22.9 us
    unnamed x50, local copies, waits for them, and re-layouts  11.5 us
    ppermute x1, waiting for transfers between devices, local_short(): taps_other = lax.ppermute(taps, 'dp', ring)  5.82 us
  transfers between devices with their start and end apart: 23, of which 7 were waited for; matrix products, arithmetic and copies ran while one was open for 0% of the time, Pallas kernels for 18%

profile of v3, /device:TPU:0, one launch (start us, length us, event | category | flops | bytes accessed | tf_op | source)
XLA Modules:
  0.0 119.1 jit_solution(18137710082647090684)
XLA Ops:
  7.2 0.0 copy-start.19
  7.2 0.0 copy-start.20
  7.2 0.0 all-gather.3.cloned.1.call-start
  7.2 0.5 collective-permute-start.3
  7.8 2.6 %collective-permute-start.4 = (bf16[256,512]{1,0:T(8,128)(2,1)}, bf16[256,512]{1,0:T(8,128)(2,1)S(1)}, u32[]{:S(2)}, u32[]{:S(2)}) collective-permute-start(bf16[256,512]{1,0:T(8,128)(2,1)} %bitcast.16), channel_id=1, source_target_pairs={{0,2},{1,3},{2,0},{3,1},{4,6},{5,7},{6,4},{7,5},{8,10},{9,11},{10,... | collective-permute-start | bytes 786440 | tf_op jit(solution)/shard_map/ppermute | solution.py:482
  10.3 0.1 collective-permute-start.5
  10.4 2.1 %shard_map.127 = (bf16[256,256]{1,0:T(8,128)(2,1)}, bf16[256,256]{1,0:T(8,128)(2,1)}, bf16[256,256]{1,0:T(8,128)(2,1)}, bf16[256,256]{1,0:T(8,128)(2,1)}) custom-call(bf16[256,512]{1,0:T(8,128)(2,1)} %bitcast.11, bf16[256,512]{1,0:T(8,128)(2,1)} %bitcast.13, f32[512,256]{1,0:T(8,128)} %refs_2_.1), custom_call_target="tpu_custom_call" | custom-call | flops 1000000 | bytes 2000000 | tf_op jit(solution)/shard_map/pallas_call | solution.py:469
  12.6 1.8 %collective-permute-start = (bf16[256,256]{1,0:T(8,128)(2,1)}, bf16[256,256]{1,0:T(8,128)(2,1)S(1)}, u32[]{:S(2)}, u32[]{:S(2)}) collective-permute-start(bf16[256,256]{1,0:T(8,128)(2,1)} %get-tuple-element.34), channel_id=1, source_target_pairs={{0,4},{4,0},{8,12},{12,8},{1,5},{5,1},{9,13},{13,9},{2,6},{6,2},{1... | collective-permute-start | bytes 393224 | tf_op jit(solution)/shard_map/ppermute | solution.py:482
  14.4 2.6 %collective-permute-start.1 = (bf16[256,256]{1,0:T(8,128)(2,1)}, bf16[256,256]{1,0:T(8,128)(2,1)S(1)}, u32[]{:S(2)}, u32[]{:S(2)}) collective-permute-start(bf16[256,256]{1,0:T(8,128)(2,1)} %get-tuple-element.35), channel_id=1, source_target_pairs={{0,8},{4,12},{8,0},{12,4},{1,9},{5,13},{9,1},{13,5},{2,10},{6,14},... | collective-permute-start | bytes 393224 | tf_op jit(solution)/shard_map/ppermute | solution.py:482
  17.0 4.1 %collective-permute-done.refs_6_.refs_1_ = bf16[256,256]{1,0:T(8,128)(2,1)S(1)} collective-permute-done((bf16[256,256]{1,0:T(8,128)(2,1)}, bf16[256,256]{1,0:T(8,128)(2,1)S(1)}, u32[]{:S(2)}, u32[]{:S(2)}) %collective-permute-start) | collective-permute-done | bytes 131104 | tf_op jit(solution)/shard_map/ppermute | solution.py:482
  21.1 2.9 %collective-permute-start.2 = (bf16[256,256]{1,0:T(8,128)(2,1)}, bf16[256,256]{1,0:T(8,128)(2,1)S(1)}, u32[]{:S(2)}, u32[]{:S(2)}) collective-permute-start(bf16[256,256]{1,0:T(8,128)(2,1)} %get-tuple-element.36), channel_id=1, source_target_pairs={{0,12},{4,8},{8,4},{12,0},{1,13},{5,9},{9,5},{13,1},{2,14},{6,10},... | collective-permute-start | bytes 393224 | tf_op jit(solution)/shard_map/ppermute | solution.py:482
  24.0 0.0 copy-start
  24.0 1.6 %copy-done = bf16[512,2048]{1,0:T(8,128)(2,1)S(1)} copy-done((bf16[512,2048]{1,0:T(8,128)(2,1)S(1)}, bf16[512,2048]{1,0:T(8,128)(2,1)}, u32[]{:S(2)}) %copy-start) | copy-done | bytes 2097176
  25.6 0.9 copy-done.3
  26.5 0.9 copy-done.12
  27.5 0.9 shard_map.128
  28.4 0.0 copy-start.8
  28.4 0.8 copy-done.8
  29.2 0.5 collective-permute-start.9
  29.6 2.6 %collective-permute-start.10 = (bf16[256,256]{1,0:T(8,128)(2,1)S(1)}, bf16[256,256]{1,0:T(8,128)(2,1)S(1)}, u32[]{:S(2)}, u32[]{:S(2)}) collective-permute-start(bf16[256,256]{1,0:T(8,128)(2,1)S(1)} %get-tuple-element.44), channel_id=1, source_target_pairs={{0,8},{4,12},{8,0},{12,4},{1,9},{5,13},{9,1},{13,5},{2,10},{6,14},... | collective-permute-start | bytes 393224 | tf_op jit(solution)/shard_map/ppermute | solution.py:482
  32.2 1.3 %collective-permute-start.11 = (bf16[256,256]{1,0:T(8,128)(2,1)S(1)}, bf16[256,256]{1,0:T(8,128)(2,1)S(1)}, u32[]{:S(2)}, u32[]{:S(2)}) collective-permute-start(bf16[256,256]{1,0:T(8,128)(2,1)S(1)} %get-tuple-element.45), channel_id=1, source_target_pairs={{0,12},{4,8},{8,4},{12,0},{1,13},{5,9},{9,5},{13,1},{2,14},{6,10},... | collective-permute-start | bytes 393224 | tf_op jit(solution)/shard_map/ppermute | solution.py:482
  33.6 4.6 %shard_map.129 = (bf16[256,128]{1,0:T(8,128)(2,1)S(1)}, bf16[256,128]{1,0:T(8,128)(2,1)S(1)}, bf16[256,128]{1,0:T(8,128)(2,1)S(1)}, bf16[256,128]{1,0:T(8,128)(2,1)S(1)}, f32[9,256,256]{2,1,0:T(8,128)S(1)}) custom-call(bf16[256,256]{1,0:T(8,128)(2,1)S(1)} %copy-done.18, bf16[256,256]{1,0:T(8,128)(2,1)S(1)} %collective-permute-done.refs_6_.refs_1_, ...), custom_call_target="tpu_custom_call" | custom-call | flops 1000000000 | bytes 9000000 | tf_op jit(solution)/shard_map/pallas_call | solution.py:469
  38.2 0.0 copy-start.14
  38.2 0.6 copy-done.14
  38.8 1.4 %copy-done.21 = f32[9,256,256]{2,1,0:T(8,128)} copy-done((f32[9,256,256]{2,1,0:T(8,128)}, f32[9,256,256]{2,1,0:T(8,128)S(1)}, u32[]{:S(2)}) %copy-start.21) | copy-done | bytes 2359320
  40.2 0.0 collective-permute-done.9.refs_1_
  40.3 2.2 %collective-permute-done.10.refs_2_ = bf16[256,256]{1,0:T(8,128)(2,1)S(1)} collective-permute-done((bf16[256,256]{1,0:T(8,128)(2,1)S(1)}, bf16[256,256]{1,0:T(8,128)(2,1)S(1)}, u32[]{:S(2)}, u32[]{:S(2)}) %collective-permute-start.10) | collective-permute-done | bytes 131104 | tf_op jit(solution)/shard_map/ppermute | solution.py:482
  42.5 0.8 shard_map.130.refs_8_
  43.3 0.0 all-gather.3.cloned.1.call-update
  43.3 2.8 %collective-permute-start.6 = (bf16[256,128]{1,0:T(8,128)(2,1)S(1)}, bf16[256,128]{1,0:T(8,128)(2,1)S(1)}, u32[]{:S(2)}, u32[]{:S(2)}) collective-permute-start(bf16[256,128]{1,0:T(8,128)(2,1)S(1)} %get-tuple-element.39.refs_4_.refs_7_), channel_id=1, source_target_pairs={{0,4},{4,0},{8,12},{12,8},{1,5},{5,1},{9,13},{13,9},{2,6},{6,2},{1... | collective-permute-start | bytes 196616 | tf_op jit(solution)/shard_map/ppermute | solution.py:482
  46.1 0.9 collective-permute-start.7
  47.0 1.5 %collective-permute-start.8 = (bf16[256,128]{1,0:T(8,128)(2,1)S(1)}, bf16[256,128]{1,0:T(8,128)(2,1)S(1)}, u32[]{:S(2)}, u32[]{:S(2)}) collective-permute-start(bf16[256,128]{1,0:T(8,128)(2,1)S(1)} %get-tuple-element.41), channel_id=1, source_target_pairs={{0,12},{4,8},{8,4},{12,0},{1,13},{5,9},{9,5},{13,1},{2,14},{6,10},... | collective-permute-start | bytes 196616 | tf_op jit(solution)/shard_map/ppermute | solution.py:482
  48.5 1.7 %copy-done.22 = f32[9,256,256]{2,1,0:T(8,128)S(1)} copy-done((f32[9,256,256]{2,1,0:T(8,128)S(1)}, f32[9,256,256]{2,1,0:T(8,128)}, u32[]{:S(2)}) %copy-start.22) | copy-done | bytes 2359320
  50.2 4.6 %shard_map.131 = (bf16[256,256]{1,0:T(8,128)(2,1)S(1)}, bf16[256,256]{1,0:T(8,128)(2,1)S(1)}, bf16[256,256]{1,0:T(8,128)(2,1)S(1)}, bf16[256,256]{1,0:T(8,128)(2,1)S(1)}) custom-call(bf16[256,256]{1,0:T(8,128)(2,1)S(1)} %get-tuple-element.43.refs_0_, bf16[256,256]{1,0:T(8,128)(2,1)S(1)} %collective-permute-done.9.refs_1_, ...), custom_call_target="tpu_custom_call" | custom-call | flops 1000000000 | bytes 9000000 | tf_op jit(solution)/shard_map/pallas_call | solution.py:469
  54.8 0.0 collective-permute-done.7.refs_2_
  54.8 0.0 collective-permute-done.8.refs_3_
  54.8 0.0 copy-start.9
  54.8 1.0 copy-done.9
  55.9 0.8 copy-done.15
  56.7 1.7 %shard_map.132 = (bf16[512,256]{1,0:T(8,128)(2,1)S(1)}, bf16[256,512]{1,0:T(8,128)(2,1)}, f32[2,256,512]{2,1,0:T(8,128)S(1)}, f32[2,256,512]{2,1,0:T(8,128)}) custom-call(bf16[256,128]{1,0:T(8,128)(2,1)S(1)} %copy-done.15, bf16[256,128]{1,0:T(8,128)(2,1)S(1)} %collective-permute-done.6.refs_1_, bf16[256,128]{1,0:T(8,128)(2,1)S(1)} %collective-permute-done.7.refs_2_, ...), custom_call_target="tpu_custom_call" | custom-call | flops 536870912 | bytes 5000000 | tf_op jit(solution)/shard_map/pallas_call | solution.py:469
  58.5 0.0 collective-permute-start.12
  58.5 2.4 %collective-permute-start.19 = (bf16[512,256]{1,0:T(8,128)(2,1)S(1)}, bf16[512,256]{1,0:T(8,128)(2,1)S(1)}, u32[]{:S(2)}, u32[]{:S(2)}) collective-permute-start(bf16[512,256]{1,0:T(8,128)(2,1)S(1)} %get-tuple-element.59.refs_0_), channel_id=1, source_target_pairs={{0,12},{4,8},{8,4},{12,0},{1,13},{5,9},{9,5},{13,1},{2,14},{6,10},... | collective-permute-start | bytes 786440 | tf_op jit(solution)/shard_map/ppermute | solution.py:601
  60.8 0.1 collective-permute-start.14
  61.0 1.9 %collective-permute-start.18 = (bf16[512,256]{1,0:T(8,128)(2,1)S(1)}, bf16[512,256]{1,0:T(8,128)(2,1)S(1)}, u32[]{:S(2)}, u32[]{:S(2)}) collective-permute-start(bf16[512,256]{1,0:T(8,128)(2,1)S(1)} %get-tuple-element.59.refs_0_), channel_id=1, source_target_pairs={{0,4},{4,0},{8,12},{12,8},{1,5},{5,1},{9,13},{13,9},{2,6},{6,2},{1... | collective-permute-start | bytes 786440 | tf_op jit(solution)/shard_map/ppermute | solution.py:602
  62.9 9.1 %collective-permute-done.14.refs_1_._ = bf16[256,256]{1,0:T(8,128)(2,1)S(1)} collective-permute-done((bf16[256,256]{1,0:T(8,128)(2,1)S(1)}, bf16[256,256]{1,0:T(8,128)(2,1)S(1)}, u32[]{:S(2)}, u32[]{:S(2)}) %collective-permute-start.14) | collective-permute-done | bytes 131104 | tf_op jit(solution)/shard_map/ppermute | solution.py:482
  72.0 1.9 %collective-permute-start.20 = (bf16[512,256]{1,0:T(8,128)(2,1)S(1)}, bf16[512,256]{1,0:T(8,128)(2,1)S(1)}, u32[]{:S(2)}, u32[]{:S(2)}) collective-permute-start(bf16[512,256]{1,0:T(8,128)(2,1)S(1)} %shard_map.137), channel_id=1, source_target_pairs={{0,4},{4,0},{8,12},{12,8},{1,5},{5,1},{9,13},{13,9},{2,6},{6,2},{1... | collective-permute-start | bytes 786440 | tf_op jit(solution)/shard_map/ppermute | solution.py:604
  73.9 0.9 collective-permute-start.15
  74.8 9.0 %collective-permute-done.15.refs_2_.refs_5_ = bf16[256,256]{1,0:T(8,128)(2,1)S(1)} collective-permute-done((bf16[256,256]{1,0:T(8,128)(2,1)S(1)}, bf16[256,256]{1,0:T(8,128)(2,1)S(1)}, u32[]{:S(2)}, u32[]{:S(2)}) %collective-permute-start.15) | collective-permute-done | bytes 131104 | tf_op jit(solution)/shard_map/ppermute | solution.py:482
  83.9 0.0 copy-start.23
  83.9 2.0 %collective-permute-done.20.refs_2_ = bf16[512,256]{1,0:T(8,128)(2,1)S(1)} collective-permute-done((bf16[512,256]{1,0:T(8,128)(2,1)S(1)}, bf16[512,256]{1,0:T(8,128)(2,1)S(1)}, u32[]{:S(2)}, u32[]{:S(2)}) %collective-permute-start.20) | collective-permute-done | bytes 262176 | tf_op jit(solution)/shard_map/ppermute | solution.py:604
  86.0 0.7 copy-done.24
  86.6 3.1 %shard_map.138.one_ref = bf16[512,512]{1,0:T(8,128)(2,1)} custom-call(bf16[512,256]{1,0:T(8,128)(2,1)} %copy-done.13, bf16[512,256]{1,0:T(8,128)(2,1)} %copy-done.23, bf16[512,256]{1,0:T(8,128)(2,1)} %copy-done.24, bf16[512,256]{1,0:T(8,128)(2,1)} %copy-done.7, bf16[4,256,512]{2,1,0:T(8,128)(2,1)} %bitcast.19, bf16[256,256]{1,0:T(8,128)(2,1)} %copy-done.10), custom_call_target="tpu_custom_call" | custom-call | flops 536870912 | bytes 3000000 | tf_op jit(solution)/shard_map/pallas_call | solution.py:469
  89.7 1.5 %collective-permute-start.21 = (bf16[512,512]{1,0:T(8,128)(2,1)}, bf16[512,512]{1,0:T(8,128)(2,1)S(1)}, u32[]{:S(2)}, u32[]{:S(2)}) collective-permute-start(bf16[512,512]{1,0:T(8,128)(2,1)} %shard_map.138.one_ref), channel_id=1, source_target_pairs={{0,16},{16,0},{1,17},{17,1},{2,18},{18,2},{3,19},{19,3},{4,20},{20... | collective-permute-start | bytes 1572872 | tf_op jit(solution)/shard_map/ppermute | solution.py:638
  91.2 1.6 %collective-permute-start.16 = (bf16[256,256]{1,0:T(8,128)(2,1)S(1)}, bf16[256,256]{1,0:T(8,128)(2,1)S(1)}, u32[]{:S(2)}, u32[]{:S(2)}) collective-permute-start(bf16[256,256]{1,0:T(8,128)(2,1)S(1)} %copy-done.17), channel_id=1, source_target_pairs={{0,12},{4,8},{8,4},{12,0},{1,13},{5,9},{9,5},{13,1},{2,14},{6,10},... | collective-permute-start | bytes 393224 | tf_op jit(solution)/shard_map/ppermute | solution.py:482
  92.8 5.4 %collective-permute-done.16.refs_3_ = bf16[256,256]{1,0:T(8,128)(2,1)S(1)} collective-permute-done((bf16[256,256]{1,0:T(8,128)(2,1)S(1)}, bf16[256,256]{1,0:T(8,128)(2,1)S(1)}, u32[]{:S(2)}, u32[]{:S(2)}) %collective-permute-start.16) | collective-permute-done | bytes 131104 | tf_op jit(solution)/shard_map/ppermute | solution.py:482
  98.3 0.9 copy-done.11
  99.2 0.9 shard_map.135
  100.1 0.5 collective-permute-start.17
  100.6 1.3 %shard_map.133 = (f32[256,512]{1,0:T(8,128)S(1)}, bf16[256,512]{1,0:T(8,128)(2,1)S(1)}) custom-call(f32[2,256,512]{2,1,0:T(8,128)S(1)} %get-tuple-element.48.keep_ref, f32[2,256,512]{2,1,0:T(8,128)} %collective-permute-done.12.other_ref), custom_call_target="tpu_custom_call" | custom-call | flops 1000000 | bytes 3000000 | tf_op jit(solution)/shard_map/pallas_call | solution.py:469
  102.0 1.6 %collective-permute-start.13 = (bf16[256,512]{1,0:T(8,128)(2,1)S(1)}, bf16[256,512]{1,0:T(8,128)(2,1)S(1)}, u32[]{:S(2)}, u32[]{:S(2)}) collective-permute-start(bf16[256,512]{1,0:T(8,128)(2,1)S(1)} %get-tuple-element.51), channel_id=1, source_target_pairs={{0,2},{1,3},{2,0},{3,1},{4,6},{5,7},{6,4},{7,5},{8,10},{9,11},{10,... | collective-permute-start | bytes 786440 | tf_op jit(solution)/shard_map/ppermute | solution.py:613
  103.6 5.8 %collective-permute-done.17.other_ref = bf16[256,512]{1,0:T(8,128)(2,1)S(1)} collective-permute-done((bf16[256,512]{1,0:T(8,128)(2,1)S(1)}, bf16[256,512]{1,0:T(8,128)(2,1)S(1)}, u32[]{:S(2)}, u32[]{:S(2)}) %collective-permute-start.17) | collective-permute-done | bytes 262176 | tf_op jit(solution)/shard_map/ppermute | solution.py:625
  109.4 1.0 shard_map.136
  110.4 0.7 shard_map.134
  111.1 1.1 shard_map.139
  (46 shorter events, 0.1 us)
Async XLA Ops:
  7.2 26.4 %copy-start.19 = (bf16[2,256,256]{2,1,0:T(8,128)(2,1)S(1)}, bf16[2,256,256]{2,1,0:T(8,128)(2,1)}, u32[]{:S(2)}) copy-start(bf16[2,256,256]{2,1,0:T(8,128)(2,1)} %constant.4.clone.refs_4_.refs_5_) | copy-start | bytes 786436
  7.2 26.4 %copy-start.20 = (f32[128,128]{1,0:T(8,128)S(1)}, f32[128,128]{1,0:T(8,128)}, u32[]{:S(2)}) copy-start(f32[128,128]{1,0:T(8,128)} %constant.5.clone.refs_5_.refs_6_) | copy-start | bytes 196612
  7.2 78.7 %all-gather.3.cloned.1.call-start = ((), (), s32[]{:S(2)}) async-start(), calls=%async_computation | async-start | bytes 1310720 | tf_op jit(solution)/shard_map/all_gather | solution.py:565
  7.2 16.7 %collective-permute-start.3 = (bf16[256,512]{1,0:T(8,128)(2,1)}, bf16[256,512]{1,0:T(8,128)(2,1)S(1)}, u32[]{:S(2)}, u32[]{:S(2)}) collective-permute-start(bf16[256,512]{1,0:T(8,128)(2,1)} %bitcast.15), channel_id=1, source_target_pairs={{0,1},{1,0},{2,3},{3,2},{4,5},{5,4},{6,7},{7,6},{8,9},{9,8},{10,11... | collective-permute-start | bytes 786440 | tf_op jit(solution)/shard_map/ppermute | solution.py:482
  7.8 16.2 %collective-permute-start.4 = (bf16[256,512]{1,0:T(8,128)(2,1)}, bf16[256,512]{1,0:T(8,128)(2,1)S(1)}, u32[]{:S(2)}, u32[]{:S(2)}) collective-permute-start(bf16[256,512]{1,0:T(8,128)(2,1)} %bitcast.16), channel_id=1, source_target_pairs={{0,2},{1,3},{2,0},{3,1},{4,6},{5,7},{6,4},{7,5},{8,10},{9,11},{10,... | collective-permute-start | bytes 786440 | tf_op jit(solution)/shard_map/ppermute | solution.py:482
  10.3 13.6 %collective-permute-start.5 = (bf16[256,512]{1,0:T(8,128)(2,1)}, bf16[256,512]{1,0:T(8,128)(2,1)S(1)}, u32[]{:S(2)}, u32[]{:S(2)}) collective-permute-start(bf16[256,512]{1,0:T(8,128)(2,1)} %bitcast.17), channel_id=1, source_target_pairs={{0,3},{1,2},{2,1},{3,0},{4,7},{5,6},{6,5},{7,4},{8,11},{9,10},{10,... | collective-permute-start | bytes 786440 | tf_op jit(solution)/shard_map/ppermute | solution.py:482
  12.6 8.5 %collective-permute-start = (bf16[256,256]{1,0:T(8,128)(2,1)}, bf16[256,256]{1,0:T(8,128)(2,1)S(1)}, u32[]{:S(2)}, u32[]{:S(2)}) collective-permute-start(bf16[256,256]{1,0:T(8,128)(2,1)} %get-tuple-element.34), channel_id=1, source_target_pairs={{0,4},{4,0},{8,12},{12,8},{1,5},{5,1},{9,13},{13,9},{2,6},{6,2},{1... | collective-permute-start | bytes 393224 | tf_op jit(solution)/shard_map/ppermute | solution.py:482
  14.4 19.1 %collective-permute-start.1 = (bf16[256,256]{1,0:T(8,128)(2,1)}, bf16[256,256]{1,0:T(8,128)(2,1)S(1)}, u32[]{:S(2)}, u32[]{:S(2)}) collective-permute-start(bf16[256,256]{1,0:T(8,128)(2,1)} %get-tuple-element.35), channel_id=1, source_target_pairs={{0,8},{4,12},{8,0},{12,4},{1,9},{5,13},{9,1},{13,5},{2,10},{6,14},... | collective-permute-start | bytes 393224 | tf_op jit(solution)/shard_map/ppermute | solution.py:482
  21.1 12.5 %collective-permute-start.2 = (bf16[256,256]{1,0:T(8,128)(2,1)}, bf16[256,256]{1,0:T(8,128)(2,1)S(1)}, u32[]{:S(2)}, u32[]{:S(2)}) collective-permute-start(bf16[256,256]{1,0:T(8,128)(2,1)} %get-tuple-element.36), channel_id=1, source_target_pairs={{0,12},{4,8},{8,4},{12,0},{1,13},{5,9},{9,5},{13,1},{2,14},{6,10},... | collective-permute-start | bytes 393224 | tf_op jit(solution)/shard_map/ppermute | solution.py:482
  24.0 1.6 %copy-start = (bf16[512,2048]{1,0:T(8,128)(2,1)S(1)}, bf16[512,2048]{1,0:T(8,128)(2,1)}, u32[]{:S(2)}) copy-start(bf16[512,2048]{1,0:T(8,128)(2,1)} %refs_6_.2) | copy-start | bytes 6291460
  25.6 0.9 copy-start.3
  26.5 0.9 copy-start.12
  27.5 6.1 %copy-start.18 = (bf16[256,256]{1,0:T(8,128)(2,1)S(1)}, bf16[256,256]{1,0:T(8,128)(2,1)}, u32[]{:S(2)}) copy-start(bf16[256,256]{1,0:T(8,128)(2,1)} %get-tuple-element.33.refs_0_) | copy-start | bytes 393220
  28.4 0.8 copy-start.8
  29.2 11.1 %collective-permute-start.9 = (bf16[256,256]{1,0:T(8,128)(2,1)S(1)}, bf16[256,256]{1,0:T(8,128)(2,1)S(1)}, u32[]{:S(2)}, u32[]{:S(2)}) collective-permute-start(bf16[256,256]{1,0:T(8,128)(2,1)S(1)} %get-tuple-element.37.refs_6_), channel_id=1, source_target_pairs={{0,4},{4,0},{8,12},{12,8},{1,5},{5,1},{9,13},{13,9},{2,6},{6,2},{1... | collective-permute-start | bytes 393224 | tf_op jit(solution)/shard_map/ppermute | solution.py:482
  29.6 12.9 %collective-permute-start.10 = (bf16[256,256]{1,0:T(8,128)(2,1)S(1)}, bf16[256,256]{1,0:T(8,128)(2,1)S(1)}, u32[]{:S(2)}, u32[]{:S(2)}) collective-permute-start(bf16[256,256]{1,0:T(8,128)(2,1)S(1)} %get-tuple-element.44), channel_id=1, source_target_pairs={{0,8},{4,12},{8,0},{12,4},{1,9},{5,13},{9,1},{13,5},{2,10},{6,14},... | collective-permute-start | bytes 393224 | tf_op jit(solution)/shard_map/ppermute | solution.py:482
  32.2 10.3 %collective-permute-start.11 = (bf16[256,256]{1,0:T(8,128)(2,1)S(1)}, bf16[256,256]{1,0:T(8,128)(2,1)S(1)}, u32[]{:S(2)}, u32[]{:S(2)}) collective-permute-start(bf16[256,256]{1,0:T(8,128)(2,1)S(1)} %get-tuple-element.45), channel_id=1, source_target_pairs={{0,12},{4,8},{8,4},{12,0},{1,13},{5,9},{9,5},{13,1},{2,14},{6,10},... | collective-permute-start | bytes 393224 | tf_op jit(solution)/shard_map/ppermute | solution.py:482
  38.2 0.6 copy-start.14
  38.8 1.4 %copy-start.21 = (f32[9,256,256]{2,1,0:T(8,128)}, f32[9,256,256]{2,1,0:T(8,128)S(1)}, u32[]{:S(2)}) copy-start(f32[9,256,256]{2,1,0:T(8,128)S(1)} %get-tuple-element.46.refs_4_) | copy-start | bytes 7077892
  42.5 12.3 %copy-start.1 = (bf16[512,2048]{1,0:T(8,128)(2,1)S(1)}, bf16[512,2048]{1,0:T(8,128)(2,1)}, u32[]{:S(2)}) copy-start(bf16[512,2048]{1,0:T(8,128)(2,1)} %refs_6_.2) | copy-start | bytes 6291460
  42.5 12.3 %copy-start.4 = (bf16[1,256,512]{2,1,0:T(8,128)(2,1)S(1)}, bf16[1,256,512]{2,1,0:T(8,128)(2,1)}, u32[]{:S(2)}) copy-start(bf16[1,256,512]{2,1,0:T(8,128)(2,1)} %param.8) | copy-start | bytes 786436
  43.3 11.5 %collective-permute-start.6 = (bf16[256,128]{1,0:T(8,128)(2,1)S(1)}, bf16[256,128]{1,0:T(8,128)(2,1)S(1)}, u32[]{:S(2)}, u32[]{:S(2)}) collective-permute-start(bf16[256,128]{1,0:T(8,128)(2,1)S(1)} %get-tuple-element.39.refs_4_.refs_7_), channel_id=1, source_target_pairs={{0,4},{4,0},{8,12},{12,8},{1,5},{5,1},{9,13},{13,9},{2,6},{6,2},{1... | collective-permute-start | bytes 196616 | tf_op jit(solution)/shard_map/ppermute | solution.py:482
  46.1 8.7 %collective-permute-start.7 = (bf16[256,128]{1,0:T(8,128)(2,1)S(1)}, bf16[256,128]{1,0:T(8,128)(2,1)S(1)}, u32[]{:S(2)}, u32[]{:S(2)}) collective-permute-start(bf16[256,128]{1,0:T(8,128)(2,1)S(1)} %get-tuple-element.40), channel_id=1, source_target_pairs={{0,8},{4,12},{8,0},{12,4},{1,9},{5,13},{9,1},{13,5},{2,10},{6,14},... | collective-permute-start | bytes 196616 | tf_op jit(solution)/shard_map/ppermute | solution.py:482
  47.0 7.8 %collective-permute-start.8 = (bf16[256,128]{1,0:T(8,128)(2,1)S(1)}, bf16[256,128]{1,0:T(8,128)(2,1)S(1)}, u32[]{:S(2)}, u32[]{:S(2)}) collective-permute-start(bf16[256,128]{1,0:T(8,128)(2,1)S(1)} %get-tuple-element.41), channel_id=1, source_target_pairs={{0,12},{4,8},{8,4},{12,0},{1,13},{5,9},{9,5},{13,1},{2,14},{6,10},... | collective-permute-start | bytes 196616 | tf_op jit(solution)/shard_map/ppermute | solution.py:482
  48.5 1.7 %copy-start.22 = (f32[9,256,256]{2,1,0:T(8,128)S(1)}, f32[9,256,256]{2,1,0:T(8,128)}, u32[]{:S(2)}) copy-start(f32[9,256,256]{2,1,0:T(8,128)} %copy-done.21) | copy-start | bytes 7077892
  54.8 29.1 %copy-start.16 = (bf16[256,256]{1,0:T(8,128)(2,1)}, bf16[256,256]{1,0:T(8,128)(2,1)S(1)}, u32[]{:S(2)}) copy-start(bf16[256,256]{1,0:T(8,128)(2,1)S(1)} %get-tuple-element.55) | copy-start | bytes 393220
  54.8 1.0 copy-start.9
  55.9 0.8 copy-start.15
  58.4 25.4 %copy-start.13 = (bf16[512,256]{1,0:T(8,128)(2,1)}, bf16[512,256]{1,0:T(8,128)(2,1)S(1)}, u32[]{:S(2)}) copy-start(bf16[512,256]{1,0:T(8,128)(2,1)S(1)} %get-tuple-element.59.refs_0_) | copy-start | bytes 786436
  58.4 39.8 %copy-start.5 = (bf16[1,256,512]{2,1,0:T(8,128)(2,1)S(1)}, bf16[1,256,512]{2,1,0:T(8,128)(2,1)}, u32[]{:S(2)}) copy-start(bf16[1,256,512]{2,1,0:T(8,128)(2,1)} %param.9) | copy-start | bytes 786436
  58.4 39.8 %copy-start.6 = (bf16[1,256,512]{2,1,0:T(8,128)(2,1)S(1)}, bf16[1,256,512]{2,1,0:T(8,128)(2,1)}, u32[]{:S(2)}) copy-start(bf16[1,256,512]{2,1,0:T(8,128)(2,1)} %param.10) | copy-start | bytes 786436
  58.5 42.2 %collective-permute-start.12 = (f32[2,256,512]{2,1,0:T(8,128)}, f32[2,256,512]{2,1,0:T(8,128)}, u32[]{:S(2)}, u32[]{:S(2)}) collective-permute-start(f32[2,256,512]{2,1,0:T(8,128)} %get-tuple-element.49), channel_id=1, source_target_pairs={{0,1},{1,0},{2,3},{3,2},{4,5},{5,4},{6,7},{7,6},{8,9},{9,8},{10,11... | collective-permute-start | bytes 3145736 | tf_op jit(solution)/shard_map/ppermute | solution.py:611
  58.5 13.5 %collective-permute-start.19 = (bf16[512,256]{1,0:T(8,128)(2,1)S(1)}, bf16[512,256]{1,0:T(8,128)(2,1)S(1)}, u32[]{:S(2)}, u32[]{:S(2)}) collective-permute-start(bf16[512,256]{1,0:T(8,128)(2,1)S(1)} %get-tuple-element.59.refs_0_), channel_id=1, source_target_pairs={{0,12},{4,8},{8,4},{12,0},{1,13},{5,9},{9,5},{13,1},{2,14},{6,10},... | collective-permute-start | bytes 786440 | tf_op jit(solution)/shard_map/ppermute | solution.py:601
  60.8 11.1 %collective-permute-start.14 = (bf16[256,256]{1,0:T(8,128)(2,1)S(1)}, bf16[256,256]{1,0:T(8,128)(2,1)S(1)}, u32[]{:S(2)}, u32[]{:S(2)}) collective-permute-start(bf16[256,256]{1,0:T(8,128)(2,1)S(1)} %get-tuple-element.47.refs_7_), channel_id=1, source_target_pairs={{0,4},{4,0},{8,12},{12,8},{1,5},{5,1},{9,13},{13,9},{2,6},{6,2},{1... | collective-permute-start | bytes 393224 | tf_op jit(solution)/shard_map/ppermute | solution.py:482
  61.0 22.9 %collective-permute-start.18 = (bf16[512,256]{1,0:T(8,128)(2,1)S(1)}, bf16[512,256]{1,0:T(8,128)(2,1)S(1)}, u32[]{:S(2)}, u32[]{:S(2)}) collective-permute-start(bf16[512,256]{1,0:T(8,128)(2,1)S(1)} %get-tuple-element.59.refs_0_), channel_id=1, source_target_pairs={{0,4},{4,0},{8,12},{12,8},{1,5},{5,1},{9,13},{13,9},{2,6},{6,2},{1... | collective-permute-start | bytes 786440 | tf_op jit(solution)/shard_map/ppermute | solution.py:602
  72.0 14.0 %copy-start.7 = (bf16[512,256]{1,0:T(8,128)(2,1)}, bf16[512,256]{1,0:T(8,128)(2,1)S(1)}, u32[]{:S(2)}) copy-start(bf16[512,256]{1,0:T(8,128)(2,1)S(1)} %collective-permute-done.19.one_ref.refs_3_) | copy-start | bytes 786436
  72.0 13.9 %collective-permute-start.20 = (bf16[512,256]{1,0:T(8,128)(2,1)S(1)}, bf16[512,256]{1,0:T(8,128)(2,1)S(1)}, u32[]{:S(2)}, u32[]{:S(2)}) collective-permute-start(bf16[512,256]{1,0:T(8,128)(2,1)S(1)} %shard_map.137), channel_id=1, source_target_pairs={{0,4},{4,0},{8,12},{12,8},{1,5},{5,1},{9,13},{13,9},{2,6},{6,2},{1... | collective-permute-start | bytes 786440 | tf_op jit(solution)/shard_map/ppermute | solution.py:604
  73.9 10.0 %collective-permute-start.15 = (bf16[256,256]{1,0:T(8,128)(2,1)S(1)}, bf16[256,256]{1,0:T(8,128)(2,1)S(1)}, u32[]{:S(2)}, u32[]{:S(2)}) collective-permute-start(bf16[256,256]{1,0:T(8,128)(2,1)S(1)} %get-tuple-element.54), channel_id=1, source_target_pairs={{0,8},{4,12},{8,0},{12,4},{1,9},{5,13},{9,1},{13,5},{2,10},{6,14},... | collective-permute-start | bytes 393224 | tf_op jit(solution)/shard_map/ppermute | solution.py:482
  83.9 2.0 %copy-start.10 = (bf16[256,256]{1,0:T(8,128)(2,1)}, bf16[256,256]{1,0:T(8,128)(2,1)S(1)}, u32[]{:S(2)}) copy-start(bf16[256,256]{1,0:T(8,128)(2,1)S(1)} %collective-permute-done.15.refs_2_.refs_5_) | copy-start | bytes 393220
  83.9 2.0 %copy-start.23 = (bf16[512,256]{1,0:T(8,128)(2,1)}, bf16[512,256]{1,0:T(8,128)(2,1)S(1)}, u32[]{:S(2)}) copy-start(bf16[512,256]{1,0:T(8,128)(2,1)S(1)} %collective-permute-done.18.refs_1_) | copy-start | bytes 786436
  85.9 0.7 copy-start.24
  85.9 5.3 %copy-start.17 = (bf16[256,256]{1,0:T(8,128)(2,1)S(1)}, bf16[256,256]{1,0:T(8,128)(2,1)}, u32[]{:S(2)}) copy-start(bf16[256,256]{1,0:T(8,128)(2,1)} %copy-done.16) | copy-start | bytes 393220
  89.7 21.4 %collective-permute-start.21 = (bf16[512,512]{1,0:T(8,128)(2,1)}, bf16[512,512]{1,0:T(8,128)(2,1)S(1)}, u32[]{:S(2)}, u32[]{:S(2)}) collective-permute-start(bf16[512,512]{1,0:T(8,128)(2,1)} %shard_map.138.one_ref), channel_id=1, source_target_pairs={{0,16},{16,0},{1,17},{17,1},{2,18},{18,2},{3,19},{19,3},{4,20},{20... | collective-permute-start | bytes 1572872 | tf_op jit(solution)/shard_map/ppermute | solution.py:638
  91.2 7.1 %collective-permute-start.16 = (bf16[256,256]{1,0:T(8,128)(2,1)S(1)}, bf16[256,256]{1,0:T(8,128)(2,1)S(1)}, u32[]{:S(2)}, u32[]{:S(2)}) collective-permute-start(bf16[256,256]{1,0:T(8,128)(2,1)S(1)} %copy-done.17), channel_id=1, source_target_pairs={{0,12},{4,8},{8,4},{12,0},{1,13},{5,9},{9,5},{13,1},{2,14},{6,10},... | collective-permute-start | bytes 393224 | tf_op jit(solution)/shard_map/ppermute | solution.py:482
  98.3 0.9 copy-start.11
  100.1 11.0 %copy-start.2 = (bf16[512,512]{1,0:T(8,128)(2,1)S(1)}, bf16[512,512]{1,0:T(8,128)(2,1)}, u32[]{:S(2)}) copy-start(bf16[512,512]{1,0:T(8,128)(2,1)} %shard_map.138.one_ref) | copy-start | bytes 1572868
  100.1 9.3 %collective-permute-start.17 = (bf16[256,512]{1,0:T(8,128)(2,1)S(1)}, bf16[256,512]{1,0:T(8,128)(2,1)S(1)}, u32[]{:S(2)}, u32[]{:S(2)}) collective-permute-start(bf16[256,512]{1,0:T(8,128)(2,1)S(1)} %get-tuple-element.58.one_ref), channel_id=1, source_target_pairs={{0,16},{16,0},{1,17},{17,1},{2,18},{18,2},{3,19},{19,3},{4,20},{20... | collective-permute-start | bytes 786440 | tf_op jit(solution)/shard_map/ppermute | solution.py:625
  102.0 8.4 %collective-permute-start.13 = (bf16[256,512]{1,0:T(8,128)(2,1)S(1)}, bf16[256,512]{1,0:T(8,128)(2,1)S(1)}, u32[]{:S(2)}, u32[]{:S(2)}) collective-permute-start(bf16[256,512]{1,0:T(8,128)(2,1)S(1)} %get-tuple-element.51), channel_id=1, source_target_pairs={{0,2},{1,3},{2,0},{3,1},{4,6},{5,7},{6,4},{7,5},{8,10},{9,11},{10,... | collective-permute-start | bytes 786440 | tf_op jit(solution)/shard_map/ppermute | solution.py:613
Sparse Core Ops, SparseCore 0:
  43.4 18.0 all-gather.2

commit v4 on v3

--- a/solution.py
+++ b/solution.py
@@ -196,7 +196,7 @@
 
 
 def each_chunk(lanes, body):
-    @pl.loop(0, LANES // ROWS, unroll=2)
+    @pl.loop(0, LANES // ROWS, unroll=4)
     def _(step):
         for lane in range(0, lanes, LANES):
             body(pl.multiple_of(step * ROWS, ROWS), lane)
@@ -419,10 +419,6 @@
     far_ref[...] = (keep_ref[y ^ 1] + other_ref[y ^ 1]).astype(BF16)
 
 
-def sum_kernel(mine_ref, other_ref, out_ref):
-    out_ref[...] = (mine_ref[...] + other_ref[...].astype(F32)).astype(BF16)
-
-
 def pass_kernel(one_ref, _, out_ref):
     out_ref[...] = one_ref[...]
 
@@ -441,10 +437,6 @@
     out_ref[...] = total.astype(BF16)
 
 
-def add_kernel(factor, one_ref, other_ref, out_ref):
-    out_ref[...] = (one_ref[...].astype(F32) + other_ref[...].astype(F32)) * factor
-
-
 def mixed_kernel(seqs, *refs):
     held, (key_ref, value_ref, grad_key_ref, grad_value_ref, taps_ref) = refs[:seqs], refs[seqs:]
     me = lax.axis_index("ctx")
@@ -456,8 +448,11 @@
         taps_ref[:, cols] = ref[:, pl.ds(LANES, LANES)]
 
 
-def taps_kernel(factor, one_ref, other_ref, out_ref):
-    out_ref[...] = (one_ref[...].astype(F32) + other_ref[...].astype(F32)).T * factor
+def closing_kernel(factor, mine_ref, far_ref, weight_ref, weight_other, taps_ref, taps_other, *outs):
+    output_ref, grad_wout_ref, grad_filter_ref = outs
+    output_ref[...] = (mine_ref[...] + far_ref[...].astype(F32)).astype(BF16)
+    grad_wout_ref[...] = (weight_ref[...].astype(F32) + weight_other[...].astype(F32)) * factor
+    grad_filter_ref[...] = (taps_ref[...].astype(F32) + taps_other[...].astype(F32)).T * factor
 
 
 def shape_of(shape, dtype):
@@ -498,7 +493,9 @@
     rows = (positions, channels)
     line = seqs * positions
 
-    cot_rows = exchange([cot] * parts, "tp")
+    over_chip, over_y = [[(j, j ^ r) for j in range(parts)] for r in (1, 2)]
+    cot_far = lax.ppermute(cot, "tp", over_y)
+    cot_rows = [cot, lax.ppermute(cot, "tp", over_chip), cot_far, lax.ppermute(cot_far, "tp", over_chip)]
 
     sent = call(
         prepare_kernel,
@@ -527,7 +524,7 @@
         *cot_rows,
         w_out,
         query,
-        held[1],
+        sent[1],
         scratch=[pltpu.VMEM((parts, positions, width), BF16)],
         left=(parts + 2,),
     )
@@ -611,7 +608,6 @@
         lax.ppermute(share_sent, "tp", [(j, j ^ 1) for j in range(parts)]),
     )
     far = lax.ppermute(far, "tp", [(j, j ^ 2) for j in range(parts)])
-    output = call(sum_kernel, shape_of((positions, width), BF16), 10**6, 2 * 10**6, mine, far)
 
     grad_key, grad_value, taps = call(
         functools.partial(mixed_kernel, seqs),
@@ -635,21 +631,15 @@
         room=60,
         scratch=[pltpu.VMEM((seqs, positions, width), BF16)],
     )
-    weight_other = lax.ppermute(weight_grad, "dp", ring)
-    grad_wout = call(
-        functools.partial(add_kernel, factor),
-        shape_of((channels, width), F32),
+    output, grad_wout, grad_filter = call(
+        functools.partial(closing_kernel, factor),
+        (shape_of((positions, width), BF16), shape_of((channels, width), F32), shape_of((channels, positions), F32)),
         10**6,
-        2 * 10**6,
+        5 * 10**6,
+        mine,
+        far,
         weight_grad,
-        weight_other,
-    )
-
-    grad_filter = call(
-        functools.partial(taps_kernel, factor),
-        shape_of((channels, positions), F32),
-        10**6,
-        10**6,
+        lax.ppermute(weight_grad, "dp", ring),
         taps,
         taps_other,
     )

time: 120 us -> 122 us (1.017)
  waiting for transfers between devices: 37.7 us -> 43.1 us
  Pallas kernels: 22.9 us -> 20 us
    ppermute x1 -> x4, waiting for transfers between devices: 0.01 us -> 6.52 us  [the longest x1 6.51 us: local_short(): cot_far = lax.ppermute(cot, 'tp', over_y)]
    ppermute x15 -> x12, starting transfers between devices: 22.9 us -> 18.7 us  [exchange(): lax.ppermute(pieces[r], axis, [(d, d ^ r) for d in range(size)])]
    ppermute x1 -> x4, starting transfers between devices: 1.49 us -> 4.53 us  [the longest x1 3.03 us: local_short(): cot_far = lax.ppermute(cot, 'tp', over_y)]
    pallas_call x13 -> x11, Pallas kernels: 22.9 us -> 20 us  [call(): pl.pallas_call(kernel, out_shape=outs, in_specs=[anywhere if n in left el...]
    ppermute x15 -> x12, waiting for transfers between devices: 29.9 us -> 28.2 us  [exchange(): lax.ppermute(pieces[r], axis, [(d, d ^ r) for d in range(size)])]
    ppermute x1, waiting for transfers between devices: 5.82 us -> 7.06 us  [local_short(): taps_other = lax.ppermute(taps, 'dp', ring)]
  transfers between devices with their start and end apart: 23 -> 23, of which waited for: 7 -> 7; matrix products, arithmetic and copies ran while one was open for 0% -> 0% of each run, Pallas kernels for 18% -> 15%
where the time goes in v4:
time: 122 us; the launch traced here: 121 us
  waiting for transfers between devices  43.1 us (35%)
  starting transfers between devices  31.5 us (26%)
  Pallas kernels  20 us (16%)
  between operations  14.2 us (12%)
  local copies, waits for them, and re-layouts  12.4 us (10%)
    ppermute x12, waiting for transfers between devices, exchange(): lax.ppermute(pieces[r], axis, [(d, d ^ r) for d in range(size)])  28.2 us
    pallas_call x11, Pallas kernels, call(): pl.pallas_call(kernel, out_shape=outs, in_specs=[anywhere if n in left el...  20 us
    ppermute x12, starting transfers between devices, exchange(): lax.ppermute(pieces[r], axis, [(d, d ^ r) for d in range(size)])  18.7 us
    unnamed x50, local copies, waits for them, and re-layouts  12.4 us
    ppermute x1, waiting for transfers between devices, local_short(): taps_other = lax.ppermute(taps, 'dp', ring)  7.06 us
    ppermute x1, waiting for transfers between devices, local_short(): cot_far = lax.ppermute(cot, 'tp', over_y)  6.51 us
    ppermute x1, starting transfers between devices, local_short(): cot_far = lax.ppermute(cot, 'tp', over_y)  3.03 us
    ppermute x1, starting transfers between devices, local_short(): across = lax.ppermute(turned, 'ctx', third)  2.5 us
  transfers between devices with their start and end apart: 23, of which 7 were waited for; matrix products, arithmetic and copies ran while one was open for 0% of the time, Pallas kernels for 15%

profile of v4, /device:TPU:0, one launch (start us, length us, event | category | flops | bytes accessed | tf_op | source)
XLA Modules:
  0.0 121.3 jit_solution(12952781974800506285)
XLA Ops:
  7.2 0.0 copy-start.20
  7.2 0.0 copy-start.21
  7.2 0.0 all-gather.3.cloned.1.call-start
  7.2 3.0 %collective-permute-start.4 = (bf16[256,512]{1,0:T(8,128)(2,1)}, bf16[256,512]{1,0:T(8,128)(2,1)S(1)}, u32[]{:S(2)}, u32[]{:S(2)}) collective-permute-start(bf16[256,512]{1,0:T(8,128)(2,1)} %bitcast.15), channel_id=1, source_target_pairs={{0,2},{1,3},{2,0},{3,1},{4,6},{5,7},{6,4},{7,5},{8,10},{9,11},{10,... | collective-permute-start | bytes 786440 | tf_op jit(solution)/shard_map/ppermute | solution.py:497
  10.3 0.0 collective-permute-start.3
  10.3 6.5 %collective-permute-done.4.refs_2_ = bf16[256,512]{1,0:T(8,128)(2,1)S(1)} collective-permute-done((bf16[256,512]{1,0:T(8,128)(2,1)}, bf16[256,512]{1,0:T(8,128)(2,1)S(1)}, u32[]{:S(2)}, u32[]{:S(2)}) %collective-permute-start.4) | collective-permute-done | bytes 262176 | tf_op jit(solution)/shard_map/ppermute | solution.py:497
  16.8 2.1 %shard_map.127 = (bf16[256,256]{1,0:T(8,128)(2,1)}, bf16[256,256]{1,0:T(8,128)(2,1)}, bf16[256,256]{1,0:T(8,128)(2,1)}, bf16[256,256]{1,0:T(8,128)(2,1)}) custom-call(bf16[256,512]{1,0:T(8,128)(2,1)} %bitcast.11, bf16[256,512]{1,0:T(8,128)(2,1)} %bitcast.13, f32[512,256]{1,0:T(8,128)} %refs_2_.1), custom_call_target="tpu_custom_call" | custom-call | flops 1000000 | bytes 2000000 | tf_op jit(solution)/shard_map/pallas_call | solution.py:464
  18.9 1.9 %collective-permute-start = (bf16[256,256]{1,0:T(8,128)(2,1)}, bf16[256,256]{1,0:T(8,128)(2,1)S(1)}, u32[]{:S(2)}, u32[]{:S(2)}) collective-permute-start(bf16[256,256]{1,0:T(8,128)(2,1)} %get-tuple-element.37.refs_6_), channel_id=1, source_target_pairs={{0,4},{4,0},{8,12},{12,8},{1,5},{5,1},{9,13},{13,9},{2,6},{6,2},{1... | collective-permute-start | bytes 393224 | tf_op jit(solution)/shard_map/ppermute | solution.py:477
  20.8 2.6 %collective-permute-start.1 = (bf16[256,256]{1,0:T(8,128)(2,1)}, bf16[256,256]{1,0:T(8,128)(2,1)S(1)}, u32[]{:S(2)}, u32[]{:S(2)}) collective-permute-start(bf16[256,256]{1,0:T(8,128)(2,1)} %get-tuple-element.38), channel_id=1, source_target_pairs={{0,8},{4,12},{8,0},{12,4},{1,9},{5,13},{9,1},{13,5},{2,10},{6,14},... | collective-permute-start | bytes 393224 | tf_op jit(solution)/shard_map/ppermute | solution.py:477
  23.4 0.0 collective-permute-start.2
  23.4 0.0 collective-permute-done.5.refs_3_
  23.4 0.0 copy-start
  23.4 1.6 %copy-done = bf16[512,2048]{1,0:T(8,128)(2,1)S(1)} copy-done((bf16[512,2048]{1,0:T(8,128)(2,1)S(1)}, bf16[512,2048]{1,0:T(8,128)(2,1)}, u32[]{:S(2)}) %copy-start) | copy-done | bytes 2097176
  25.0 0.9 copy-done.3
  25.9 0.9 copy-done.12
  26.9 0.9 copy-done.14
  27.8 0.9 shard_map.128
  28.7 0.0 copy-start.8
  28.7 0.8 copy-done.8
  29.5 0.9 collective-permute-start.9
  30.4 3.5 %collective-permute-start.10 = (bf16[256,256]{1,0:T(8,128)(2,1)S(1)}, bf16[256,256]{1,0:T(8,128)(2,1)S(1)}, u32[]{:S(2)}, u32[]{:S(2)}) collective-permute-start(bf16[256,256]{1,0:T(8,128)(2,1)S(1)} %get-tuple-element.47), channel_id=1, source_target_pairs={{0,8},{4,12},{8,0},{12,4},{1,9},{5,13},{9,1},{13,5},{2,10},{6,14},... | collective-permute-start | bytes 393224 | tf_op jit(solution)/shard_map/ppermute | solution.py:477
  33.9 0.0 collective-permute-done.1.refs_2_
  33.9 0.0 collective-permute-done.2.refs_3_
  33.9 4.4 %shard_map.129 = (bf16[256,128]{1,0:T(8,128)(2,1)S(1)}, bf16[256,128]{1,0:T(8,128)(2,1)S(1)}, bf16[256,128]{1,0:T(8,128)(2,1)S(1)}, bf16[256,128]{1,0:T(8,128)(2,1)S(1)}, f32[9,256,256]{2,1,0:T(8,128)S(1)}) custom-call(bf16[256,256]{1,0:T(8,128)(2,1)S(1)} %copy-done.19, bf16[256,256]{1,0:T(8,128)(2,1)S(1)} %collective-permute-done.refs_1_, ...), custom_call_target="tpu_custom_call" | custom-call | flops 1000000000 | bytes 9000000 | tf_op jit(solution)/shard_map/pallas_call | solution.py:464
  38.4 0.0 copy-start.15
  38.4 0.6 copy-done.15
  39.0 1.4 %copy-done.22 = f32[9,256,256]{2,1,0:T(8,128)} copy-done((f32[9,256,256]{2,1,0:T(8,128)}, f32[9,256,256]{2,1,0:T(8,128)S(1)}, u32[]{:S(2)}) %copy-start.22) | copy-done | bytes 2359320
  40.4 4.7 %collective-permute-done.10.refs_2_ = bf16[256,256]{1,0:T(8,128)(2,1)S(1)} collective-permute-done((bf16[256,256]{1,0:T(8,128)(2,1)S(1)}, bf16[256,256]{1,0:T(8,128)(2,1)S(1)}, u32[]{:S(2)}, u32[]{:S(2)}) %collective-permute-start.10) | collective-permute-done | bytes 131104 | tf_op jit(solution)/shard_map/ppermute | solution.py:477
  45.1 0.8 shard_map.130.refs_8_
  45.9 0.0 all-gather.3.cloned.1.call-update
  45.9 3.5 %collective-permute-start.6 = (bf16[256,128]{1,0:T(8,128)(2,1)S(1)}, bf16[256,128]{1,0:T(8,128)(2,1)S(1)}, u32[]{:S(2)}, u32[]{:S(2)}) collective-permute-start(bf16[256,128]{1,0:T(8,128)(2,1)S(1)} %get-tuple-element.42.refs_4_.refs_7_), channel_id=1, source_target_pairs={{0,4},{4,0},{8,12},{12,8},{1,5},{5,1},{9,13},{13,9},{2,6},{6,2},{1... | collective-permute-start | bytes 196616 | tf_op jit(solution)/shard_map/ppermute | solution.py:477
  49.5 1.9 %collective-permute-start.7 = (bf16[256,128]{1,0:T(8,128)(2,1)S(1)}, bf16[256,128]{1,0:T(8,128)(2,1)S(1)}, u32[]{:S(2)}, u32[]{:S(2)}) collective-permute-start(bf16[256,128]{1,0:T(8,128)(2,1)S(1)} %get-tuple-element.43), channel_id=1, source_target_pairs={{0,8},{4,12},{8,0},{12,4},{1,9},{5,13},{9,1},{13,5},{2,10},{6,14},... | collective-permute-start | bytes 196616 | tf_op jit(solution)/shard_map/ppermute | solution.py:477
  51.4 1.4 %collective-permute-start.8 = (bf16[256,128]{1,0:T(8,128)(2,1)S(1)}, bf16[256,128]{1,0:T(8,128)(2,1)S(1)}, u32[]{:S(2)}, u32[]{:S(2)}) collective-permute-start(bf16[256,128]{1,0:T(8,128)(2,1)S(1)} %get-tuple-element.44), channel_id=1, source_target_pairs={{0,12},{4,8},{8,4},{12,0},{1,13},{5,9},{9,5},{13,1},{2,14},{6,10},... | collective-permute-start | bytes 196616 | tf_op jit(solution)/shard_map/ppermute | solution.py:477
  52.7 1.7 %copy-done.23 = f32[9,256,256]{2,1,0:T(8,128)S(1)} copy-done((f32[9,256,256]{2,1,0:T(8,128)S(1)}, f32[9,256,256]{2,1,0:T(8,128)}, u32[]{:S(2)}) %copy-start.23) | copy-done | bytes 2359320
  54.4 4.3 %shard_map.131 = (bf16[256,256]{1,0:T(8,128)(2,1)S(1)}, bf16[256,256]{1,0:T(8,128)(2,1)S(1)}, bf16[256,256]{1,0:T(8,128)(2,1)S(1)}, bf16[256,256]{1,0:T(8,128)(2,1)S(1)}) custom-call(bf16[256,256]{1,0:T(8,128)(2,1)S(1)} %get-tuple-element.46.refs_0_, bf16[256,256]{1,0:T(8,128)(2,1)S(1)} %collective-permute-done.9.refs_1_, ...), custom_call_target="tpu_custom_call" | custom-call | flops 1000000000 | bytes 9000000 | tf_op jit(solution)/shard_map/pallas_call | solution.py:464
  58.7 0.0 collective-permute-done.7.refs_2_
  58.7 0.0 collective-permute-done.8.refs_3_
  58.8 0.0 copy-start.9
  58.8 1.0 copy-done.9
  59.8 0.8 copy-done.16
  60.7 1.7 %shard_map.132 = (bf16[512,256]{1,0:T(8,128)(2,1)S(1)}, bf16[256,512]{1,0:T(8,128)(2,1)}, f32[2,256,512]{2,1,0:T(8,128)S(1)}, f32[2,256,512]{2,1,0:T(8,128)}) custom-call(bf16[256,128]{1,0:T(8,128)(2,1)S(1)} %copy-done.16, bf16[256,128]{1,0:T(8,128)(2,1)S(1)} %collective-permute-done.6.refs_1_, bf16[256,128]{1,0:T(8,128)(2,1)S(1)} %collective-permute-done.7.refs_2_, ...), custom_call_target="tpu_custom_call" | custom-call | flops 536870912 | bytes 5000000 | tf_op jit(solution)/shard_map/pallas_call | solution.py:464
  62.4 0.0 collective-permute-start.12
  62.4 2.5 %collective-permute-start.15 = (bf16[512,256]{1,0:T(8,128)(2,1)S(1)}, bf16[512,256]{1,0:T(8,128)(2,1)S(1)}, u32[]{:S(2)}, u32[]{:S(2)}) collective-permute-start(bf16[512,256]{1,0:T(8,128)(2,1)S(1)} %get-tuple-element.55.refs_0_), channel_id=1, source_target_pairs={{0,12},{4,8},{8,4},{12,0},{1,13},{5,9},{9,5},{13,1},{2,14},{6,10},... | collective-permute-start | bytes 786440 | tf_op jit(solution)/shard_map/ppermute | solution.py:598
  64.9 0.2 collective-permute-start.16
  65.1 1.9 %collective-permute-start.14 = (bf16[512,256]{1,0:T(8,128)(2,1)S(1)}, bf16[512,256]{1,0:T(8,128)(2,1)S(1)}, u32[]{:S(2)}, u32[]{:S(2)}) collective-permute-start(bf16[512,256]{1,0:T(8,128)(2,1)S(1)} %get-tuple-element.55.refs_0_), channel_id=1, source_target_pairs={{0,4},{4,0},{8,12},{12,8},{1,5},{5,1},{9,13},{13,9},{2,6},{6,2},{1... | collective-permute-start | bytes 786440 | tf_op jit(solution)/shard_map/ppermute | solution.py:599
  66.9 9.0 %collective-permute-done.16._.refs_1_ = bf16[256,256]{1,0:T(8,128)(2,1)S(1)} collective-permute-done((bf16[256,256]{1,0:T(8,128)(2,1)S(1)}, bf16[256,256]{1,0:T(8,128)(2,1)S(1)}, u32[]{:S(2)}, u32[]{:S(2)}) %collective-permute-start.16) | collective-permute-done | bytes 131104 | tf_op jit(solution)/shard_map/ppermute | solution.py:477
  75.9 0.0 collective-permute-done.15.one_ref.refs_3_
  75.9 1.7 %collective-permute-start.17 = (bf16[512,256]{1,0:T(8,128)(2,1)S(1)}, bf16[512,256]{1,0:T(8,128)(2,1)}, u32[]{:S(2)}, u32[]{:S(2)}) collective-permute-start(bf16[512,256]{1,0:T(8,128)(2,1)S(1)} %shard_map.134), channel_id=1, source_target_pairs={{0,4},{4,0},{8,12},{12,8},{1,5},{5,1},{9,13},{13,9},{2,6},{6,2},{1... | collective-permute-start | bytes 786440 | tf_op jit(solution)/shard_map/ppermute | solution.py:601
  77.7 1.3 %collective-permute-start.18 = (bf16[256,256]{1,0:T(8,128)(2,1)S(1)}, bf16[256,256]{1,0:T(8,128)(2,1)S(1)}, u32[]{:S(2)}, u32[]{:S(2)}) collective-permute-start(bf16[256,256]{1,0:T(8,128)(2,1)S(1)} %get-tuple-element.56), channel_id=1, source_target_pairs={{0,8},{4,12},{8,0},{12,4},{1,9},{5,13},{9,1},{13,5},{2,10},{6,14},... | collective-permute-start | bytes 393224 | tf_op jit(solution)/shard_map/ppermute | solution.py:477
  78.9 9.0 %collective-permute-done.18.refs_5_.refs_2_ = bf16[256,256]{1,0:T(8,128)(2,1)S(1)} collective-permute-done((bf16[256,256]{1,0:T(8,128)(2,1)S(1)}, bf16[256,256]{1,0:T(8,128)(2,1)S(1)}, u32[]{:S(2)}, u32[]{:S(2)}) %collective-permute-start.18) | collective-permute-done | bytes 131104 | tf_op jit(solution)/shard_map/ppermute | solution.py:477
  88.0 0.0 copy-start.24
  88.0 0.7 copy-done.24
  88.7 1.3 %collective-permute-done.17.refs_2_ = bf16[512,256]{1,0:T(8,128)(2,1)} collective-permute-done((bf16[512,256]{1,0:T(8,128)(2,1)S(1)}, bf16[512,256]{1,0:T(8,128)(2,1)}, u32[]{:S(2)}, u32[]{:S(2)}) %collective-permute-start.17) | collective-permute-done | bytes 262176 | tf_op jit(solution)/shard_map/ppermute | solution.py:601
  90.0 3.1 %shard_map.135.weight_ref = bf16[512,512]{1,0:T(8,128)(2,1)} custom-call(bf16[512,256]{1,0:T(8,128)(2,1)} %copy-done.13, bf16[512,256]{1,0:T(8,128)(2,1)} %copy-done.24, bf16[512,256]{1,0:T(8,128)(2,1)} %collective-permute-done.17.refs_2_, bf16[512,256]{1,0:T(8,128)(2,1)} %copy-done.7, bf16[4,256,512]{2,1,0:T(8,128)(2,1)} %bitcast.18, ...), custom_call_target="tpu_custom_call" | custom-call | flops 536870912 | bytes 3000000 | tf_op jit(solution)/shard_map/pallas_call | solution.py:464
  93.1 1.5 %collective-permute-start.19 = (bf16[512,512]{1,0:T(8,128)(2,1)}, bf16[512,512]{1,0:T(8,128)(2,1)S(1)}, u32[]{:S(2)}, u32[]{:S(2)}) collective-permute-start(bf16[512,512]{1,0:T(8,128)(2,1)} %shard_map.135.weight_ref), channel_id=1, source_target_pairs={{0,16},{16,0},{1,17},{17,1},{2,18},{18,2},{3,19},{19,3},{4,20},{20... | collective-permute-start | bytes 1572872 | tf_op jit(solution)/shard_map/ppermute | solution.py:642
  94.6 1.6 %collective-permute-start.20 = (bf16[256,256]{1,0:T(8,128)(2,1)S(1)}, bf16[256,256]{1,0:T(8,128)(2,1)S(1)}, u32[]{:S(2)}, u32[]{:S(2)}) collective-permute-start(bf16[256,256]{1,0:T(8,128)(2,1)S(1)} %copy-done.18), channel_id=1, source_target_pairs={{0,12},{4,8},{8,4},{12,0},{1,13},{5,9},{9,5},{13,1},{2,14},{6,10},... | collective-permute-start | bytes 393224 | tf_op jit(solution)/shard_map/ppermute | solution.py:477
  96.2 5.4 %collective-permute-done.20.refs_3_ = bf16[256,256]{1,0:T(8,128)(2,1)S(1)} collective-permute-done((bf16[256,256]{1,0:T(8,128)(2,1)S(1)}, bf16[256,256]{1,0:T(8,128)(2,1)S(1)}, u32[]{:S(2)}, u32[]{:S(2)}) %collective-permute-start.20) | collective-permute-done | bytes 131104 | tf_op jit(solution)/shard_map/ppermute | solution.py:477
  101.6 0.9 copy-done.11
  102.5 0.9 shard_map.136
  103.5 0.5 collective-permute-start.21
  104.0 0.1 shard_map.133
  104.1 1.6 %collective-permute-start.13 = (bf16[256,512]{1,0:T(8,128)(2,1)S(1)}, bf16[256,512]{1,0:T(8,128)(2,1)S(1)}, u32[]{:S(2)}, u32[]{:S(2)}) collective-permute-start(bf16[256,512]{1,0:T(8,128)(2,1)S(1)} %get-tuple-element.54), channel_id=1, source_target_pairs={{0,2},{1,3},{2,0},{3,1},{4,6},{5,7},{6,4},{7,5},{8,10},{9,11},{10,... | collective-permute-start | bytes 786440 | tf_op jit(solution)/shard_map/ppermute | solution.py:610
  105.7 7.1 %collective-permute-done.21.taps_other = bf16[256,512]{1,0:T(8,128)(2,1)S(1)} collective-permute-done((bf16[256,512]{1,0:T(8,128)(2,1)S(1)}, bf16[256,512]{1,0:T(8,128)(2,1)S(1)}, u32[]{:S(2)}, u32[]{:S(2)}) %collective-permute-start.21) | collective-permute-done | bytes 262176 | tf_op jit(solution)/shard_map/ppermute | solution.py:621
  112.8 1.7 %shard_map.137 = (bf16[256,512]{1,0:T(8,128)(2,1)}, f32[512,512]{1,0:T(8,128)}, f32[512,256]{1,0:T(8,128)}) custom-call(f32[256,512]{1,0:T(8,128)S(1)} %get-tuple-element.53.mine_ref, bf16[256,512]{1,0:T(8,128)(2,1)S(1)} %collective-permute-done.13.far_ref, bf16[512,512]{1,0:T(8,128)(2,1)S(1)} %copy-done.2, ...), custom_call_target="tpu_custom_call" | custom-call | flops 1000000 | bytes 5000000 | tf_op jit(solution)/shard_map/pallas_call | solution.py:464
  (44 shorter events, 0.1 us)
Async XLA Ops:
  7.2 26.7 %copy-start.20 = (bf16[2,256,256]{2,1,0:T(8,128)(2,1)S(1)}, bf16[2,256,256]{2,1,0:T(8,128)(2,1)}, u32[]{:S(2)}) copy-start(bf16[2,256,256]{2,1,0:T(8,128)(2,1)} %constant.4.clone.refs_4_.refs_5_) | copy-start | bytes 786436
  7.2 26.7 %copy-start.21 = (f32[128,128]{1,0:T(8,128)S(1)}, f32[128,128]{1,0:T(8,128)}, u32[]{:S(2)}) copy-start(f32[128,128]{1,0:T(8,128)} %constant.5.clone.refs_5_.refs_6_) | copy-start | bytes 196612
  7.2 82.8 %all-gather.3.cloned.1.call-start = ((), (), s32[]{:S(2)}) async-start(), calls=%async_computation | async-start | bytes 1310720 | tf_op jit(solution)/shard_map/all_gather | solution.py:562
  7.2 9.6 %collective-permute-start.4 = (bf16[256,512]{1,0:T(8,128)(2,1)}, bf16[256,512]{1,0:T(8,128)(2,1)S(1)}, u32[]{:S(2)}, u32[]{:S(2)}) collective-permute-start(bf16[256,512]{1,0:T(8,128)(2,1)} %bitcast.15), channel_id=1, source_target_pairs={{0,2},{1,3},{2,0},{3,1},{4,6},{5,7},{6,4},{7,5},{8,10},{9,11},{10,... | collective-permute-start | bytes 786440 | tf_op jit(solution)/shard_map/ppermute | solution.py:497
  10.3 13.1 %collective-permute-start.3 = (bf16[256,512]{1,0:T(8,128)(2,1)}, bf16[256,512]{1,0:T(8,128)(2,1)S(1)}, u32[]{:S(2)}, u32[]{:S(2)}) collective-permute-start(bf16[256,512]{1,0:T(8,128)(2,1)} %bitcast.16), channel_id=1, source_target_pairs={{0,1},{1,0},{2,3},{3,2},{4,5},{5,4},{6,7},{7,6},{8,9},{9,8},{10,11... | collective-permute-start | bytes 786440 | tf_op jit(solution)/shard_map/ppermute | solution.py:498
  16.8 6.6 %collective-permute-start.5 = (bf16[256,512]{1,0:T(8,128)(2,1)S(1)}, bf16[256,512]{1,0:T(8,128)(2,1)S(1)}, u32[]{:S(2)}, u32[]{:S(2)}) collective-permute-start(bf16[256,512]{1,0:T(8,128)(2,1)S(1)} %collective-permute-done.4.refs_2_), channel_id=1, source_target_pairs={{0,1},{1,0},{2,3},{3,2},{4,5},{5,4},{6,7},{7,6},{8,9},{9,8},{10,11... | collective-permute-start | bytes 786440 | tf_op jit(solution)/shard_map/ppermute | solution.py:498
  18.9 14.9 %collective-permute-start = (bf16[256,256]{1,0:T(8,128)(2,1)}, bf16[256,256]{1,0:T(8,128)(2,1)S(1)}, u32[]{:S(2)}, u32[]{:S(2)}) collective-permute-start(bf16[256,256]{1,0:T(8,128)(2,1)} %get-tuple-element.37.refs_6_), channel_id=1, source_target_pairs={{0,4},{4,0},{8,12},{12,8},{1,5},{5,1},{9,13},{13,9},{2,6},{6,2},{1... | collective-permute-start | bytes 393224 | tf_op jit(solution)/shard_map/ppermute | solution.py:477
  20.8 13.1 %collective-permute-start.1 = (bf16[256,256]{1,0:T(8,128)(2,1)}, bf16[256,256]{1,0:T(8,128)(2,1)S(1)}, u32[]{:S(2)}, u32[]{:S(2)}) collective-permute-start(bf16[256,256]{1,0:T(8,128)(2,1)} %get-tuple-element.38), channel_id=1, source_target_pairs={{0,8},{4,12},{8,0},{12,4},{1,9},{5,13},{9,1},{13,5},{2,10},{6,14},... | collective-permute-start | bytes 393224 | tf_op jit(solution)/shard_map/ppermute | solution.py:477
  23.4 10.5 %collective-permute-start.2 = (bf16[256,256]{1,0:T(8,128)(2,1)}, bf16[256,256]{1,0:T(8,128)(2,1)S(1)}, u32[]{:S(2)}, u32[]{:S(2)}) collective-permute-start(bf16[256,256]{1,0:T(8,128)(2,1)} %get-tuple-element.39), channel_id=1, source_target_pairs={{0,12},{4,8},{8,4},{12,0},{1,13},{5,9},{9,5},{13,1},{2,14},{6,10},... | collective-permute-start | bytes 393224 | tf_op jit(solution)/shard_map/ppermute | solution.py:477
  23.4 1.6 %copy-start = (bf16[512,2048]{1,0:T(8,128)(2,1)S(1)}, bf16[512,2048]{1,0:T(8,128)(2,1)}, u32[]{:S(2)}) copy-start(bf16[512,2048]{1,0:T(8,128)(2,1)} %refs_6_.2) | copy-start | bytes 6291460
  25.0 0.9 copy-start.3
  25.9 0.9 copy-start.12
  26.9 0.9 copy-start.14
  27.8 6.1 %copy-start.19 = (bf16[256,256]{1,0:T(8,128)(2,1)S(1)}, bf16[256,256]{1,0:T(8,128)(2,1)}, u32[]{:S(2)}) copy-start(bf16[256,256]{1,0:T(8,128)(2,1)} %get-tuple-element.36.refs_0_) | copy-start | bytes 393220
  28.7 0.8 copy-start.8
  29.5 10.9 %collective-permute-start.9 = (bf16[256,256]{1,0:T(8,128)(2,1)S(1)}, bf16[256,256]{1,0:T(8,128)(2,1)S(1)}, u32[]{:S(2)}, u32[]{:S(2)}) collective-permute-start(bf16[256,256]{1,0:T(8,128)(2,1)S(1)} %get-tuple-element.40.refs_6_), channel_id=1, source_target_pairs={{0,4},{4,0},{8,12},{12,8},{1,5},{5,1},{9,13},{13,9},{2,6},{6,2},{1... | collective-permute-start | bytes 393224 | tf_op jit(solution)/shard_map/ppermute | solution.py:477
  30.4 14.8 %collective-permute-start.10 = (bf16[256,256]{1,0:T(8,128)(2,1)S(1)}, bf16[256,256]{1,0:T(8,128)(2,1)S(1)}, u32[]{:S(2)}, u32[]{:S(2)}) collective-permute-start(bf16[256,256]{1,0:T(8,128)(2,1)S(1)} %get-tuple-element.47), channel_id=1, source_target_pairs={{0,8},{4,12},{8,0},{12,4},{1,9},{5,13},{9,1},{13,5},{2,10},{6,14},... | collective-permute-start | bytes 393224 | tf_op jit(solution)/shard_map/ppermute | solution.py:477
  33.9 11.3 %collective-permute-start.11 = (bf16[256,256]{1,0:T(8,128)(2,1)S(1)}, bf16[256,256]{1,0:T(8,128)(2,1)S(1)}, u32[]{:S(2)}, u32[]{:S(2)}) collective-permute-start(bf16[256,256]{1,0:T(8,128)(2,1)S(1)} %get-tuple-element.48), channel_id=1, source_target_pairs={{0,12},{4,8},{8,4},{12,0},{1,13},{5,9},{9,5},{13,1},{2,14},{6,10},... | collective-permute-start | bytes 393224 | tf_op jit(solution)/shard_map/ppermute | solution.py:477
  38.4 0.6 copy-start.15
  39.0 1.4 %copy-start.22 = (f32[9,256,256]{2,1,0:T(8,128)}, f32[9,256,256]{2,1,0:T(8,128)S(1)}, u32[]{:S(2)}) copy-start(f32[9,256,256]{2,1,0:T(8,128)S(1)} %get-tuple-element.49.refs_4_) | copy-start | bytes 7077892
  45.1 13.6 %copy-start.1 = (bf16[512,2048]{1,0:T(8,128)(2,1)S(1)}, bf16[512,2048]{1,0:T(8,128)(2,1)}, u32[]{:S(2)}) copy-start(bf16[512,2048]{1,0:T(8,128)(2,1)} %refs_6_.2) | copy-start | bytes 6291460
  45.1 13.6 %copy-start.4 = (bf16[1,256,512]{2,1,0:T(8,128)(2,1)S(1)}, bf16[1,256,512]{2,1,0:T(8,128)(2,1)}, u32[]{:S(2)}) copy-start(bf16[1,256,512]{2,1,0:T(8,128)(2,1)} %param.8) | copy-start | bytes 786436
  45.9 12.8 %collective-permute-start.6 = (bf16[256,128]{1,0:T(8,128)(2,1)S(1)}, bf16[256,128]{1,0:T(8,128)(2,1)S(1)}, u32[]{:S(2)}, u32[]{:S(2)}) collective-permute-start(bf16[256,128]{1,0:T(8,128)(2,1)S(1)} %get-tuple-element.42.refs_4_.refs_7_), channel_id=1, source_target_pairs={{0,4},{4,0},{8,12},{12,8},{1,5},{5,1},{9,13},{13,9},{2,6},{6,2},{1... | collective-permute-start | bytes 196616 | tf_op jit(solution)/shard_map/ppermute | solution.py:477
  49.5 9.3 %collective-permute-start.7 = (bf16[256,128]{1,0:T(8,128)(2,1)S(1)}, bf16[256,128]{1,0:T(8,128)(2,1)S(1)}, u32[]{:S(2)}, u32[]{:S(2)}) collective-permute-start(bf16[256,128]{1,0:T(8,128)(2,1)S(1)} %get-tuple-element.43), channel_id=1, source_target_pairs={{0,8},{4,12},{8,0},{12,4},{1,9},{5,13},{9,1},{13,5},{2,10},{6,14},... | collective-permute-start | bytes 196616 | tf_op jit(solution)/shard_map/ppermute | solution.py:477
  51.4 7.4 %collective-permute-start.8 = (bf16[256,128]{1,0:T(8,128)(2,1)S(1)}, bf16[256,128]{1,0:T(8,128)(2,1)S(1)}, u32[]{:S(2)}, u32[]{:S(2)}) collective-permute-start(bf16[256,128]{1,0:T(8,128)(2,1)S(1)} %get-tuple-element.44), channel_id=1, source_target_pairs={{0,12},{4,8},{8,4},{12,0},{1,13},{5,9},{9,5},{13,1},{2,14},{6,10},... | collective-permute-start | bytes 196616 | tf_op jit(solution)/shard_map/ppermute | solution.py:477
  52.7 1.7 %copy-start.23 = (f32[9,256,256]{2,1,0:T(8,128)S(1)}, f32[9,256,256]{2,1,0:T(8,128)}, u32[]{:S(2)}) copy-start(f32[9,256,256]{2,1,0:T(8,128)} %copy-done.22) | copy-start | bytes 7077892
  58.7 29.3 %copy-start.17 = (bf16[256,256]{1,0:T(8,128)(2,1)}, bf16[256,256]{1,0:T(8,128)(2,1)S(1)}, u32[]{:S(2)}) copy-start(bf16[256,256]{1,0:T(8,128)(2,1)S(1)} %get-tuple-element.58) | copy-start | bytes 393220
  58.8 1.0 copy-start.9
  59.8 0.8 copy-start.16
  62.4 25.6 %copy-start.13 = (bf16[512,256]{1,0:T(8,128)(2,1)}, bf16[512,256]{1,0:T(8,128)(2,1)S(1)}, u32[]{:S(2)}) copy-start(bf16[512,256]{1,0:T(8,128)(2,1)S(1)} %get-tuple-element.55.refs_0_) | copy-start | bytes 786436
  62.4 39.2 %copy-start.5 = (bf16[1,256,512]{2,1,0:T(8,128)(2,1)S(1)}, bf16[1,256,512]{2,1,0:T(8,128)(2,1)}, u32[]{:S(2)}) copy-start(bf16[1,256,512]{2,1,0:T(8,128)(2,1)} %param.9) | copy-start | bytes 786436
  62.4 39.2 %copy-start.6 = (bf16[1,256,512]{2,1,0:T(8,128)(2,1)S(1)}, bf16[1,256,512]{2,1,0:T(8,128)(2,1)}, u32[]{:S(2)}) copy-start(bf16[1,256,512]{2,1,0:T(8,128)(2,1)} %param.10) | copy-start | bytes 786436
  62.4 41.6 %collective-permute-start.12 = (f32[2,256,512]{2,1,0:T(8,128)}, f32[2,256,512]{2,1,0:T(8,128)S(1)}, u32[]{:S(2)}, u32[]{:S(2)}) collective-permute-start(f32[2,256,512]{2,1,0:T(8,128)} %get-tuple-element.52), channel_id=1, source_target_pairs={{0,1},{1,0},{2,3},{3,2},{4,5},{5,4},{6,7},{7,6},{8,9},{9,8},{10,11... | collective-permute-start | bytes 3145736 | tf_op jit(solution)/shard_map/ppermute | solution.py:608
  62.4 13.5 %collective-permute-start.15 = (bf16[512,256]{1,0:T(8,128)(2,1)S(1)}, bf16[512,256]{1,0:T(8,128)(2,1)S(1)}, u32[]{:S(2)}, u32[]{:S(2)}) collective-permute-start(bf16[512,256]{1,0:T(8,128)(2,1)S(1)} %get-tuple-element.55.refs_0_), channel_id=1, source_target_pairs={{0,12},{4,8},{8,4},{12,0},{1,13},{5,9},{9,5},{13,1},{2,14},{6,10},... | collective-permute-start | bytes 786440 | tf_op jit(solution)/shard_map/ppermute | solution.py:598
  64.9 11.0 %collective-permute-start.16 = (bf16[256,256]{1,0:T(8,128)(2,1)S(1)}, bf16[256,256]{1,0:T(8,128)(2,1)S(1)}, u32[]{:S(2)}, u32[]{:S(2)}) collective-permute-start(bf16[256,256]{1,0:T(8,128)(2,1)S(1)} %get-tuple-element.50.refs_7_), channel_id=1, source_target_pairs={{0,4},{4,0},{8,12},{12,8},{1,5},{5,1},{9,13},{13,9},{2,6},{6,2},{1... | collective-permute-start | bytes 393224 | tf_op jit(solution)/shard_map/ppermute | solution.py:477
  65.1 22.9 %collective-permute-start.14 = (bf16[512,256]{1,0:T(8,128)(2,1)S(1)}, bf16[512,256]{1,0:T(8,128)(2,1)S(1)}, u32[]{:S(2)}, u32[]{:S(2)}) collective-permute-start(bf16[512,256]{1,0:T(8,128)(2,1)S(1)} %get-tuple-element.55.refs_0_), channel_id=1, source_target_pairs={{0,4},{4,0},{8,12},{12,8},{1,5},{5,1},{9,13},{13,9},{2,6},{6,2},{1... | collective-permute-start | bytes 786440 | tf_op jit(solution)/shard_map/ppermute | solution.py:599
  75.9 14.1 %copy-start.7 = (bf16[512,256]{1,0:T(8,128)(2,1)}, bf16[512,256]{1,0:T(8,128)(2,1)S(1)}, u32[]{:S(2)}) copy-start(bf16[512,256]{1,0:T(8,128)(2,1)S(1)} %collective-permute-done.15.one_ref.refs_3_) | copy-start | bytes 786436
  75.9 14.1 %collective-permute-start.17 = (bf16[512,256]{1,0:T(8,128)(2,1)S(1)}, bf16[512,256]{1,0:T(8,128)(2,1)}, u32[]{:S(2)}, u32[]{:S(2)}) collective-permute-start(bf16[512,256]{1,0:T(8,128)(2,1)S(1)} %shard_map.134), channel_id=1, source_target_pairs={{0,4},{4,0},{8,12},{12,8},{1,5},{5,1},{9,13},{13,9},{2,6},{6,2},{1... | collective-permute-start | bytes 786440 | tf_op jit(solution)/shard_map/ppermute | solution.py:601
  77.7 10.3 %collective-permute-start.18 = (bf16[256,256]{1,0:T(8,128)(2,1)S(1)}, bf16[256,256]{1,0:T(8,128)(2,1)S(1)}, u32[]{:S(2)}, u32[]{:S(2)}) collective-permute-start(bf16[256,256]{1,0:T(8,128)(2,1)S(1)} %get-tuple-element.56), channel_id=1, source_target_pairs={{0,8},{4,12},{8,0},{12,4},{1,9},{5,13},{9,1},{13,5},{2,10},{6,14},... | collective-permute-start | bytes 393224 | tf_op jit(solution)/shard_map/ppermute | solution.py:477
  88.0 2.0 %copy-start.10 = (bf16[256,256]{1,0:T(8,128)(2,1)}, bf16[256,256]{1,0:T(8,128)(2,1)S(1)}, u32[]{:S(2)}) copy-start(bf16[256,256]{1,0:T(8,128)(2,1)S(1)} %collective-permute-done.18.refs_5_.refs_2_) | copy-start | bytes 393220
  88.0 0.7 copy-start.24
  90.0 4.6 %copy-start.18 = (bf16[256,256]{1,0:T(8,128)(2,1)S(1)}, bf16[256,256]{1,0:T(8,128)(2,1)}, u32[]{:S(2)}) copy-start(bf16[256,256]{1,0:T(8,128)(2,1)} %copy-done.17) | copy-start | bytes 393220
  93.1 19.7 %copy-start.2 = (bf16[512,512]{1,0:T(8,128)(2,1)S(1)}, bf16[512,512]{1,0:T(8,128)(2,1)}, u32[]{:S(2)}) copy-start(bf16[512,512]{1,0:T(8,128)(2,1)} %shard_map.135.weight_ref) | copy-start | bytes 1572868
  93.1 19.7 %collective-permute-start.19 = (bf16[512,512]{1,0:T(8,128)(2,1)}, bf16[512,512]{1,0:T(8,128)(2,1)S(1)}, u32[]{:S(2)}, u32[]{:S(2)}) collective-permute-start(bf16[512,512]{1,0:T(8,128)(2,1)} %shard_map.135.weight_ref), channel_id=1, source_target_pairs={{0,16},{16,0},{1,17},{17,1},{2,18},{18,2},{3,19},{19,3},{4,20},{20... | collective-permute-start | bytes 1572872 | tf_op jit(solution)/shard_map/ppermute | solution.py:642
  94.6 7.1 %collective-permute-start.20 = (bf16[256,256]{1,0:T(8,128)(2,1)S(1)}, bf16[256,256]{1,0:T(8,128)(2,1)S(1)}, u32[]{:S(2)}, u32[]{:S(2)}) collective-permute-start(bf16[256,256]{1,0:T(8,128)(2,1)S(1)} %copy-done.18), channel_id=1, source_target_pairs={{0,12},{4,8},{8,4},{12,0},{1,13},{5,9},{9,5},{13,1},{2,14},{6,10},... | collective-permute-start | bytes 393224 | tf_op jit(solution)/shard_map/ppermute | solution.py:477
  101.6 0.9 copy-start.11
  103.5 9.3 %collective-permute-start.21 = (bf16[256,512]{1,0:T(8,128)(2,1)S(1)}, bf16[256,512]{1,0:T(8,128)(2,1)S(1)}, u32[]{:S(2)}, u32[]{:S(2)}) collective-permute-start(bf16[256,512]{1,0:T(8,128)(2,1)S(1)} %get-tuple-element.59.taps_ref), channel_id=1, source_target_pairs={{0,16},{16,0},{1,17},{17,1},{2,18},{18,2},{3,19},{19,3},{4,20},{20... | collective-permute-start | bytes 786440 | tf_op jit(solution)/shard_map/ppermute | solution.py:621
  104.1 8.7 %collective-permute-start.13 = (bf16[256,512]{1,0:T(8,128)(2,1)S(1)}, bf16[256,512]{1,0:T(8,128)(2,1)S(1)}, u32[]{:S(2)}, u32[]{:S(2)}) collective-permute-start(bf16[256,512]{1,0:T(8,128)(2,1)S(1)} %get-tuple-element.54), channel_id=1, source_target_pairs={{0,2},{1,3},{2,0},{3,1},{4,6},{5,7},{6,4},{7,5},{8,10},{9,11},{10,... | collective-permute-start | bytes 786440 | tf_op jit(solution)/shard_map/ppermute | solution.py:610
Sparse Core Ops, SparseCore 0:
  46.0 19.6 all-gather.2

commit v5 on v4

--- a/solution.py
+++ b/solution.py
@@ -494,8 +494,7 @@
     line = seqs * positions
 
     over_chip, over_y = [[(j, j ^ r) for j in range(parts)] for r in (1, 2)]
-    cot_far = lax.ppermute(cot, "tp", over_y)
-    cot_rows = [cot, lax.ppermute(cot, "tp", over_chip), cot_far, lax.ppermute(cot_far, "tp", over_chip)]
+    cot_core, cot_far = lax.ppermute(cot, "tp", over_chip), lax.ppermute(cot, "tp", over_y)
 
     sent = call(
         prepare_kernel,
@@ -515,6 +514,8 @@
         room=60,
     )
     held = exchange(sent, "ctx")
+    far_passed = call(pass_kernel, shape_of(rows, BF16), 10**6, 10**6, cot_far, sent[1], left=(1,))
+    cot_rows = [cot, cot_core, cot_far, lax.ppermute(far_passed, "tp", over_chip)]
 
     gated_grad, *conv_grad = call(
         functools.partial(gradient_kernel, parts),

time: 122 us -> 120 us (0.984)
  waiting for transfers between devices: 43.1 us -> 41.2 us
  Pallas kernels: 20 us -> 21.3 us
    ppermute x2, waiting for transfers between devices: 6.52 us -> 4.34 us  [the longest x1 4.33 us: local_short(): lax.ppermute(cot, 'tp', over_y)]
    ppermute x1, waiting for transfers between devices: 7.06 us -> 5.84 us  [local_short(): taps_other = lax.ppermute(taps, 'dp', ring)]
    pallas_call x11 -> x12, Pallas kernels: 20 us -> 21.3 us  [call(): pl.pallas_call(kernel, out_shape=outs, in_specs=[anywhere if n in left el...]
  transfers between devices with their start and end apart: 23 -> 23, of which waited for: 7 -> 8; matrix products, arithmetic and copies ran while one was open for 0% -> 0% of each run, Pallas kernels for 15% -> 16%
where the time goes in v5:
time: 120 us
  waiting for transfers between devices  41.2 us (34%)
  starting transfers between devices  31.6 us (26%)
  Pallas kernels  21.3 us (18%)
  between operations  14.3 us (12%)
  local copies, waits for them, and re-layouts  11.5 us (10%)
    ppermute x12, waiting for transfers between devices, exchange(): lax.ppermute(pieces[r], axis, [(d, d ^ r) for d in range(size)])  29.1 us
    pallas_call x12, Pallas kernels, call(): pl.pallas_call(kernel, out_shape=outs, in_specs=[anywhere if n in left el...  21.3 us
    ppermute x12, starting transfers between devices, exchange(): lax.ppermute(pieces[r], axis, [(d, d ^ r) for d in range(size)])  18.5 us
    unnamed x50, local copies, waits for them, and re-layouts  11.5 us
    ppermute x1, waiting for transfers between devices, local_short(): taps_other = lax.ppermute(taps, 'dp', ring)  5.84 us
    ppermute x1, waiting for transfers between devices, local_short(): lax.ppermute(cot, 'tp', over_y)  4.33 us
    ppermute x1, starting transfers between devices, local_short(): lax.ppermute(cot, 'tp', over_y)  3.03 us
    ppermute x1, starting transfers between devices, local_short(): across = lax.ppermute(turned, 'ctx', third)  2.5 us
  transfers between devices with their start and end apart: 23, of which 8 were waited for; matrix products, arithmetic and copies ran while one was open for 0% of the time, Pallas kernels for 16%

profile of v5, /device:TPU:0, one launch (start us, length us, event | category | flops | bytes accessed | tf_op | source)
XLA Modules:
  0.0 119.8 jit_solution(16235517009579912501)
XLA Ops:
  7.2 0.0 all-gather.3.cloned.1.call-start
  7.2 3.0 %collective-permute-start.4 = (bf16[256,512]{1,0:T(8,128)(2,1)}, bf16[256,512]{1,0:T(8,128)(2,1)S(1)}, u32[]{:S(2)}, u32[]{:S(2)}) collective-permute-start(bf16[256,512]{1,0:T(8,128)(2,1)} %bitcast.15), channel_id=1, source_target_pairs={{0,2},{1,3},{2,0},{3,1},{4,6},{5,7},{6,4},{7,5},{8,10},{9,11},{10,... | collective-permute-start | bytes 786440 | tf_op jit(solution)/shard_map/ppermute | solution.py:497
  10.2 2.1 %shard_map.127 = (bf16[256,256]{1,0:T(8,128)(2,1)}, bf16[256,256]{1,0:T(8,128)(2,1)}, bf16[256,256]{1,0:T(8,128)(2,1)}, bf16[256,256]{1,0:T(8,128)(2,1)}) custom-call(bf16[256,512]{1,0:T(8,128)(2,1)} %bitcast.11, bf16[256,512]{1,0:T(8,128)(2,1)} %bitcast.13, f32[512,256]{1,0:T(8,128)} %refs_2_.1), custom_call_target="tpu_custom_call" | custom-call | flops 1000000 | bytes 2000000 | tf_op jit(solution)/shard_map/pallas_call | solution.py:464
  12.4 0.0 copy-start.18
  12.4 0.0 copy-start.19
  12.4 0.0 copy-start.20
  12.4 4.3 %collective-permute-done.4.one_ref.refs_2_ = bf16[256,512]{1,0:T(8,128)(2,1)S(1)} collective-permute-done((bf16[256,512]{1,0:T(8,128)(2,1)}, bf16[256,512]{1,0:T(8,128)(2,1)S(1)}, u32[]{:S(2)}, u32[]{:S(2)}) %collective-permute-start.4) | collective-permute-done | bytes 262176 | tf_op jit(solution)/shard_map/ppermute | solution.py:497
  16.8 0.1 collective-permute-start.5
  16.9 1.9 %collective-permute-start = (bf16[256,256]{1,0:T(8,128)(2,1)}, bf16[256,256]{1,0:T(8,128)(2,1)S(1)}, u32[]{:S(2)}, u32[]{:S(2)}) collective-permute-start(bf16[256,256]{1,0:T(8,128)(2,1)} %get-tuple-element.37._.refs_6_), channel_id=1, source_target_pairs={{0,4},{4,0},{8,12},{12,8},{1,5},{5,1},{9,13},{13,9},{2,6},{6,2},{1... | collective-permute-start | bytes 393224 | tf_op jit(solution)/shard_map/ppermute | solution.py:477
  18.7 2.6 %collective-permute-start.1 = (bf16[256,256]{1,0:T(8,128)(2,1)}, bf16[256,256]{1,0:T(8,128)(2,1)S(1)}, u32[]{:S(2)}, u32[]{:S(2)}) collective-permute-start(bf16[256,256]{1,0:T(8,128)(2,1)} %get-tuple-element.38), channel_id=1, source_target_pairs={{0,8},{4,12},{8,0},{12,4},{1,9},{5,13},{9,1},{13,5},{2,10},{6,14},... | collective-permute-start | bytes 393224 | tf_op jit(solution)/shard_map/ppermute | solution.py:477
  21.3 0.0 collective-permute-start.2
  21.3 0.0 collective-permute-done.3.refs_1_
  21.3 0.0 collective-permute-done.5.refs_3_
  21.3 0.0 copy-start
  21.3 1.6 %copy-done = bf16[512,2048]{1,0:T(8,128)(2,1)S(1)} copy-done((bf16[512,2048]{1,0:T(8,128)(2,1)S(1)}, bf16[512,2048]{1,0:T(8,128)(2,1)}, u32[]{:S(2)}) %copy-start) | copy-done | bytes 2097176
  22.9 0.9 copy-done.3
  23.9 0.9 copy-done.12
  24.8 0.9 shard_map.129
  25.7 0.0 copy-start.8
  25.7 0.8 copy-done.8
  26.5 0.9 collective-permute-start.9
  27.4 3.5 %collective-permute-start.10 = (bf16[256,256]{1,0:T(8,128)(2,1)S(1)}, bf16[256,256]{1,0:T(8,128)(2,1)S(1)}, u32[]{:S(2)}, u32[]{:S(2)}) collective-permute-start(bf16[256,256]{1,0:T(8,128)(2,1)S(1)} %get-tuple-element.47), channel_id=1, source_target_pairs={{0,8},{4,12},{8,0},{12,4},{1,9},{5,13},{9,1},{13,5},{2,10},{6,14},... | collective-permute-start | bytes 393224 | tf_op jit(solution)/shard_map/ppermute | solution.py:477
  30.9 0.0 collective-permute-done.refs_1_
  30.9 0.0 collective-permute-start.11
  30.9 1.0 collective-permute-done.1.refs_2_
  31.9 0.0 collective-permute-done.2.refs_3_
  31.9 4.4 %shard_map.130 = (bf16[256,128]{1,0:T(8,128)(2,1)S(1)}, bf16[256,128]{1,0:T(8,128)(2,1)S(1)}, bf16[256,128]{1,0:T(8,128)(2,1)S(1)}, bf16[256,128]{1,0:T(8,128)(2,1)S(1)}, f32[9,256,256]{2,1,0:T(8,128)S(1)}) custom-call(bf16[256,256]{1,0:T(8,128)(2,1)S(1)} %copy-done.18, bf16[256,256]{1,0:T(8,128)(2,1)S(1)} %collective-permute-done.refs_1_, ...), custom_call_target="tpu_custom_call" | custom-call | flops 1000000000 | bytes 9000000 | tf_op jit(solution)/shard_map/pallas_call | solution.py:464
  36.3 0.0 copy-start.14
  36.4 0.6 copy-done.14
  37.0 1.4 %copy-done.21 = f32[9,256,256]{2,1,0:T(8,128)} copy-done((f32[9,256,256]{2,1,0:T(8,128)}, f32[9,256,256]{2,1,0:T(8,128)S(1)}, u32[]{:S(2)}) %copy-start.21) | copy-done | bytes 2359320
  38.4 0.0 collective-permute-done.9.refs_1_
  38.4 4.7 %collective-permute-done.10.refs_2_ = bf16[256,256]{1,0:T(8,128)(2,1)S(1)} collective-permute-done((bf16[256,256]{1,0:T(8,128)(2,1)S(1)}, bf16[256,256]{1,0:T(8,128)(2,1)S(1)}, u32[]{:S(2)}, u32[]{:S(2)}) %collective-permute-start.10) | collective-permute-done | bytes 131104 | tf_op jit(solution)/shard_map/ppermute | solution.py:477
  43.1 0.8 shard_map.131.refs_8_
  43.9 0.0 all-gather.3.cloned.1.call-update
  43.9 4.3 %collective-permute-start.6 = (bf16[256,128]{1,0:T(8,128)(2,1)S(1)}, bf16[256,128]{1,0:T(8,128)(2,1)S(1)}, u32[]{:S(2)}, u32[]{:S(2)}) collective-permute-start(bf16[256,128]{1,0:T(8,128)(2,1)S(1)} %get-tuple-element.42.refs_4_.refs_7_), channel_id=1, source_target_pairs={{0,4},{4,0},{8,12},{12,8},{1,5},{5,1},{9,13},{13,9},{2,6},{6,2},{1... | collective-permute-start | bytes 196616 | tf_op jit(solution)/shard_map/ppermute | solution.py:477
  48.2 1.1 collective-permute-start.7
  49.3 1.4 %collective-permute-start.8 = (bf16[256,128]{1,0:T(8,128)(2,1)S(1)}, bf16[256,128]{1,0:T(8,128)(2,1)S(1)}, u32[]{:S(2)}, u32[]{:S(2)}) collective-permute-start(bf16[256,128]{1,0:T(8,128)(2,1)S(1)} %get-tuple-element.44), channel_id=1, source_target_pairs={{0,12},{4,8},{8,4},{12,0},{1,13},{5,9},{9,5},{13,1},{2,14},{6,10},... | collective-permute-start | bytes 196616 | tf_op jit(solution)/shard_map/ppermute | solution.py:477
  50.7 1.7 %copy-done.22 = f32[9,256,256]{2,1,0:T(8,128)S(1)} copy-done((f32[9,256,256]{2,1,0:T(8,128)S(1)}, f32[9,256,256]{2,1,0:T(8,128)}, u32[]{:S(2)}) %copy-start.22) | copy-done | bytes 2359320
  52.3 4.3 %shard_map.132 = (bf16[256,256]{1,0:T(8,128)(2,1)S(1)}, bf16[256,256]{1,0:T(8,128)(2,1)S(1)}, bf16[256,256]{1,0:T(8,128)(2,1)S(1)}, bf16[256,256]{1,0:T(8,128)(2,1)S(1)}) custom-call(bf16[256,256]{1,0:T(8,128)(2,1)S(1)} %get-tuple-element.46.refs_0_, bf16[256,256]{1,0:T(8,128)(2,1)S(1)} %collective-permute-done.9.refs_1_, ...), custom_call_target="tpu_custom_call" | custom-call | flops 1000000000 | bytes 9000000 | tf_op jit(solution)/shard_map/pallas_call | solution.py:464
  56.7 0.0 copy-start.9
  56.7 1.0 copy-done.9
  57.8 0.8 copy-done.15
  58.6 1.7 %shard_map.133 = (bf16[512,256]{1,0:T(8,128)(2,1)S(1)}, bf16[256,512]{1,0:T(8,128)(2,1)}, f32[2,256,512]{2,1,0:T(8,128)S(1)}, f32[2,256,512]{2,1,0:T(8,128)}) custom-call(bf16[256,128]{1,0:T(8,128)(2,1)S(1)} %copy-done.15, bf16[256,128]{1,0:T(8,128)(2,1)S(1)} %collective-permute-done.6.refs_1_, bf16[256,128]{1,0:T(8,128)(2,1)S(1)} %collective-permute-done.7.refs_2_, ...), custom_call_target="tpu_custom_call" | custom-call | flops 536870912 | bytes 5000000 | tf_op jit(solution)/shard_map/pallas_call | solution.py:464
  60.4 2.5 %collective-permute-start.15 = (bf16[512,256]{1,0:T(8,128)(2,1)S(1)}, bf16[512,256]{1,0:T(8,128)(2,1)S(1)}, u32[]{:S(2)}, u32[]{:S(2)}) collective-permute-start(bf16[512,256]{1,0:T(8,128)(2,1)S(1)} %get-tuple-element.55.refs_0_), channel_id=1, source_target_pairs={{0,12},{4,8},{8,4},{12,0},{1,13},{5,9},{9,5},{13,1},{2,14},{6,10},... | collective-permute-start | bytes 786440 | tf_op jit(solution)/shard_map/ppermute | solution.py:599
  62.9 0.2 collective-permute-start.16
  63.0 1.9 %collective-permute-start.14 = (bf16[512,256]{1,0:T(8,128)(2,1)S(1)}, bf16[512,256]{1,0:T(8,128)(2,1)S(1)}, u32[]{:S(2)}, u32[]{:S(2)}) collective-permute-start(bf16[512,256]{1,0:T(8,128)(2,1)S(1)} %get-tuple-element.55.refs_0_), channel_id=1, source_target_pairs={{0,4},{4,0},{8,12},{12,8},{1,5},{5,1},{9,13},{13,9},{2,6},{6,2},{1... | collective-permute-start | bytes 786440 | tf_op jit(solution)/shard_map/ppermute | solution.py:600
  64.9 9.0 %collective-permute-done.16._.refs_1_ = bf16[256,256]{1,0:T(8,128)(2,1)S(1)} collective-permute-done((bf16[256,256]{1,0:T(8,128)(2,1)S(1)}, bf16[256,256]{1,0:T(8,128)(2,1)S(1)}, u32[]{:S(2)}, u32[]{:S(2)}) %collective-permute-start.16) | collective-permute-done | bytes 131104 | tf_op jit(solution)/shard_map/ppermute | solution.py:477
  73.9 2.0 %collective-permute-start.17 = (bf16[512,256]{1,0:T(8,128)(2,1)S(1)}, bf16[512,256]{1,0:T(8,128)(2,1)S(1)}, u32[]{:S(2)}, u32[]{:S(2)}) collective-permute-start(bf16[512,256]{1,0:T(8,128)(2,1)S(1)} %shard_map.135), channel_id=1, source_target_pairs={{0,4},{4,0},{8,12},{12,8},{1,5},{5,1},{9,13},{13,9},{2,6},{6,2},{1... | collective-permute-start | bytes 786440 | tf_op jit(solution)/shard_map/ppermute | solution.py:602
  75.8 1.1 collective-permute-start.18
  76.9 9.0 %collective-permute-done.18.refs_5_.refs_2_ = bf16[256,256]{1,0:T(8,128)(2,1)S(1)} collective-permute-done((bf16[256,256]{1,0:T(8,128)(2,1)S(1)}, bf16[256,256]{1,0:T(8,128)(2,1)S(1)}, u32[]{:S(2)}, u32[]{:S(2)}) %collective-permute-start.18) | collective-permute-done | bytes 131104 | tf_op jit(solution)/shard_map/ppermute | solution.py:477
  85.9 0.0 copy-start.23
  85.9 1.9 %collective-permute-done.17.refs_2_ = bf16[512,256]{1,0:T(8,128)(2,1)S(1)} collective-permute-done((bf16[512,256]{1,0:T(8,128)(2,1)S(1)}, bf16[512,256]{1,0:T(8,128)(2,1)S(1)}, u32[]{:S(2)}, u32[]{:S(2)}) %collective-permute-start.17) | collective-permute-done | bytes 262176 | tf_op jit(solution)/shard_map/ppermute | solution.py:602
  87.9 0.7 copy-done.24
  88.5 3.1 %shard_map.136.weight_ref = bf16[512,512]{1,0:T(8,128)(2,1)} custom-call(bf16[512,256]{1,0:T(8,128)(2,1)} %copy-done.13, bf16[512,256]{1,0:T(8,128)(2,1)} %copy-done.23, bf16[512,256]{1,0:T(8,128)(2,1)} %copy-done.24, bf16[512,256]{1,0:T(8,128)(2,1)} %copy-done.7, bf16[4,256,512]{2,1,0:T(8,128)(2,1)} %bitcast.18, bf16[256,256]{1,0:T(8,128)(2,1)} %copy-done.10), custom_call_target="tpu_custom_call" | custom-call | flops 536870912 | bytes 3000000 | tf_op jit(solution)/shard_map/pallas_call | solution.py:464
  91.6 1.5 %collective-permute-start.19 = (bf16[512,512]{1,0:T(8,128)(2,1)}, bf16[512,512]{1,0:T(8,128)(2,1)S(1)}, u32[]{:S(2)}, u32[]{:S(2)}) collective-permute-start(bf16[512,512]{1,0:T(8,128)(2,1)} %shard_map.136.weight_ref), channel_id=1, source_target_pairs={{0,16},{16,0},{1,17},{17,1},{2,18},{18,2},{3,19},{19,3},{4,20},{20... | collective-permute-start | bytes 1572872 | tf_op jit(solution)/shard_map/ppermute | solution.py:643
  93.1 1.6 %collective-permute-start.20 = (bf16[256,256]{1,0:T(8,128)(2,1)S(1)}, bf16[256,256]{1,0:T(8,128)(2,1)S(1)}, u32[]{:S(2)}, u32[]{:S(2)}) collective-permute-start(bf16[256,256]{1,0:T(8,128)(2,1)S(1)} %copy-done.17), channel_id=1, source_target_pairs={{0,12},{4,8},{8,4},{12,0},{1,13},{5,9},{9,5},{13,1},{2,14},{6,10},... | collective-permute-start | bytes 393224 | tf_op jit(solution)/shard_map/ppermute | solution.py:477
  94.7 5.4 %collective-permute-done.20.refs_3_ = bf16[256,256]{1,0:T(8,128)(2,1)S(1)} collective-permute-done((bf16[256,256]{1,0:T(8,128)(2,1)S(1)}, bf16[256,256]{1,0:T(8,128)(2,1)S(1)}, u32[]{:S(2)}, u32[]{:S(2)}) %collective-permute-start.20) | collective-permute-done | bytes 131104 | tf_op jit(solution)/shard_map/ppermute | solution.py:477
  100.1 0.9 copy-done.11
  101.0 0.9 shard_map.137
  102.0 0.5 collective-permute-start.21
  102.5 1.3 %shard_map.134 = (f32[256,512]{1,0:T(8,128)S(1)}, bf16[256,512]{1,0:T(8,128)(2,1)S(1)}) custom-call(f32[2,256,512]{2,1,0:T(8,128)S(1)} %get-tuple-element.51.keep_ref, f32[2,256,512]{2,1,0:T(8,128)} %collective-permute-done.12.other_ref), custom_call_target="tpu_custom_call" | custom-call | flops 1000000 | bytes 3000000 | tf_op jit(solution)/shard_map/pallas_call | solution.py:464
  103.8 1.6 %collective-permute-start.13 = (bf16[256,512]{1,0:T(8,128)(2,1)S(1)}, bf16[256,512]{1,0:T(8,128)(2,1)S(1)}, u32[]{:S(2)}, u32[]{:S(2)}) collective-permute-start(bf16[256,512]{1,0:T(8,128)(2,1)S(1)} %get-tuple-element.54), channel_id=1, source_target_pairs={{0,2},{1,3},{2,0},{3,1},{4,6},{5,7},{6,4},{7,5},{8,10},{9,11},{10,... | collective-permute-start | bytes 786440 | tf_op jit(solution)/shard_map/ppermute | solution.py:611
  105.4 5.8 %collective-permute-done.21.taps_other = bf16[256,512]{1,0:T(8,128)(2,1)S(1)} collective-permute-done((bf16[256,512]{1,0:T(8,128)(2,1)S(1)}, bf16[256,512]{1,0:T(8,128)(2,1)S(1)}, u32[]{:S(2)}, u32[]{:S(2)}) %collective-permute-start.21) | collective-permute-done | bytes 262176 | tf_op jit(solution)/shard_map/ppermute | solution.py:622
  111.3 1.7 %shard_map.138 = (bf16[256,512]{1,0:T(8,128)(2,1)}, f32[512,512]{1,0:T(8,128)}, f32[512,256]{1,0:T(8,128)}) custom-call(f32[256,512]{1,0:T(8,128)S(1)} %get-tuple-element.53.mine_ref, bf16[256,512]{1,0:T(8,128)(2,1)S(1)} %collective-permute-done.13.far_ref, bf16[512,512]{1,0:T(8,128)(2,1)S(1)} %copy-done.2, ...), custom_call_target="tpu_custom_call" | custom-call | flops 1000000 | bytes 5000000 | tf_op jit(solution)/shard_map/pallas_call | solution.py:464
  (45 shorter events, 0.1 us)
Async XLA Ops:
  7.2 80.7 %all-gather.3.cloned.1.call-start = ((), (), s32[]{:S(2)}) async-start(), calls=%async_computation | async-start | bytes 1310720 | tf_op jit(solution)/shard_map/all_gather | solution.py:563
  7.2 9.6 %collective-permute-start.4 = (bf16[256,512]{1,0:T(8,128)(2,1)}, bf16[256,512]{1,0:T(8,128)(2,1)S(1)}, u32[]{:S(2)}, u32[]{:S(2)}) collective-permute-start(bf16[256,512]{1,0:T(8,128)(2,1)} %bitcast.15), channel_id=1, source_target_pairs={{0,2},{1,3},{2,0},{3,1},{4,6},{5,7},{6,4},{7,5},{8,10},{9,11},{10,... | collective-permute-start | bytes 786440 | tf_op jit(solution)/shard_map/ppermute | solution.py:497
  10.2 11.1 %collective-permute-start.3 = (bf16[256,512]{1,0:T(8,128)(2,1)}, bf16[256,512]{1,0:T(8,128)(2,1)S(1)}, u32[]{:S(2)}, u32[]{:S(2)}) collective-permute-start(bf16[256,512]{1,0:T(8,128)(2,1)} %bitcast.16), channel_id=1, source_target_pairs={{0,1},{1,0},{2,3},{3,2},{4,5},{5,4},{6,7},{7,6},{8,9},{9,8},{10,11... | collective-permute-start | bytes 786440 | tf_op jit(solution)/shard_map/ppermute | solution.py:497
  12.4 19.5 %copy-start.18 = (bf16[256,256]{1,0:T(8,128)(2,1)S(1)}, bf16[256,256]{1,0:T(8,128)(2,1)}, u32[]{:S(2)}) copy-start(bf16[256,256]{1,0:T(8,128)(2,1)} %get-tuple-element.36.refs_0_) | copy-start | bytes 393220
  12.4 19.5 %copy-start.19 = (bf16[2,256,256]{2,1,0:T(8,128)(2,1)S(1)}, bf16[2,256,256]{2,1,0:T(8,128)(2,1)}, u32[]{:S(2)}) copy-start(bf16[2,256,256]{2,1,0:T(8,128)(2,1)} %constant.4.clone.refs_4_.refs_5_) | copy-start | bytes 786436
  12.4 19.5 %copy-start.20 = (f32[128,128]{1,0:T(8,128)S(1)}, f32[128,128]{1,0:T(8,128)}, u32[]{:S(2)}) copy-start(f32[128,128]{1,0:T(8,128)} %constant.5.clone.refs_5_.refs_6_) | copy-start | bytes 196612
  16.8 4.5 %collective-permute-start.5 = (bf16[256,512]{1,0:T(8,128)(2,1)S(1)}, bf16[256,512]{1,0:T(8,128)(2,1)S(1)}, u32[]{:S(2)}, u32[]{:S(2)}) collective-permute-start(bf16[256,512]{1,0:T(8,128)(2,1)S(1)} %shard_map.128), channel_id=1, source_target_pairs={{0,1},{1,0},{2,3},{3,2},{4,5},{5,4},{6,7},{7,6},{8,9},{9,8},{10,11... | collective-permute-start | bytes 786440 | tf_op jit(solution)/shard_map/ppermute | solution.py:518
  16.9 14.0 %collective-permute-start = (bf16[256,256]{1,0:T(8,128)(2,1)}, bf16[256,256]{1,0:T(8,128)(2,1)S(1)}, u32[]{:S(2)}, u32[]{:S(2)}) collective-permute-start(bf16[256,256]{1,0:T(8,128)(2,1)} %get-tuple-element.37._.refs_6_), channel_id=1, source_target_pairs={{0,4},{4,0},{8,12},{12,8},{1,5},{5,1},{9,13},{13,9},{2,6},{6,2},{1... | collective-permute-start | bytes 393224 | tf_op jit(solution)/shard_map/ppermute | solution.py:477
  18.7 13.2 %collective-permute-start.1 = (bf16[256,256]{1,0:T(8,128)(2,1)}, bf16[256,256]{1,0:T(8,128)(2,1)S(1)}, u32[]{:S(2)}, u32[]{:S(2)}) collective-permute-start(bf16[256,256]{1,0:T(8,128)(2,1)} %get-tuple-element.38), channel_id=1, source_target_pairs={{0,8},{4,12},{8,0},{12,4},{1,9},{5,13},{9,1},{13,5},{2,10},{6,14},... | collective-permute-start | bytes 393224 | tf_op jit(solution)/shard_map/ppermute | solution.py:477
  21.3 10.6 %collective-permute-start.2 = (bf16[256,256]{1,0:T(8,128)(2,1)}, bf16[256,256]{1,0:T(8,128)(2,1)S(1)}, u32[]{:S(2)}, u32[]{:S(2)}) collective-permute-start(bf16[256,256]{1,0:T(8,128)(2,1)} %get-tuple-element.39), channel_id=1, source_target_pairs={{0,12},{4,8},{8,4},{12,0},{1,13},{5,9},{9,5},{13,1},{2,14},{6,10},... | collective-permute-start | bytes 393224 | tf_op jit(solution)/shard_map/ppermute | solution.py:477
  21.3 1.6 %copy-start = (bf16[512,2048]{1,0:T(8,128)(2,1)S(1)}, bf16[512,2048]{1,0:T(8,128)(2,1)}, u32[]{:S(2)}) copy-start(bf16[512,2048]{1,0:T(8,128)(2,1)} %refs_6_.2) | copy-start | bytes 6291460
  22.9 0.9 copy-start.3
  23.9 0.9 copy-start.12
  25.7 0.8 copy-start.8
  26.5 11.9 %collective-permute-start.9 = (bf16[256,256]{1,0:T(8,128)(2,1)S(1)}, bf16[256,256]{1,0:T(8,128)(2,1)S(1)}, u32[]{:S(2)}, u32[]{:S(2)}) collective-permute-start(bf16[256,256]{1,0:T(8,128)(2,1)S(1)} %get-tuple-element.40.refs_6_), channel_id=1, source_target_pairs={{0,4},{4,0},{8,12},{12,8},{1,5},{5,1},{9,13},{13,9},{2,6},{6,2},{1... | collective-permute-start | bytes 393224 | tf_op jit(solution)/shard_map/ppermute | solution.py:477
  27.4 15.7 %collective-permute-start.10 = (bf16[256,256]{1,0:T(8,128)(2,1)S(1)}, bf16[256,256]{1,0:T(8,128)(2,1)S(1)}, u32[]{:S(2)}, u32[]{:S(2)}) collective-permute-start(bf16[256,256]{1,0:T(8,128)(2,1)S(1)} %get-tuple-element.47), channel_id=1, source_target_pairs={{0,8},{4,12},{8,0},{12,4},{1,9},{5,13},{9,1},{13,5},{2,10},{6,14},... | collective-permute-start | bytes 393224 | tf_op jit(solution)/shard_map/ppermute | solution.py:477
  30.9 12.2 %collective-permute-start.11 = (bf16[256,256]{1,0:T(8,128)(2,1)S(1)}, bf16[256,256]{1,0:T(8,128)(2,1)S(1)}, u32[]{:S(2)}, u32[]{:S(2)}) collective-permute-start(bf16[256,256]{1,0:T(8,128)(2,1)S(1)} %get-tuple-element.48), channel_id=1, source_target_pairs={{0,12},{4,8},{8,4},{12,0},{1,13},{5,9},{9,5},{13,1},{2,14},{6,10},... | collective-permute-start | bytes 393224 | tf_op jit(solution)/shard_map/ppermute | solution.py:477
  36.3 0.6 copy-start.14
  37.0 1.4 %copy-start.21 = (f32[9,256,256]{2,1,0:T(8,128)}, f32[9,256,256]{2,1,0:T(8,128)S(1)}, u32[]{:S(2)}) copy-start(f32[9,256,256]{2,1,0:T(8,128)S(1)} %get-tuple-element.49.refs_4_) | copy-start | bytes 7077892
  43.1 13.6 %copy-start.1 = (bf16[512,2048]{1,0:T(8,128)(2,1)S(1)}, bf16[512,2048]{1,0:T(8,128)(2,1)}, u32[]{:S(2)}) copy-start(bf16[512,2048]{1,0:T(8,128)(2,1)} %refs_6_.2) | copy-start | bytes 6291460
  43.1 13.6 %copy-start.4 = (bf16[1,256,512]{2,1,0:T(8,128)(2,1)S(1)}, bf16[1,256,512]{2,1,0:T(8,128)(2,1)}, u32[]{:S(2)}) copy-start(bf16[1,256,512]{2,1,0:T(8,128)(2,1)} %param.8) | copy-start | bytes 786436
  43.9 12.8 %collective-permute-start.6 = (bf16[256,128]{1,0:T(8,128)(2,1)S(1)}, bf16[256,128]{1,0:T(8,128)(2,1)S(1)}, u32[]{:S(2)}, u32[]{:S(2)}) collective-permute-start(bf16[256,128]{1,0:T(8,128)(2,1)S(1)} %get-tuple-element.42.refs_4_.refs_7_), channel_id=1, source_target_pairs={{0,4},{4,0},{8,12},{12,8},{1,5},{5,1},{9,13},{13,9},{2,6},{6,2},{1... | collective-permute-start | bytes 196616 | tf_op jit(solution)/shard_map/ppermute | solution.py:477
  48.2 8.4 %collective-permute-start.7 = (bf16[256,128]{1,0:T(8,128)(2,1)S(1)}, bf16[256,128]{1,0:T(8,128)(2,1)S(1)}, u32[]{:S(2)}, u32[]{:S(2)}) collective-permute-start(bf16[256,128]{1,0:T(8,128)(2,1)S(1)} %get-tuple-element.43), channel_id=1, source_target_pairs={{0,8},{4,12},{8,0},{12,4},{1,9},{5,13},{9,1},{13,5},{2,10},{6,14},... | collective-permute-start | bytes 196616 | tf_op jit(solution)/shard_map/ppermute | solution.py:477
  49.3 7.4 %collective-permute-start.8 = (bf16[256,128]{1,0:T(8,128)(2,1)S(1)}, bf16[256,128]{1,0:T(8,128)(2,1)S(1)}, u32[]{:S(2)}, u32[]{:S(2)}) collective-permute-start(bf16[256,128]{1,0:T(8,128)(2,1)S(1)} %get-tuple-element.44), channel_id=1, source_target_pairs={{0,12},{4,8},{8,4},{12,0},{1,13},{5,9},{9,5},{13,1},{2,14},{6,10},... | collective-permute-start | bytes 196616 | tf_op jit(solution)/shard_map/ppermute | solution.py:477
  50.7 1.7 %copy-start.22 = (f32[9,256,256]{2,1,0:T(8,128)S(1)}, f32[9,256,256]{2,1,0:T(8,128)}, u32[]{:S(2)}) copy-start(f32[9,256,256]{2,1,0:T(8,128)} %copy-done.21) | copy-start | bytes 7077892
  56.6 29.3 %copy-start.16 = (bf16[256,256]{1,0:T(8,128)(2,1)}, bf16[256,256]{1,0:T(8,128)(2,1)S(1)}, u32[]{:S(2)}) copy-start(bf16[256,256]{1,0:T(8,128)(2,1)S(1)} %get-tuple-element.58) | copy-start | bytes 393220
  56.7 1.0 copy-start.9
  57.8 0.8 copy-start.15
  60.3 25.6 %copy-start.13 = (bf16[512,256]{1,0:T(8,128)(2,1)}, bf16[512,256]{1,0:T(8,128)(2,1)S(1)}, u32[]{:S(2)}) copy-start(bf16[512,256]{1,0:T(8,128)(2,1)S(1)} %get-tuple-element.55.refs_0_) | copy-start | bytes 786436
  60.3 39.8 %copy-start.5 = (bf16[1,256,512]{2,1,0:T(8,128)(2,1)S(1)}, bf16[1,256,512]{2,1,0:T(8,128)(2,1)}, u32[]{:S(2)}) copy-start(bf16[1,256,512]{2,1,0:T(8,128)(2,1)} %param.9) | copy-start | bytes 786436
  60.3 39.8 %copy-start.6 = (bf16[1,256,512]{2,1,0:T(8,128)(2,1)S(1)}, bf16[1,256,512]{2,1,0:T(8,128)(2,1)}, u32[]{:S(2)}) copy-start(bf16[1,256,512]{2,1,0:T(8,128)(2,1)} %param.10) | copy-start | bytes 786436
  60.3 42.2 %collective-permute-start.12 = (f32[2,256,512]{2,1,0:T(8,128)}, f32[2,256,512]{2,1,0:T(8,128)}, u32[]{:S(2)}, u32[]{:S(2)}) collective-permute-start(f32[2,256,512]{2,1,0:T(8,128)} %get-tuple-element.52), channel_id=1, source_target_pairs={{0,1},{1,0},{2,3},{3,2},{4,5},{5,4},{6,7},{7,6},{8,9},{9,8},{10,11... | collective-permute-start | bytes 3145736 | tf_op jit(solution)/shard_map/ppermute | solution.py:609
  60.4 13.5 %collective-permute-start.15 = (bf16[512,256]{1,0:T(8,128)(2,1)S(1)}, bf16[512,256]{1,0:T(8,128)(2,1)S(1)}, u32[]{:S(2)}, u32[]{:S(2)}) collective-permute-start(bf16[512,256]{1,0:T(8,128)(2,1)S(1)} %get-tuple-element.55.refs_0_), channel_id=1, source_target_pairs={{0,12},{4,8},{8,4},{12,0},{1,13},{5,9},{9,5},{13,1},{2,14},{6,10},... | collective-permute-start | bytes 786440 | tf_op jit(solution)/shard_map/ppermute | solution.py:599
  62.9 11.0 %collective-permute-start.16 = (bf16[256,256]{1,0:T(8,128)(2,1)S(1)}, bf16[256,256]{1,0:T(8,128)(2,1)S(1)}, u32[]{:S(2)}, u32[]{:S(2)}) collective-permute-start(bf16[256,256]{1,0:T(8,128)(2,1)S(1)} %get-tuple-element.50.refs_7_), channel_id=1, source_target_pairs={{0,4},{4,0},{8,12},{12,8},{1,5},{5,1},{9,13},{13,9},{2,6},{6,2},{1... | collective-permute-start | bytes 393224 | tf_op jit(solution)/shard_map/ppermute | solution.py:477
  63.0 22.9 %collective-permute-start.14 = (bf16[512,256]{1,0:T(8,128)(2,1)S(1)}, bf16[512,256]{1,0:T(8,128)(2,1)S(1)}, u32[]{:S(2)}, u32[]{:S(2)}) collective-permute-start(bf16[512,256]{1,0:T(8,128)(2,1)S(1)} %get-tuple-element.55.refs_0_), channel_id=1, source_target_pairs={{0,4},{4,0},{8,12},{12,8},{1,5},{5,1},{9,13},{13,9},{2,6},{6,2},{1... | collective-permute-start | bytes 786440 | tf_op jit(solution)/shard_map/ppermute | solution.py:600
  73.8 14.0 %copy-start.7 = (bf16[512,256]{1,0:T(8,128)(2,1)}, bf16[512,256]{1,0:T(8,128)(2,1)S(1)}, u32[]{:S(2)}) copy-start(bf16[512,256]{1,0:T(8,128)(2,1)S(1)} %collective-permute-done.15.one_ref.refs_3_) | copy-start | bytes 786436
  73.9 13.9 %collective-permute-start.17 = (bf16[512,256]{1,0:T(8,128)(2,1)S(1)}, bf16[512,256]{1,0:T(8,128)(2,1)S(1)}, u32[]{:S(2)}, u32[]{:S(2)}) collective-permute-start(bf16[512,256]{1,0:T(8,128)(2,1)S(1)} %shard_map.135), channel_id=1, source_target_pairs={{0,4},{4,0},{8,12},{12,8},{1,5},{5,1},{9,13},{13,9},{2,6},{6,2},{1... | collective-permute-start | bytes 786440 | tf_op jit(solution)/shard_map/ppermute | solution.py:602
  75.8 10.1 %collective-permute-start.18 = (bf16[256,256]{1,0:T(8,128)(2,1)S(1)}, bf16[256,256]{1,0:T(8,128)(2,1)S(1)}, u32[]{:S(2)}, u32[]{:S(2)}) collective-permute-start(bf16[256,256]{1,0:T(8,128)(2,1)S(1)} %get-tuple-element.56), channel_id=1, source_target_pairs={{0,8},{4,12},{8,0},{12,4},{1,9},{5,13},{9,1},{13,5},{2,10},{6,14},... | collective-permute-start | bytes 393224 | tf_op jit(solution)/shard_map/ppermute | solution.py:477
  85.9 1.9 %copy-start.10 = (bf16[256,256]{1,0:T(8,128)(2,1)}, bf16[256,256]{1,0:T(8,128)(2,1)S(1)}, u32[]{:S(2)}) copy-start(bf16[256,256]{1,0:T(8,128)(2,1)S(1)} %collective-permute-done.18.refs_5_.refs_2_) | copy-start | bytes 393220
  85.9 1.9 %copy-start.23 = (bf16[512,256]{1,0:T(8,128)(2,1)}, bf16[512,256]{1,0:T(8,128)(2,1)S(1)}, u32[]{:S(2)}) copy-start(bf16[512,256]{1,0:T(8,128)(2,1)S(1)} %collective-permute-done.14.refs_1_) | copy-start | bytes 786436
  87.8 0.7 copy-start.24
  87.8 5.2 %copy-start.17 = (bf16[256,256]{1,0:T(8,128)(2,1)S(1)}, bf16[256,256]{1,0:T(8,128)(2,1)}, u32[]{:S(2)}) copy-start(bf16[256,256]{1,0:T(8,128)(2,1)} %copy-done.16) | copy-start | bytes 393220
  91.6 19.7 %copy-start.2 = (bf16[512,512]{1,0:T(8,128)(2,1)S(1)}, bf16[512,512]{1,0:T(8,128)(2,1)}, u32[]{:S(2)}) copy-start(bf16[512,512]{1,0:T(8,128)(2,1)} %shard_map.136.weight_ref) | copy-start | bytes 1572868
  91.6 19.7 %collective-permute-start.19 = (bf16[512,512]{1,0:T(8,128)(2,1)}, bf16[512,512]{1,0:T(8,128)(2,1)S(1)}, u32[]{:S(2)}, u32[]{:S(2)}) collective-permute-start(bf16[512,512]{1,0:T(8,128)(2,1)} %shard_map.136.weight_ref), channel_id=1, source_target_pairs={{0,16},{16,0},{1,17},{17,1},{2,18},{18,2},{3,19},{19,3},{4,20},{20... | collective-permute-start | bytes 1572872 | tf_op jit(solution)/shard_map/ppermute | solution.py:643
  93.1 7.1 %collective-permute-start.20 = (bf16[256,256]{1,0:T(8,128)(2,1)S(1)}, bf16[256,256]{1,0:T(8,128)(2,1)S(1)}, u32[]{:S(2)}, u32[]{:S(2)}) collective-permute-start(bf16[256,256]{1,0:T(8,128)(2,1)S(1)} %copy-done.17), channel_id=1, source_target_pairs={{0,12},{4,8},{8,4},{12,0},{1,13},{5,9},{9,5},{13,1},{2,14},{6,10},... | collective-permute-start | bytes 393224 | tf_op jit(solution)/shard_map/ppermute | solution.py:477
  100.1 0.9 copy-start.11
  102.0 9.3 %collective-permute-start.21 = (bf16[256,512]{1,0:T(8,128)(2,1)S(1)}, bf16[256,512]{1,0:T(8,128)(2,1)S(1)}, u32[]{:S(2)}, u32[]{:S(2)}) collective-permute-start(bf16[256,512]{1,0:T(8,128)(2,1)S(1)} %get-tuple-element.59.taps_ref), channel_id=1, source_target_pairs={{0,16},{16,0},{1,17},{17,1},{2,18},{18,2},{3,19},{19,3},{4,20},{20... | collective-permute-start | bytes 786440 | tf_op jit(solution)/shard_map/ppermute | solution.py:622
  103.8 7.4 %collective-permute-start.13 = (bf16[256,512]{1,0:T(8,128)(2,1)S(1)}, bf16[256,512]{1,0:T(8,128)(2,1)S(1)}, u32[]{:S(2)}, u32[]{:S(2)}) collective-permute-start(bf16[256,512]{1,0:T(8,128)(2,1)S(1)} %get-tuple-element.54), channel_id=1, source_target_pairs={{0,2},{1,3},{2,0},{3,1},{4,6},{5,7},{6,4},{7,5},{8,10},{9,11},{10,... | collective-permute-start | bytes 786440 | tf_op jit(solution)/shard_map/ppermute | solution.py:611
Sparse Core Ops, SparseCore 0:
  44.0 19.6 all-gather.2
